TPU v7x, 32 devices: a whole 2x2x4 slice. The times are simulated.
32 devices in a mesh: dp: 2 (over x), seq: 4 (over z), tensor: 4 (over y, core).
Axes of the slice: x: 2, y: 2, z: 4, core: 2. Of those that a mesh axis runs over, the one named last changes fastest.
Arguments:
- tokens: bfloat16 [2048, 4, 1536], P(('seq', 'tensor'), 'dp'), may hold values from -6 to 6
- attn_gain: bfloat16 [1536], replicated, may hold values from 0.5 to 1.5
- w_query: bfloat16 [1536, 1536], P(None, 'tensor'), may hold values from -0.15625 to 0.15625
- w_key: bfloat16 [1536, 768], P(None, 'tensor'), may hold values from -0.15625 to 0.15625
- w_value: bfloat16 [1536, 768], P(None, 'tensor'), may hold values from -0.15625 to 0.15625
- w_output: bfloat16 [1536, 1536], P('tensor'), may hold values from -0.625 to 0.625
- ffn_gain: bfloat16 [1536], replicated, may hold values from 0.5 to 1.5
- w_gate: bfloat16 [1536, 4096], P(None, 'tensor'), may hold values from -0.15625 to 0.15625
- w_up: bfloat16 [1536, 4096], P(None, 'tensor'), may hold values from -0.15625 to 0.15625
- w_down: bfloat16 [4096, 1536], P('tensor'), may hold values from -0.09375 to 0.09375
- cotangent: bfloat16 [2048, 4, 1536], P(('seq', 'tensor'), 'dp'), may hold values from -6 to 6
Outputs:
- activation: bfloat16 [2048, 4, 1536], P(('seq', 'tensor'), 'dp')
- input_grad: float32 [2048, 4, 1536], P(('seq', 'tensor'), 'dp')
- attn_gain_grad: float32 [1536], replicated
- query_grad: float32 [1536, 1536], P(None, 'tensor')
- key_grad: float32 [1536, 768], P(None, 'tensor')
- value_grad: float32 [1536, 768], P(None, 'tensor')
- output_grad: float32 [1536, 1536], P('tensor')
- ffn_gain_grad: float32 [1536], replicated
- gate_grad: float32 [1536, 4096], P(None, 'tensor')
- up_grad: float32 [1536, 4096], P(None, 'tensor')
- down_grad: float32 [4096, 1536], P('tensor')
All inputs are finite; a program needn't handle non-finite values.
Results may differ from a plain program's by a relative error of at most 0.014.
Values may be sent and summed in bfloat16 or wider, within the bound.
A program may use at most 192 MiB of HBM per device.

v0:
```python
import jax
import jax.numpy as jnp
from jax import lax
from jax.sharding import PartitionSpec as P

HEAD_DIM = 96


epsilon = 1e-05
theta = 100000.0


def rotary_tables(positions, head_size):
    middle = head_size // 2
    rates = theta ** (-(jnp.arange(middle, dtype=jnp.float32) * 2.0 / head_size))
    angles = positions.astype(jnp.float32)[:, None] * rates[None, :]
    return (jnp.cos(angles), jnp.sin(angles))


def rotary(values, cosine, sine):
    middle = values.shape[-1] // 2
    first = values[..., :middle]
    second = values[..., middle:]
    return jnp.concatenate(
        [first * cosine - second * sine, second * cosine + first * sine], axis=-1
    )


def norm_rows(values, gain):
    inverse = lax.rsqrt(jnp.mean(values * values, axis=-1, keepdims=True) + epsilon)
    return (values * inverse * gain, inverse)


def norm_back(values, inverse, gain, grad):
    scaled = grad * gain
    gain_part = jnp.sum(grad * values * inverse, axis=(0, 1))
    cubed = inverse * inverse * inverse
    d_values = inverse * scaled - values * cubed * jnp.mean(scaled * values, axis=-1, keepdims=True)
    return (gain_part, d_values)


def score_block(query_seq, keys_seq, row_start, kv_local):
    span_rows = query_seq.shape[0]
    full_length = keys_seq.shape[0]
    grouped = query_seq.reshape(span_rows, kv_local, -1, HEAD_DIM)
    raw = jnp.einsum("ckgd,tkd->kgct", grouped, keys_seq, preferred_element_type=jnp.float32)
    scores = raw * HEAD_DIM ** (-0.5)
    query_places = row_start + jnp.arange(span_rows, dtype=jnp.int32)
    key_places = jnp.arange(full_length, dtype=jnp.int32)
    allowed = key_places[None, :] <= query_places[:, None]
    return (grouped, jnp.where(allowed[None, None], scores, -1e30))


def attend_forward(query_seq, keys_seq, values_seq, row_start, kv_local):
    grouped, scores = score_block(query_seq, keys_seq, row_start, kv_local)
    peak = jnp.max(scores, axis=-1, keepdims=True)
    weights = jnp.exp(scores - peak)
    totals = jnp.sum(weights, axis=-1, keepdims=True)
    probs = (weights / totals).astype(jnp.bfloat16)
    attended = jnp.einsum("kgct,tkd->ckgd", probs, values_seq, preferred_element_type=jnp.float32)
    return (attended.reshape(query_seq.shape[0], -1), peak + jnp.log(totals))


def attend_backward(query_seq, keys_seq, values_seq, d_out_seq, log_total, row_start, kv_local):
    grouped, scores = score_block(query_seq, keys_seq, row_start, kv_local)
    probs = jnp.exp(scores - log_total)
    d_grouped = d_out_seq.reshape(grouped.shape)
    d_probs = jnp.einsum(
        "ckgd,tkd->kgct", d_grouped, values_seq, preferred_element_type=jnp.float32
    )
    delta = jnp.sum(probs * d_probs, axis=-1, keepdims=True)
    d_scores = (probs * (d_probs - delta) * HEAD_DIM ** (-0.5)).astype(jnp.bfloat16)
    d_query = jnp.einsum("kgct,tkd->ckgd", d_scores, keys_seq, preferred_element_type=jnp.float32)
    d_keys = jnp.einsum("kgct,ckgd->tkd", d_scores, grouped, preferred_element_type=jnp.float32)
    d_values = jnp.einsum(
        "kgct,ckgd->tkd", probs.astype(jnp.bfloat16), d_grouped, preferred_element_type=jnp.float32
    )
    return (d_query.reshape(query_seq.shape), d_keys, d_values)


def local(
    tokens, attn_gain, w_query, w_key, w_value, w_output, ffn_gain, w_gate, w_up, w_down, cotangent
):
    rows_local, seqs_local, model_width = tokens.shape
    span_rows = rows_local * lax.axis_size("tensor")
    query_local = w_query.shape[1] // HEAD_DIM
    kv_local = w_key.shape[1] // HEAD_DIM
    row_start = lax.axis_index("seq") * span_rows
    cosine, sine = rotary_tables(row_start + jnp.arange(span_rows, dtype=jnp.int32), HEAD_DIM)
    cosine = cosine[:, None, None, :]
    sine = sine[:, None, None, :]
    inputs = tokens.astype(jnp.float32)
    normed_one, inverse_one = norm_rows(inputs, attn_gain.astype(jnp.float32))
    gathered_one = lax.all_gather(normed_one.astype(jnp.bfloat16), "tensor", axis=0, tiled=True)
    query_proj = jnp.einsum(
        "csd,dn->csn", gathered_one, w_query, preferred_element_type=jnp.float32
    )
    key_proj = jnp.einsum("csd,dn->csn", gathered_one, w_key, preferred_element_type=jnp.float32)
    value_proj = jnp.einsum(
        "csd,dn->csn", gathered_one, w_value, preferred_element_type=jnp.float32
    )
    query_rot = rotary(
        query_proj.reshape(span_rows, seqs_local, query_local, HEAD_DIM), cosine, sine
    ).astype(jnp.bfloat16)
    key_rot = rotary(
        key_proj.reshape(span_rows, seqs_local, kv_local, HEAD_DIM), cosine, sine
    ).astype(jnp.bfloat16)
    value_low = value_proj.reshape(span_rows, seqs_local, kv_local, HEAD_DIM).astype(jnp.bfloat16)
    keys_all, values_all = (
        lax.all_gather(key_rot, "seq", axis=0, tiled=True),
        lax.all_gather(value_low, "seq", axis=0, tiled=True),
    )
    query_seqs = jnp.moveaxis(query_rot, 1, 0)
    key_seqs = jnp.moveaxis(keys_all, 1, 0)
    value_seqs = jnp.moveaxis(values_all, 1, 0)

    def forward_one(inputs_seq):
        return attend_forward(inputs_seq[0], inputs_seq[1], inputs_seq[2], row_start, kv_local)

    attended_seqs, log_totals = lax.map(forward_one, (query_seqs, key_seqs, value_seqs))
    attended = jnp.moveaxis(attended_seqs, 0, 1).astype(jnp.bfloat16)
    attn_part = jnp.einsum("csn,nd->csd", attended, w_output, preferred_element_type=jnp.float32)
    attn_local = lax.psum_scatter(attn_part, "tensor", scatter_dimension=0, tiled=True)
    mid = inputs + attn_local
    normed_two, inverse_two = norm_rows(mid, ffn_gain.astype(jnp.float32))
    gathered_two = lax.all_gather(normed_two.astype(jnp.bfloat16), "tensor", axis=0, tiled=True)
    gate = jnp.einsum("csd,df->csf", gathered_two, w_gate, preferred_element_type=jnp.float32)
    up_proj = jnp.einsum("csd,df->csf", gathered_two, w_up, preferred_element_type=jnp.float32)
    sigmoid_gate = jax.nn.sigmoid(gate)
    silu_gate = gate * sigmoid_gate
    hidden = (silu_gate * up_proj).astype(jnp.bfloat16)
    down_part = jnp.einsum("csf,fd->csd", hidden, w_down, preferred_element_type=jnp.float32)
    down_local = lax.psum_scatter(
        down_part.astype(jnp.bfloat16), "tensor", scatter_dimension=0, tiled=True
    ).astype(jnp.float32)
    activation = (mid + down_local).astype(jnp.bfloat16)
    grad_rows = lax.all_gather(cotangent, "tensor", axis=0, tiled=True)
    down_grad = jnp.einsum("csf,csd->fd", hidden, grad_rows, preferred_element_type=jnp.float32)
    d_hidden = jnp.einsum("csd,fd->csf", grad_rows, w_down, preferred_element_type=jnp.float32)
    d_gate = (d_hidden * up_proj * sigmoid_gate * (1.0 + gate * (1.0 - sigmoid_gate))).astype(
        jnp.bfloat16
    )
    d_up = (d_hidden * silu_gate).astype(jnp.bfloat16)
    gate_grad = jnp.einsum("csd,csf->df", gathered_two, d_gate, preferred_element_type=jnp.float32)
    up_grad = jnp.einsum("csd,csf->df", gathered_two, d_up, preferred_element_type=jnp.float32)
    d_two_part = jnp.einsum("csf,df->csd", d_gate, w_gate, preferred_element_type=jnp.float32)
    d_two_part = d_two_part + jnp.einsum(
        "csf,df->csd", d_up, w_up, preferred_element_type=jnp.float32
    )
    d_normed_two = lax.psum_scatter(d_two_part, "tensor", scatter_dimension=0, tiled=True)
    ffn_gain_part, d_mid_norm = norm_back(
        mid, inverse_two, ffn_gain.astype(jnp.float32), d_normed_two
    )
    d_mid = cotangent.astype(jnp.float32) + d_mid_norm
    d_branch = lax.all_gather(d_mid.astype(jnp.bfloat16), "tensor", axis=0, tiled=True)
    output_grad = jnp.einsum("csn,csd->nd", attended, d_branch, preferred_element_type=jnp.float32)
    d_attended = jnp.einsum(
        "csd,nd->csn", d_branch, w_output, preferred_element_type=jnp.float32
    ).astype(jnp.bfloat16)
    d_attended_seqs = jnp.moveaxis(
        d_attended.reshape(span_rows, seqs_local, query_local, HEAD_DIM), 1, 0
    )

    def backward_one(inputs_seq):
        return attend_backward(
            inputs_seq[0],
            inputs_seq[1],
            inputs_seq[2],
            inputs_seq[3],
            inputs_seq[4],
            row_start,
            kv_local,
        )

    d_query_seqs, d_key_seqs, d_value_seqs = lax.map(
        backward_one, (query_seqs, key_seqs, value_seqs, d_attended_seqs, log_totals)
    )
    d_key_local, d_value_local = (
        lax.psum_scatter(jnp.moveaxis(d_key_seqs, 0, 1), "seq", scatter_dimension=0, tiled=True),
        lax.psum_scatter(jnp.moveaxis(d_value_seqs, 0, 1), "seq", scatter_dimension=0, tiled=True),
    )
    d_query = (
        rotary(jnp.moveaxis(d_query_seqs, 0, 1), cosine, -sine)
        .astype(jnp.bfloat16)
        .reshape(span_rows, seqs_local, -1)
    )
    d_key = (
        rotary(d_key_local, cosine, -sine).astype(jnp.bfloat16).reshape(span_rows, seqs_local, -1)
    )
    d_value = d_value_local.astype(jnp.bfloat16).reshape(span_rows, seqs_local, -1)
    query_grad = jnp.einsum(
        "csd,csn->dn", gathered_one, d_query, preferred_element_type=jnp.float32
    )
    key_grad = jnp.einsum("csd,csn->dn", gathered_one, d_key, preferred_element_type=jnp.float32)
    value_grad = jnp.einsum(
        "csd,csn->dn", gathered_one, d_value, preferred_element_type=jnp.float32
    )
    d_one_part = jnp.einsum("csn,dn->csd", d_query, w_query, preferred_element_type=jnp.float32)
    d_one_part = d_one_part + jnp.einsum(
        "csn,dn->csd", d_key, w_key, preferred_element_type=jnp.float32
    )
    d_one_part = d_one_part + jnp.einsum(
        "csn,dn->csd", d_value, w_value, preferred_element_type=jnp.float32
    )
    d_normed_one = lax.psum_scatter(d_one_part, "tensor", scatter_dimension=0, tiled=True)
    attn_gain_part, d_input_norm = norm_back(
        inputs, inverse_one, attn_gain.astype(jnp.float32), d_normed_one
    )
    input_grad = d_mid + d_input_norm
    (
        query_grad,
        key_grad,
        value_grad,
        output_grad,
        attn_gain_part,
        gate_grad,
        up_grad,
        down_grad,
        ffn_gain_part,
    ) = lax.psum(
        (
            query_grad,
            key_grad,
            value_grad,
            output_grad,
            attn_gain_part,
            gate_grad,
            up_grad,
            down_grad,
            ffn_gain_part,
        ),
        ("dp", "seq"),
    )
    attn_gain_grad, ffn_gain_grad = lax.psum((attn_gain_part, ffn_gain_part), "tensor")
    return (
        activation,
        input_grad,
        attn_gain_grad,
        query_grad,
        key_grad,
        value_grad,
        output_grad,
        ffn_gain_grad,
        gate_grad,
        up_grad,
        down_grad,
    )


def solution(mesh):
    placed = (
        P(("seq", "tensor"), "dp", None),
        P(),
        P(None, "tensor"),
        P(None, "tensor"),
        P(None, "tensor"),
        P("tensor", None),
        P(),
        P(None, "tensor"),
        P(None, "tensor"),
        P("tensor", None),
        P(("seq", "tensor"), "dp", None),
    )
    return jax.shard_map(
        local,
        mesh=mesh,
        in_specs=placed,
        out_specs=(
            P(("seq", "tensor"), "dp", None),
            P(("seq", "tensor"), "dp", None),
            P(),
            P(None, "tensor"),
            P(None, "tensor"),
            P(None, "tensor"),
            P("tensor", None),
            P(),
            P(None, "tensor"),
            P(None, "tensor"),
            P("tensor", None),
        ),
        check_vma=False,
    )
```

profile of v0, /device:TPU:0, one launch (start us, length us, event | category | flops | bytes accessed | tf_op | source)
XLA Modules:
  0.0 1609.1 jit_solution(4228097088529950023)
XLA Ops:
  10.6 2.3 fusion.69
  14.0 30.2 %all-gather.7.cloned.1.call-done = bf16[512,2,1536]{2,0,1:T(8,128)(2,1)} async-done(((bf16[128,2,1536]{2,0,1:T(8,128)(2,1)}), bf16[512,2,1536]{2,0,1:T(8,128)(2,1)}) %all-gather.7.cloned.1.call-update) | async-done | bytes 3145744 | tf_op jit(solution)/shard_map/all_gather | solution.py:94
  44.3 3.2 fusion.87
  48.4 3.9 convolution_convert_fusion.2
  52.5 3.6 fusion.81
  57.3 28.3 %all-gather.11.cloned.1.call-done = bf16[2048,2,2,96]{0,3,2,1:T(8,128)(2,1)} async-done(((bf16[512,2,2,96]{0,3,2,1:T(8,128)(2,1)}), bf16[2048,2,2,96]{0,3,2,1:T(8,128)(2,1)}) %all-gather.11.cloned.1.call-update) | async-done | bytes 1572880 | tf_op jit(solution)/shard_map/all_gather | solution.py:110
  85.6 38.1 %all-gather.9.cloned.1.call-done = bf16[2048,2,2,96]{0,3,2,1:T(8,128)(2,1)} async-done(((bf16[512,2,2,96]{0,3,2,1:T(8,128)(2,1)}), bf16[2048,2,2,96]{0,3,2,1:T(8,128)(2,1)}) %all-gather.9.cloned.1.call-update) | async-done | bytes 1572880 | tf_op jit(solution)/shard_map/all_gather | solution.py:111
  123.8 32.3 %while.26 = (s32[]{:T(128)}, bf16[2,512,384]{1,2,0:T(8,128)(2,1)}, f32[2,2,2,512,1]{3,2,1,4,0:T(2,128)}, bf16[2,2048,2,96]{1,3,2,0:T(8,128)(2,1)}, s32[]{:T(128)...) while((s32[]{:T(128)}, bf16[2,512,384]{1,2,0:T(8,128)(2,1)}, ...), condition=%wide.region_4.5_spmd, body=%wide.region_1.4_spmd.sunk | while | flops 1661991424 | bytes 64820860 | solution.py:120
  125.6 4.5 fusion.146
  130.1 3.7 fusion.147
  134.5 4.7 fusion.148
  141.8 4.5 fusion.146
  146.3 3.7 fusion.147
  150.6 4.7 fusion.148
  156.0 6.0 fusion.77
  162.8 56.7 %reduce-scatter.7.cloned.1.call-done = f32[128,2,1536]{2,0,1:T(8,128)} async-done(((f32[512,2,1536]{2,0,1:T(8,128)}), f32[128,2,1536]{2,0,1:T(8,128)}) %reduce-scatter.7.cloned.1.call-update) | async-done | bytes 1572880 | tf_op jit(solution)/shard_map/reduce_scatter | solution.py:123
  223.7 2.1 copy.45
  226.3 26.0 %all-gather.13.cloned.1.call-done = bf16[512,2,1536]{2,0,1:T(8,128)(2,1)} async-done(((bf16[128,2,1536]{2,0,1:T(8,128)(2,1)}), bf16[512,2,1536]{2,0,1:T(8,128)(2,1)}) %all-gather.13.cloned.1.call-update) | async-done | bytes 3145744 | tf_op jit(solution)/shard_map/all_gather | solution.py:126
  252.3 8.4 fusion.61
  260.7 4.9 fusion.65
  265.6 17.3 %all-gather.15.cloned.1.call-done = bf16[512,2,1536]{2,0,1:T(8,128)(2,1)} async-done(((bf16[128,2,1536]{2,0,1:T(8,128)(2,1)}), bf16[512,2,1536]{2,0,1:T(8,128)(2,1)}) %all-gather.15.cloned.1.call-update) | async-done | bytes 3145744 | tf_op jit(solution)/shard_map/all_gather | solution.py:137
  283.0 9.5 multiply_convert_fusion
  292.5 3.5 fusion.63
  296.0 5.5 convolution_add_fusion
  301.5 58.5 %reduce-scatter.11.cloned.1.call-done = f32[128,2,1536]{2,0,1:T(8,128)} async-done(((f32[512,2,1536]{2,0,1:T(8,128)}), f32[128,2,1536]{2,0,1:T(8,128)}) %reduce-scatter.11.cloned.1.call-update) | async-done | bytes 1572880 | tf_op jit(solution)/shard_map/reduce_scatter | solution.py:150
  360.0 3.0 multiply_reduce_fusion
  363.6 2.4 fusion.93
  366.1 28.6 %all-gather.17.cloned.1.call-done = bf16[512,2,1536]{2,0,1:T(8,128)(2,1)} async-done(((bf16[128,2,1536]{2,0,1:T(8,128)(2,1)}), bf16[512,2,1536]{2,0,1:T(8,128)(2,1)}) %all-gather.17.cloned.1.call-update) | async-done | bytes 3145744 | tf_op jit(solution)/shard_map/all_gather | solution.py:155
  394.7 4.5 convolution_convert_fusion.1
  399.2 166.4 %while.27 = (s32[]{:T(128)}, f32[2,512,4,96]{1,3,2,0:T(8,128)}, f32[2,2048,2,96]{1,3,2,0:T(8,128)}, f32[2,2048,2,96]{1,3,2,0:T(8,128)}, bf16[2,2048,2,96]{1,3,2,...) while((s32[]{:T(128)}, f32[2,512,4,96]{1,3,2,0:T(8,128)}, ...), condition=%wide.region_12.13_spmd, body=%wide.region_10.12_spmd.sunk | while | flops 4136641024 | bytes 209779408 | solution.py:175
  400.6 9.5 fusion.158
  410.1 8.2 fusion.157
  420.8 25.2 %fusion.160 = f32[2,2048,2,96]{1,3,2,0:T(8,128)} fusion(f32[2,2048,2,96]{1,3,2,0:T(8,128)} %get-tuple-element.354, s32[]{:T(128)} %get-tuple-element.352, bf16[512,2,2,96]{0,3,2,1:T(8,128)(2,1)} %bitcast.299, f32[2,2048,512,2]{2,1,3,0:T(8,128)} %fusion.157, f32[2,2048,512,2]{2,1,3,0:T(8,128)} %fusion.158, ...), kind=kOutput, calls=%fused_computation.37.clone.1 | convolution fusion | flops 851447808 | bytes 71188992 | tf_op jit(solution)/shard_map/while/body/eval_jaxpr/kgct,ckgd->tkd/dot_general | solution.py:74
  445.9 24.8 %fusion.159 = f32[2,96,2,512]{3,1,2,0:T(8,128)} fusion(f32[2,2048,512,2]{2,1,3,0:T(8,128)} %fusion.157, f32[2,2048,512,2]{2,1,3,0:T(8,128)} %fusion.158, f32[2,2,512]{2,1,0:T(2,128)S(1)} %dynamic-slice_bitcast_fusion.2, pred[512,2048]{0,1:T(8,128)(4,1)} %iota_compare_fusion.5, bf16[2,2048,2,96]{1,3,2,0:T(8,128)(2,1)} %get-tuple-element.367, ...), kind=kOutput, calls=%fused_computation.34.clone.1 | convolution fusion | flops 851447808 | bytes 70795776 | tf_op jit(solution)/shard_map/while/body/eval_jaxpr/kgct,tkd->ckgd/dot_general | solution.py:73
  470.8 2.1 constant_dynamic-update-slice_fusion.5
  472.8 9.6 fusion.161
  483.6 9.5 fusion.158
  493.1 8.2 fusion.157
  503.8 25.2 %fusion.160 = f32[2,2048,2,96]{1,3,2,0:T(8,128)} fusion(f32[2,2048,2,96]{1,3,2,0:T(8,128)} %get-tuple-element.354, s32[]{:T(128)} %get-tuple-element.352, bf16[512,2,2,96]{0,3,2,1:T(8,128)(2,1)} %bitcast.299, f32[2,2048,512,2]{2,1,3,0:T(8,128)} %fusion.157, f32[2,2048,512,2]{2,1,3,0:T(8,128)} %fusion.158, ...), kind=kOutput, calls=%fused_computation.37.clone.1 | convolution fusion | flops 851447808 | bytes 71188992 | tf_op jit(solution)/shard_map/while/body/eval_jaxpr/kgct,ckgd->tkd/dot_general | solution.py:74
  529.0 24.8 %fusion.159 = f32[2,96,2,512]{3,1,2,0:T(8,128)} fusion(f32[2,2048,512,2]{2,1,3,0:T(8,128)} %fusion.157, f32[2,2048,512,2]{2,1,3,0:T(8,128)} %fusion.158, f32[2,2,512]{2,1,0:T(2,128)S(1)} %dynamic-slice_bitcast_fusion.2, pred[512,2048]{0,1:T(8,128)(4,1)} %iota_compare_fusion.5, bf16[2,2048,2,96]{1,3,2,0:T(8,128)(2,1)} %get-tuple-element.367, ...), kind=kOutput, calls=%fused_computation.34.clone.1 | convolution fusion | flops 851447808 | bytes 70795776 | tf_op jit(solution)/shard_map/while/body/eval_jaxpr/kgct,tkd->ckgd/dot_general | solution.py:73
  553.8 2.1 constant_dynamic-update-slice_fusion.5
  555.9 9.6 fusion.161
  569.3 4.5 fusion.79
  573.8 52.3 %reduce-scatter.13.cloned.1.call-done = f32[512,2,2,96]{0,3,2,1:T(8,128)} async-done(((f32[2048,2,2,96]{0,3,2,1:T(8,128)}), f32[512,2,2,96]{0,3,2,1:T(8,128)}) %reduce-scatter.13.cloned.1.call-update) | async-done | bytes 786448 | tf_op jit(solution)/shard_map/reduce_scatter | solution.py:179
  627.4 4.8 fusion.85
  632.2 57.0 %reduce-scatter.15.cloned.1.call-done = f32[512,2,2,96]{0,3,2,1:T(8,128)} async-done(((f32[2048,2,2,96]{0,3,2,1:T(8,128)}), f32[512,2,2,96]{0,3,2,1:T(8,128)}) %reduce-scatter.15.cloned.1.call-update) | async-done | bytes 786448 | tf_op jit(solution)/shard_map/reduce_scatter | solution.py:180
  691.1 8.5 add_add_fusion
  699.7 6.5 convolution_convert_fusion
  706.2 9.8 convolution_bitcast_fusion.1
  716.0 5.9 convolution_bitcast_fusion.2
  721.9 5.5 convolution_bitcast_fusion
  727.5 4.1 convolution_bitcast_fusion.3
  731.6 3.3 convolution_bitcast_fusion.4
  738.5 19.6 %reduce-scatter.17.cloned.1.call-done = f32[128,2,1536]{2,0,1:T(8,128)} async-done(((f32[512,2,1536]{2,0,1:T(8,128)}), f32[128,2,1536]{2,0,1:T(8,128)}) %reduce-scatter.17.cloned.1.call-update) | async-done | bytes 1572880 | tf_op jit(solution)/shard_map/reduce_scatter | solution.py:205
  760.2 38.5 %reduce-scatter.9.cloned.1.call-done = bf16[128,2,1536]{2,0,1:T(8,128)(2,1)} async-done(((bf16[512,2,1536]{2,0,1:T(8,128)(2,1)}), bf16[128,2,1536]{2,0,1:T(8,128)(2,1)}) %reduce-scatter.9.cloned.1.call-update) | async-done | bytes 786448 | tf_op jit(solution)/shard_map/reduce_scatter | solution.py:133
  798.7 3.9 fusion.72
  802.6 2.4 copy.54
  806.7 39.4 %all-reduce = (f32[1536]{0:T(1024)S(1)}, f32[1536]{0:T(1024)S(1)}) all-reduce(f32[1536]{0:T(1024)S(1)} %get-tuple-element.132, f32[1536]{0:T(1024)S(1)} %copy-done.24), channel_id=1, replica_groups=mesh['dp'=2,'seq'=4,'tensor'=4] {'dp','seq'}, use_global_device_ids=true, to_apply=%region_18.19 | all-reduce | flops 3072 | bytes 24576 | tf_op jit(solution)/shard_map/psum | solution.py:220
  846.1 11.5 all-reduce.2
  857.6 725.0 %all-reduce.5.cloned.1.call-done = (f32[1536,384]{1,0:T(8,128)}, f32[1536,192]{0,1:T(8,128)}, f32[1536,192]{0,1:T(8,128)}, f32[384,1536]{1,0:T(8,128)}, f32[1536...) async-done(((f32[1536,384]{1,0:T(8,128)}, f32[1536,192]{0,1:T(8,128)}, f32[1536,192]{0,1:T(8,128)}, f32[384,1536]{1,0:T(8,128)}, f32[1536,1024]{1,0:T(8,128)}, ...) | async-done | bytes 25952272 | tf_op jit(solution)/shard_map/psum | solution.py:220
  1582.6 3.4 copy.118
  1591.4 3.2 copy.122
  1594.8 3.2 copy.123
  1599.4 2.7 copy.124
  (185 shorter events, 47.9 us)
Async XLA Ops:
  7.2 275.8 %copy-start = (bf16[1024,1536]{1,0:T(8,128)(2,1)S(1)}, bf16[1024,1536]{1,0:T(8,128)(2,1)}, u32[]{:S(2)}) copy-start(bf16[1024,1536]{1,0:T(8,128)(2,1)} %param.24) | copy-start | bytes 9437188
  7.2 37.1 %all-gather.7.cloned.1.call-start = ((), (), s32[]{:S(2)}) async-start(), calls=%async_computation.6 | async-start | bytes 3932160 | tf_op jit(solution)/shard_map/all_gather | solution.py:94
  9.3 0.7 copy-start.27
  12.9 72.8 %all-gather.11.cloned.1.call-start = ((), (), s32[]{:S(2)}) async-start(), calls=%async_computation.8 | async-start | bytes 1966080 | tf_op jit(solution)/shard_map/all_gather | solution.py:110
  14.0 42.1 %copy-start.13 = (f32[512,48]{0,1:T(8,128)}, f32[512,48]{0,1:T(8,128)S(1)}, u32[]{:S(2)}) copy-start(f32[512,48]{0,1:T(8,128)S(1)} %get-tuple-element.200) | copy-start | bytes 294916
  48.4 75.4 %all-gather.9.cloned.1.call-start = ((), (), s32[]{:S(2)}) async-start(), calls=%async_computation.7 | async-start | bytes 1966080 | tf_op jit(solution)/shard_map/all_gather | solution.py:111
  52.4 167.1 %reduce-scatter.7.cloned.1.call-start = ((), (), s32[]{:S(2)}) async-start(), calls=%async_computation.9 | async-start | bytes 7864320 | tf_op jit(solution)/shard_map/reduce_scatter | solution.py:123
  130.1 4.3 copy-start.6
  146.3 4.3 copy-start.6
  162.1 0.7 copy-start.34
  162.1 90.2 %all-gather.13.cloned.1.call-start = ((), (), s32[]{:S(2)}) async-start(), calls=%async_computation.10 | async-start | bytes 3932160 | tf_op jit(solution)/shard_map/all_gather | solution.py:126
  162.8 200.3 %copy-start.20 = (f32[1536]{0:T(1024)}, f32[1536]{0:T(1024)S(1)}, u32[]{:S(2)}) copy-start(f32[1536]{0:T(1024)S(1)} %convert_element_type.95) | copy-start | bytes 18436
  221.3 1.2 copy-start.1
  221.4 141.7 %copy-start.25 = (f32[128,2]{0,1:T(2,128)}, f32[128,2]{0,1:T(2,128)S(1)}, u32[]{:S(2)}) copy-start(f32[128,2]{0,1:T(2,128)S(1)} %get-tuple-element.204) | copy-start | bytes 3076
  221.4 141.7 %copy-start.29 = (f32[128,2]{0,1:T(2,128)}, f32[128,2]{0,1:T(2,128)S(1)}, u32[]{:S(2)}) copy-start(f32[128,2]{0,1:T(2,128)S(1)} %get-tuple-element.203) | copy-start | bytes 3076
  223.6 59.3 %all-gather.15.cloned.1.call-start = ((), (), s32[]{:S(2)}) async-start(), calls=%async_computation.12 | async-start | bytes 3932160 | tf_op jit(solution)/shard_map/all_gather | solution.py:137
  225.8 134.2 %reduce-scatter.11.cloned.1.call-start = ((), (), s32[]{:S(2)}) async-start(), calls=%async_computation.13 | async-start | bytes 7864320 | tf_op jit(solution)/shard_map/reduce_scatter | solution.py:150
  252.3 8.4 copy-start.35
  252.3 8.4 copy-start.38
  283.0 9.5 copy-start.36
  292.5 3.5 copy-start.44
  292.5 3.5 copy-start.43
  292.5 3.5 copy-start.37
  301.5 93.3 %all-gather.17.cloned.1.call-start = ((), (), s32[]{:S(2)}) async-start(), calls=%async_computation.14 | async-start | bytes 3932160 | tf_op jit(solution)/shard_map/all_gather | solution.py:155
  360.0 3.6 copy-start.2
  360.0 3.6 copy-start.4
  366.0 260.1 %reduce-scatter.13.cloned.1.call-start = ((), (), s32[]{:S(2)}) async-start(), calls=%async_computation.15 | async-start | bytes 3932160 | tf_op jit(solution)/shard_map/reduce_scatter | solution.py:179
  400.6 9.5 copy-start.3
  400.6 9.5 copy-start.7
  483.6 9.5 copy-start.3
  483.6 9.5 copy-start.7
  565.7 0.9 copy-start.14
  565.7 0.9 copy-start.19
  565.7 123.4 %reduce-scatter.15.cloned.1.call-start = ((), (), s32[]{:S(2)}) async-start(), calls=%async_computation.16 | async-start | bytes 3932160 | tf_op jit(solution)/shard_map/reduce_scatter | solution.py:180
  566.3 191.9 %reduce-scatter.17.cloned.1.call-start = ((), (), s32[]{:S(2)}) async-start(), calls=%async_computation.17 | async-start | bytes 7864320 | tf_op jit(solution)/shard_map/reduce_scatter | solution.py:205
  566.3 2.9 copy-start.18
  568.4 0.9 copy-start.11
  690.3 0.7 copy-start.9
  699.6 99.1 %reduce-scatter.9.cloned.1.call-start = ((), (), s32[]{:S(2)}) async-start(), calls=%async_computation.11 | async-start | bytes 3932160 | tf_op jit(solution)/shard_map/reduce_scatter | solution.py:133
  706.1 876.5 %all-reduce.5.cloned.1.call-start = ((), (), s32[]{:S(2)}) async-start(), calls=%async_computation.18 | async-start | bytes 51904512 | tf_op jit(solution)/shard_map/psum | solution.py:220
  706.2 9.8 copy-start.39
  706.2 9.8 copy-start.45
  716.0 5.9 copy-start.40
  716.0 5.9 copy-start.42
  721.9 5.6 copy-start.41
  727.5 4.1 copy-start.5
  727.5 4.1 copy-start.12
  734.8 1.8 copy-start.10
  738.4 19.7 %copy-start.23 = (f32[1536]{0:T(1024)S(1)}, f32[1536]{0:T(1024)}, u32[]{:S(2)}) copy-start(f32[1536]{0:T(1024)} %copy-done.22) | copy-start | bytes 18436
  738.4 19.7 %copy-start.28 = (f32[128,2]{0,1:T(2,128)S(1)}, f32[128,2]{0,1:T(2,128)}, u32[]{:S(2)}) copy-start(f32[128,2]{0,1:T(2,128)} %copy-done.27) | copy-start | bytes 3076
  738.4 60.2 %copy-start.21 = (f32[1536]{0:T(1024)S(1)}, f32[1536]{0:T(1024)}, u32[]{:S(2)}) copy-start(f32[1536]{0:T(1024)} %copy-done.20) | copy-start | bytes 18436
  738.4 60.2 %copy-start.26 = (f32[128,2]{0,1:T(2,128)S(1)}, f32[128,2]{0,1:T(2,128)}, u32[]{:S(2)}) copy-start(f32[128,2]{0,1:T(2,128)} %copy-done.25) | copy-start | bytes 3076
  738.5 60.2 %copy-start.30 = (f32[128,2]{0,1:T(2,128)S(1)}, f32[128,2]{0,1:T(2,128)}, u32[]{:S(2)}) copy-start(f32[128,2]{0,1:T(2,128)} %copy-done.29) | copy-start | bytes 3076
  738.5 60.2 %copy-start.32 = (f32[128,2]{0,1:T(2,128)S(1)}, f32[128,2]{0,1:T(2,128)}, u32[]{:S(2)}) copy-start(f32[128,2]{0,1:T(2,128)} %copy-done.31) | copy-start | bytes 3076
  738.5 60.2 %copy-start.33 = (f32[128,2]{0,1:T(2,128)S(1)}, f32[128,2]{0,1:T(2,128)}, u32[]{:S(2)}) copy-start(f32[128,2]{0,1:T(2,128)} %get-tuple-element.201) | copy-start | bytes 3076
  802.6 4.1 copy-start.24
  1582.6 3.4 copy-start.17
  1582.6 4.4 copy-start.16
  1586.0 2.3 copy-start.15
  1587.0 4.3 copy-start.8
  1588.3 6.2 slice-start.2
  1591.4 3.4 slice-start.3
  1591.4 7.0 slice-start
  1594.8 4.6 slice-start.1
  (2 other events, 1.1 us)
Sparse Core Ops, SparseCore 0:
  13.0 31.2 all-gather.6
  48.5 37.0 all-gather.10
  87.8 35.9 all-gather.8
  162.2 57.2 reduce-scatter.6
  223.7 28.5 all-gather.12
  254.4 28.5 all-gather.14
  301.6 58.3 reduce-scatter.10
  366.2 28.5 all-gather.16
  565.8 60.2 reduce-scatter.12
  628.8 60.2 reduce-scatter.14
  699.7 58.3 reduce-scatter.16
  760.7 37.9 reduce-scatter.8
  805.8 776.7 all-reduce.4
where the time goes:
time: 1620 us; the launch traced here: 1610 us
  waiting for transfers between devices  1180 us (73%)
  matrix products  282 us (17%)
  blocking collectives  50.9 us (3%)
  local copies, waits for them, and re-layouts  41.9 us (3%)
  other arithmetic  40.7 us (3%)
    psum x1, waiting for transfers between devices, local(): lax.psum((query_grad, key_grad, value_grad, output_grad, attn_gain_part,...  725 us
    reduce_scatter x1, waiting for transfers between devices, local(): lax.psum_scatter(d_two_part, 'tensor', scatter_dimension=0, tiled=True)  58.5 us
    reduce_scatter x1, waiting for transfers between devices, local(): lax.psum_scatter(jnp.moveaxis(d_value_seqs, 0, 1), 'seq', scatter_dimensi...  57 us
    reduce_scatter x1, waiting for transfers between devices, local(): lax.psum_scatter(attn_part, 'tensor', scatter_dimension=0, tiled=True)  56.7 us
    reduce_scatter x1, waiting for transfers between devices, local(): lax.psum_scatter(jnp.moveaxis(d_key_seqs, 0, 1), 'seq', scatter_dimension...  52.3 us
    dot_general x2, matrix products, attend_backward(): jnp.einsum('kgct,ckgd->tkd', d_scores, grouped, preferred_element_type=jn...  50.3 us
    dot_general x2, matrix products, attend_backward(): jnp.einsum('kgct,tkd->ckgd', d_scores, keys_seq, preferred_element_type=j...  49.7 us
    psum x1, blocking collectives, local(): lax.psum((query_grad, key_grad, value_grad, output_grad, attn_gain_part,...  39.4 us
  transfers between devices with their start and end apart: 13, of which 13 were waited for; matrix products, arithmetic and copies ran while one was open for 5% of the time, Pallas kernels for 0%

commit v1 on v0

v1 whole, which is shorter than its diff:
```python
import functools
import numpy as np
import jax, jax.numpy as jnp
from jax import lax
from jax.sharding import PartitionSpec as P
import jax.experimental.pallas as pl
import jax.experimental.pallas.tpu as pltpu

MESH = pl.DeviceIdType.MESH
bf16 = jnp.bfloat16
f32 = jnp.float32
HEAD_DIM = 96
HALF = 48
epsilon = 1e-05
theta = 100000.0
LOG2E = 1.4426950408889634
SCALE = HEAD_DIM ** -0.5
VMEM_BYTES = 63 << 20

K_LANES = [list(range(0, 48)) + list(range(64, 112)), list(range(16, 64)) + list(range(80, 128))]
F_LANES = [list(range(48, 64)) + list(range(112, 128)), list(range(0, 16)) + list(range(64, 80))]
V_LANES = [list(range(0, 48)) + list(range(64, 80)), list(range(48, 64)) + list(range(80, 128))]


def pick_tables():
    q = np.zeros((384, 512), np.float32)
    kv = np.zeros((384, 384), np.float32)
    o = np.zeros((512, 384), np.float32)
    for h in range(4):
        for d in range(96):
            q[h * 96 + d, h * 128 + K_LANES[h // 2][d]] = 1
            lane = F_LANES[h // 2][d] if d < 32 else V_LANES[h // 2][d - 32]
            o[h * 128 + lane, h * 96 + d] = 1
    for g in range(2):
        for d in range(96):
            kv[g * 96 + d, g * 128 + K_LANES[g][d]] = 1
            lane = g * 128 + F_LANES[g][d] if d < 32 else 256 + V_LANES[g][d - 32]
            kv[192 + g * 96 + d, lane] = 1
    return q, kv, o


def in_ranges(lane, lanes):
    mask = None
    lo = prev = lanes[0]
    runs = []
    for x in lanes[1:] + [None]:
        if x is None or x != prev + 1:
            runs.append((lo, prev))
            lo = x
        prev = x
    for a, b in runs:
        m = jnp.logical_and(lane >= a, lane <= b)
        mask = m if mask is None else jnp.logical_or(mask, m)
    return mask


def rope_tables(row_start, span, t):
    rate = np.zeros((2, 128), np.float32)
    sign = np.zeros((2, 128), np.float32)
    for g in range(2):
        for d in range(96):
            rate[g, K_LANES[g][d]] = d % HALF
            sign[g, K_LANES[g][d]] = -1.0 if d < HALF else 1.0
    used = np.abs(sign)
    rates = used * theta ** (-(jnp.asarray(rate) * 2.0 / HEAD_DIM))
    i = jnp.arange(span, dtype=jnp.int32)
    c = span // 4
    places = (row_start + ((i // c) ^ t) * c + i % c).astype(f32)
    angle = places[None, :, None] * rates[:, None, :]
    return jnp.cos(angle), jnp.sin(angle) * sign[:, None, :]


def nt(a, b):
    return lax.dot_general(a, b, (((1,), (1,)), ((), ())), preferred_element_type=f32)


def nn(a, b):
    return jnp.dot(a, b, preferred_element_type=f32)


def tn(a, b):
    return lax.dot_general(a, b, (((0,), (0,)), ((), ())), preferred_element_type=f32)


def rc(src, dst, ss, rr, dev):
    return pltpu.make_async_remote_copy(src, dst, ss, rr, device_id=dev, device_id_type=MESH)


def entry(devs, z_line):
    b = pltpu.get_barrier_semaphore()
    count = len(devs)
    for dev in devs:
        pl.semaphore_signal(b, inc=1, device_id=dev, device_id_type=MESH)
    if z_line:
        zi = lax.axis_index("seq")
        nz = lax.axis_size("seq")
        @pl.when(zi > 0)
        def _():
            pl.semaphore_signal(b, inc=1, device_id={"seq": zi - 1}, device_id_type=MESH)
        @pl.when(zi < nz - 1)
        def _():
            pl.semaphore_signal(b, inc=1, device_id={"seq": zi + 1}, device_id_type=MESH)
        count = count + (zi > 0).astype(jnp.int32) + (zi < nz - 1).astype(jnp.int32)
    pl.semaphore_wait(b, count)


def causal(sT, qt, TQ, RP, t):
    span = sT.shape[0]
    ki = lax.broadcasted_iota(jnp.int32, (span, 1), 0)
    qi = lax.broadcasted_iota(jnp.int32, (1, TQ), 1) + (qt % (span // TQ)) * TQ
    kpos = ((ki // RP) ^ t) * RP + ki % RP
    qpos = ((qi // RP) ^ t) * RP + qi % RP
    return jnp.where(kpos <= qpos, sT, -1e30)


def rms(v, gain):
    return v * lax.rsqrt(jnp.mean(v * v, axis=-1, keepdims=True) + epsilon) * gain


def norm_back_rows(v, e, gain):
    inv = lax.rsqrt(jnp.mean(v * v, axis=-1, keepdims=True) + epsilon)
    part = jnp.sum(e * v * inv, axis=0, keepdims=True)
    sc = e * gain
    return part, inv * sc - v * (inv * inv * inv) * jnp.mean(sc * v, axis=-1, keepdims=True)


def forward_kernel(nz, tok, cot, wq, wk, wv, w_out, pq, pkv, po, cos, sin, gain1, gain2,
                   x1_out, c_out, q_out, kv_out, att_out, lse_out, wqkv_out, wo_out, mid_out, n2_out,
                   xn, X, C, KV, q, att, lse, wqkv, wo, m_s, l_s, o_s, part, rs1, ysend, rs2,
                   sA, rA, sB, rB, sC, rC, sKV, rKV, sR1, rR1, sR2, rR2, osem):
    t = lax.axis_index("tensor")
    zi = lax.axis_index("seq")
    sib, ynb = t ^ 1, t ^ 2
    S, RP, D = tok.shape
    SPAN = 4 * RP
    TQ = 256
    NT = 2 * SPAN // TQ
    g1 = gain1[...].astype(f32)
    for s in range(S):
        xn[s] = rms(tok[s].astype(f32), g1).astype(bf16)
    entry([{"tensor": sib}, {"tensor": ynb}], True)

    def ga(w, s):
        return rc((xn, cot)[w].at[s], (X, C)[w].at[s, 1], sA.at[w, s], rA.at[w, s], {"tensor": sib})
    def gb(w, s):
        return rc((xn, cot)[w].at[s], (X, C)[w].at[s, 2], sB.at[w, s], rB.at[w, s], {"tensor": ynb})
    def gc(w, s):
        buf = (X, C)[w]
        return rc(buf.at[s, 2], buf.at[s, 3], sC.at[w, s], rC.at[w, s], {"tensor": sib})
    for s in range(S):
        gb(0, s).start()
        ga(0, s).start()
    wqkv[:, 0:512] = nn(wq[...], pq[...]).astype(bf16)
    wqkv[:, 512:896] = (nn(wk[...], pkv[0:192, :]) + nn(wv[...], pkv[192:384, :])).astype(bf16)
    for s in range(S):
        X[s, 0] = xn[s]

    def kvc(s, j, hb):
        at = pl.ds(hb * 2 * RP, 2 * RP)
        return rc(KV.at[s, j, at], KV.at[s, j, at], sKV.at[s, j, hb], rKV.at[s, j, hb], {"seq": zi + 1})
    def send_own(s, hb):
        @pl.when(zi < nz - 1)
        def _():
            kvc(s, zi, hb).start()
    def arrive(s, h, hb):
        j = zi - 1 - h
        @pl.when(j >= 0)
        def _():
            kvc(s, j, hb).wait_recv()
            @pl.when(zi < nz - 1)
            def _():
                kvc(s, j, hb).start()

    def project(s, hb):
        r = nn(X[s, 2 * hb:2 * hb + 2].reshape(2 * RP, D), wqkv[...])
        base = hb * 2 * RP
        for slot in range(6):
            g = slot // 2 if slot < 4 else slot - 4
            u = r[:, slot * 128:(slot + 1) * 128]
            u = u * cos[g, base:base + 2 * RP, :] + pltpu.roll(u, 64, 1) * sin[g, base:base + 2 * RP, :]
            if slot < 4:
                q[s, g, (slot % 2) * SPAN + base:(slot % 2) * SPAN + base + 2 * RP, :] = u.astype(bf16)
            else:
                KV[s, zi, base:base + 2 * RP, g * 128:(g + 1) * 128] = u.astype(bf16)
        KV[s, zi, base:base + 2 * RP, 256:384] = r[:, 768:896].astype(bf16)

    def unit(s, j, diag):
        def tile(g, qt):
            qa = pl.ds(pl.multiple_of(qt * TQ, TQ), TQ)
            kp = KV[s, j, :, g * 128:(g + 1) * 128]
            sT = nt(kp, q[s, g, qa, :]) * (SCALE * LOG2E)
            if diag:
                sT = causal(sT, qt, TQ, RP, t)
            mx = jnp.max(sT, axis=0, keepdims=True)
            if diag:
                m = mx
            else:
                m0 = m_s[s, g, :, qa]
                m = jnp.maximum(m0, mx)
                al = jnp.exp2(m0 - m)
            p = jnp.exp2(sT - m)
            total = jnp.sum(p, axis=0, keepdims=True)
            kv = jnp.concatenate([kp, KV[s, j, :, 256:384]], axis=1)
            o = tn(kv, p.astype(bf16))
            m_s[s, g, :, qa] = m
            if diag:
                l_s[s, g, :, qa] = total
                o_s[s, g, :, qa] = o
            else:
                l_s[s, g, :, qa] = l_s[s, g, :, qa] * al + total
                o_s[s, g, :, qa] = o_s[s, g, :, qa] * al + o
        def body(qt, c):
            tile(0, qt)
            tile(1, qt)
            return c
        lax.fori_loop(0, NT, body, 0, unroll=2)
    def hop(s, h):
        @pl.when(zi - 1 - h >= 0)
        def _():
            unit(s, zi - 1 - h, False)

    def rs_a(s):
        return rc(part.at[s, 1], rs1.at[s], sR1.at[s], rR1.at[s], {"tensor": sib})
    def rs_b(s):
        return rc(ysend.at[s], rs2.at[s], sR2.at[s], rR2.at[s], {"tensor": ynb})
    def finish(s):
        lane = lax.broadcasted_iota(jnp.int32, (128, 1), 0)
        for g in range(2):
            lse[s, g] = m_s[s, g] + jnp.log2(l_s[s, g])
            fm = in_ranges(lane, F_LANES[g])
            vm = in_ranges(lane, V_LANES[g])
            o = jnp.where(fm, o_s[s, g, 0:128, :], jnp.where(vm, o_s[s, g, 128:256, :], 0.0)) * (1.0 / l_s[s, g])
            att[s, g] = o.T.astype(bf16)
        for par in (1, 0):
            a = jnp.concatenate([jnp.concatenate([att[s, g, hh * SPAN + r * RP:hh * SPAN + (r + 1) * RP, :]
                                                  for g in range(2) for hh in range(2)], axis=1) for r in (par, par + 2)], axis=0)
            part[s, par] = nn(a, wo[...]).astype(bf16).reshape(2, RP, D)
            if par == 1:
                rs_a(s).start()
    def rs_mid(s):
        rs_a(s).wait_recv()
        ysend[s] = (part[s, 0, 1].astype(f32) + rs1[s, 1].astype(f32)).astype(bf16)
        rs_b(s).start()
    def rs_end(s):
        rs_b(s).wait_recv()
        mid = tok[s].astype(f32) + part[s, 0, 0].astype(f32) + rs1[s, 0].astype(f32) + rs2[s].astype(f32)
        mid_out[s] = mid
        n2_out[s] = rms(mid, gain2[...].astype(f32)).astype(bf16)

    ga(0, 0).wait_recv()
    project(0, 0)
    send_own(0, 0)
    ga(0, 1).wait_recv()
    project(1, 0)
    wo[...] = nn(po[...], w_out[...]).astype(bf16)
    gb(0, 0).wait_recv()
    gc(0, 0).start()
    arrive(0, 0, 0)
    gc(0, 0).wait_recv()
    project(0, 1)
    send_own(0, 1)
    arrive(0, 1, 0)
    gb(0, 1).wait_recv()
    gc(0, 1).start()
    for s in range(S):
        gb(1, s).start()
        ga(1, s).start()
    unit(0, zi, True)
    arrive(0, 0, 1)
    gc(0, 1).wait_recv()
    project(1, 1)
    arrive(0, 1, 1)
    send_own(1, 0)
    send_own(1, 1)
    hop(0, 0)
    for h in range(2, nz - 1):
        arrive(0, h, 0)
        arrive(0, h, 1)
    for s in range(S):
        C[s, 0] = cot[s]
    def more(h, c):
        hop(0, h)
        return c
    hop(0, 1)
    arrive(1, 0, 0)
    arrive(1, 0, 1)
    lax.fori_loop(2, nz - 1, more, 0)
    finish(0)
    unit(1, zi, True)
    gb(1, 0).wait_recv()
    gc(1, 0).start()
    rs_mid(0)
    arrive(1, 1, 0)
    arrive(1, 1, 1)
    hop(1, 0)
    gb(1, 1).wait_recv()
    gc(1, 1).start()
    hop(1, 1)
    rs_end(0)
    def rest(h, c):
        arrive(1, h, 0)
        arrive(1, h, 1)
        hop(1, h)
        return c
    lax.fori_loop(2, nz - 1, rest, 0)
    finish(1)
    for s in range(S):
        gc(1, s).wait_recv()
        ga(1, s).wait_recv()
    outs = [pltpu.make_async_copy(a, o, osem.at[n]) for n, (a, o) in enumerate(
        ((X, x1_out), (C, c_out), (q, q_out), (KV, kv_out), (att, att_out), (lse, lse_out), (wqkv, wqkv_out), (wo, wo_out)))]
    for o in outs:
        o.start()
    rs_mid(1)
    rs_end(1)
    for s in range(S):
        for w in range(2):
            ga(w, s).wait_send()
            gb(w, s).wait_send()
            gc(w, s).wait_send()
        rs_a(s).wait_send()
        rs_b(s).wait_send()
        for j in range(nz):
            @pl.when(jnp.logical_and(j <= zi, zi < nz - 1))
            def _():
                for hb in range(2):
                    kvc(s, j, hb).wait_send()
    for o in outs:
        o.wait()


def attend_forward(tok, cot, wq, wk, wv, w_out, pq, pkv, po, cos, sin, gain1, gain2):
    nz = lax.axis_size("seq")
    S, RP, D = tok.shape
    SPAN = 4 * RP
    V = pl.BlockSpec(memory_space=pltpu.VMEM)
    A = pl.BlockSpec(memory_space=pl.ANY)
    sd = jax.ShapeDtypeStruct
    dma = pltpu.SemaphoreType.DMA
    vm = pltpu.VMEM
    return pl.pallas_call(
        functools.partial(forward_kernel, nz),
        out_shape=[sd((S, 4, RP, D), bf16), sd((S, 4, RP, D), bf16), sd((S, 2, 2 * SPAN, 128), bf16),
                   sd((S, nz, SPAN, 384), bf16), sd((S, 2, 2 * SPAN, 128), bf16), sd((S, 2, 1, 2 * SPAN), f32),
                   sd((D, 896), bf16), sd((512, D), bf16), sd((S, RP, D), f32), sd((S, RP, D), bf16)],
        in_specs=[V] * 13,
        out_specs=[A] * 8 + [V] * 2,
        scratch_shapes=[vm((S, RP, D), bf16), vm((S, 4, RP, D), bf16), vm((S, 4, RP, D), bf16),
                        vm((S, nz, SPAN, 384), bf16), vm((S, 2, 2 * SPAN, 128), bf16),
                        vm((S, 2, 2 * SPAN, 128), bf16), vm((S, 2, 1, 2 * SPAN), f32), vm((D, 896), bf16), vm((512, D), bf16),
                        vm((S, 2, 1, 2 * SPAN), f32), vm((S, 2, 1, 2 * SPAN), f32), vm((S, 2, 256, 2 * SPAN), f32),
                        vm((S, 2, 2, RP, D), bf16), vm((S, 2, RP, D), bf16), vm((S, RP, D), bf16), vm((S, RP, D), bf16)]
        + [dma((2, S))] * 6 + [dma((S, nz, 2))] * 2 + [dma((S,))] * 4 + [dma((8,))],
        compiler_params=pltpu.CompilerParams(collective_id=0, has_side_effects=True, vmem_limit_bytes=VMEM_BYTES),
        name="attend_forward")(tok, cot, wq, wk, wv, w_out, pq, pkv, po, cos, sin, gain1, gain2)


def feed_kernel(n2, mid, c_in, wg_in, wu_in, wd_in, gain2,
                db_out, ga_out, gb_out, down_out, dmid_out, gpart_out,
                X, C, DB, dn, wg, wu, wd, dh, F, G, part, rs1, ysend, rs2, pd,
                sA, rA, sB, rB, sC, rC, sR1, rR1, sR2, rR2, isem, osem):
    t = lax.axis_index("tensor")
    sib, ynb = t ^ 1, t ^ 2
    S, RP, D = n2.shape
    FL = wg.shape[1]
    loads = [pltpu.make_async_copy(a, b, isem.at[i]) for i, (a, b) in enumerate(
        ((wd_in, wd), (c_in, C), (wg_in, wg), (wu_in, wu)))]
    for c in loads:
        c.start()
    entry([{"tensor": sib}, {"tensor": ynb}], False)

    def ga(w, s):
        return rc((n2, dn)[w].at[s], (X, DB)[w].at[s, 1], sA.at[w, s], rA.at[w, s], {"tensor": sib})
    def gb(w, s):
        return rc((n2, dn)[w].at[s], (X, DB)[w].at[s, 2], sB.at[w, s], rB.at[w, s], {"tensor": ynb})
    def gc(w, s):
        buf = (X, DB)[w]
        return rc(buf.at[s, 2], buf.at[s, 3], sC.at[w, s], rC.at[w, s], {"tensor": sib})
    def ra(s, hb):
        return rc(part.at[s, 1, hb], rs1.at[s, hb], sR1.at[s, hb], rR1.at[s, hb], {"tensor": sib})
    def rb(s):
        return rc(ysend.at[s], rs2.at[s], sR2.at[s], rR2.at[s], {"tensor": ynb})
    for s in range(S):
        gb(0, s).start()
        ga(0, s).start()
    for s in range(S):
        X[s, 0] = n2[s]
    loads[0].wait()
    loads[1].wait()
    def early(s, c):
        dh[s] = nt(C[s].reshape(4 * RP, D), wd[...])
        return c
    lax.fori_loop(0, S, early, 0)
    loads[2].wait()
    loads[3].wait()

    def mlp(s, hb):
        x = X[s, pl.ds(2 * hb, 2)].reshape(2 * RP, D)
        rows = pl.ds(pl.multiple_of(hb * 2 * RP, 2 * RP), 2 * RP)
        g = nn(x, wg[...])
        u = nn(x, wu[...])
        sg = 1.0 / (1.0 + jnp.exp(-g))
        si = g * sg
        d = dh[s, rows]
        F[2, s, rows] = (si * u).astype(bf16)
        F[0, s, rows] = (d * u * sg * (1.0 + g * (1.0 - sg))).astype(bf16)
        F[1, s, rows] = (d * si).astype(bf16)
        r = nt(F[0, s, rows], wg[...]) + nt(F[1, s, rows], wu[...])
        part[s, 0, hb] = r[:RP].astype(bf16)
        part[s, 1, hb] = r[RP:].astype(bf16)
        ra(s, hb).start()
    def rs_mid(s):
        ra(s, 1).wait_recv()
        ysend[s] = (part[s, 0, 1].astype(f32) + rs1[s, 1].astype(f32)).astype(bf16)
        rb(s).start()
    gain = gain2[...].astype(f32)
    def rs_end(s):
        ra(s, 0).wait_recv()
        rb(s).wait_recv()
        e = part[s, 0, 0].astype(f32) + rs1[s, 0].astype(f32) + rs2[s].astype(f32)
        gp, dv = norm_back_rows(mid[s], e, gain)
        if s == 0:
            gpart_out[...] = gp
        else:
            gpart_out[...] += gp
        dm = C[s, 0].astype(f32) + dv
        dmid_out[s] = dm
        dn[s] = dm.astype(bf16)
        gb(1, s).start()
        ga(1, s).start()
        DB[s, 0] = dn[s]

    CH = 512
    def wgrad(a, src, f, c):
        at = pl.ds(pl.multiple_of(c * CH, CH), CH)
        left = src[:, :, :, at].reshape(S * 4 * RP, CH).T
        G[a, at, :] = nn(left, F[f].reshape(S * 4 * RP, FL)).astype(bf16)
    def down(s):
        r = nn(F[2, s], wd[...]).astype(bf16)
        for p in range(4):
            pd[t ^ p, s] = r[p * RP:(p + 1) * RP]

    ga(0, 0).wait_recv()
    mlp(0, 0)
    gb(0, 0).wait_recv()
    gc(0, 0).start()
    gc(0, 0).wait_recv()
    mlp(0, 1)
    ga(0, 1).wait_recv()
    gb(0, 1).wait_recv()
    gc(0, 1).start()
    rs_mid(0)
    mlp(1, 0)
    gc(0, 1).wait_recv()
    mlp(1, 1)
    rs_end(0)
    rs_mid(1)
    lax.fori_loop(0, D // CH, lambda c, x: (wgrad(2, C, 2, c), x)[1], 0)
    o_down = pltpu.make_async_copy(G.at[2], gb_out, osem.at[0])
    o_down.start()
    down(0)
    down(1)
    o_pd = pltpu.make_async_copy(pd, down_out, osem.at[1])
    o_pd.start()
    gb(1, 0).wait_recv()
    gc(1, 0).start()
    rs_end(1)
    lax.fori_loop(0, D // CH, lambda c, x: (wgrad(0, X, 0, c), x)[1], 0)
    lax.fori_loop(0, D // CH, lambda c, x: (wgrad(1, X, 1, c), x)[1], 0)
    o_up = pltpu.make_async_copy(G.at[pl.ds(0, 2)], ga_out, osem.at[2])
    o_up.start()
    gb(1, 1).wait_recv()
    gc(1, 1).start()
    for s in range(S):
        ga(1, s).wait_recv()
        gc(1, s).wait_recv()
    o_db = pltpu.make_async_copy(DB, db_out, osem.at[3])
    o_db.start()
    for s in range(S):
        for w in range(2):
            ga(w, s).wait_send()
            gb(w, s).wait_send()
            gc(w, s).wait_send()
        ra(s, 0).wait_send()
        ra(s, 1).wait_send()
        rb(s).wait_send()
    for o in (o_down, o_pd, o_up, o_db):
        o.wait()


def feed_forward(n2, mid, C, wg, wu, wd, gain2):
    S, RP, D = n2.shape
    FL = wg.shape[1]
    V = pl.BlockSpec(memory_space=pltpu.VMEM)
    A = pl.BlockSpec(memory_space=pl.ANY)
    sd = jax.ShapeDtypeStruct
    dma = pltpu.SemaphoreType.DMA
    vm = pltpu.VMEM
    return pl.pallas_call(
        feed_kernel,
        out_shape=[sd((S, 4, RP, D), bf16), sd((2, D, FL), bf16), sd((D, FL), bf16), sd((4, S, RP, D), bf16),
                   sd((S, RP, D), f32), sd((1, D), f32)],
        in_specs=[V, V, A, A, A, A, V],
        out_specs=[A, A, A, A, V, V],
        scratch_shapes=[vm((S, 4, RP, D), bf16), vm((S, 4, RP, D), bf16), vm((S, 4, RP, D), bf16), vm((S, RP, D), bf16),
                        vm((D, FL), bf16), vm((D, FL), bf16), vm((FL, D), bf16), vm((S, 4 * RP, FL), f32),
                        vm((3, S, 4 * RP, FL), bf16), vm((3, D, FL), bf16), vm((S, 2, 2, RP, D), bf16), vm((S, 2, RP, D), bf16),
                        vm((S, RP, D), bf16), vm((S, RP, D), bf16), vm((4, S, RP, D), bf16)]
        + [dma((2, S))] * 6 + [dma((S, 2))] * 2 + [dma((S,))] * 2 + [dma((4,)), dma((4,))],
        compiler_params=pltpu.CompilerParams(collective_id=1, has_side_effects=True, vmem_limit_bytes=VMEM_BYTES),
        name="feed_forward")(n2, mid, C, wg, wu, wd, gain2)


def line(u, nz):
    zi = lax.axis_index("seq")
    root = nz // 2 - 1 + u
    below, above = zi < root, zi > root
    dist = jnp.where(below, root - zi, zi - root)
    return dist, below, above, zi == root, jnp.where(below, zi + 1, zi - 1)


def both(a, b):
    return jnp.logical_and(a, b)


def add(*refs):
    total = refs[0][...].astype(f32)
    for r in refs[1:]:
        total = total + r[...].astype(f32)
    return total.astype(bf16)


class Flow:
    def setup(self, n, p, lag):
        self.n, self.p, self.lag = n, p, lag
        self.nz = lax.axis_size("seq")
        self.far = self.nz // 2
    def at(self, i):
        return pl.ds(pl.multiple_of(i * self.p, self.p), self.p)
    def valid(self, i):
        return both(i >= 0, i < self.n)
    def send_in(self, u, i, own, main, short, sems, act):
        dist, below, above, root, inward = line(u, self.nz)
        ss, rr, r2 = sems
        to_short = both(dist == 1, below if u == 0 else above)
        @pl.when(to_short)
        def _():
            act(rc(own, short.at[self.at(i)], ss.at[u, i], r2.at[i], {"seq": inward}))
        @pl.when(jnp.logical_not(to_short))
        def _():
            act(rc(own, main.at[u, self.at(i)], ss.at[u, i], rr.at[u, i], {"seq": inward}))
    def from_main(self, u, i, own, main, sems):
        ss, rr, r2 = sems
        rc(own, main.at[u, self.at(i)], ss.at[u, i], rr.at[u, i], {"seq": line(u, self.nz)[4]}).wait_recv()
    def from_short(self, u, i, own, short, sems):
        ss, rr, r2 = sems
        rc(own, short.at[self.at(i)], ss.at[u, i], r2.at[i], {"seq": line(u, self.nz)[4]}).wait_recv()
    def outward(self, u, i, buf, bs, br, act):
        zi = lax.axis_index("seq")
        dist, below, above, root, inward = line(u, self.nz)
        @pl.when(both(jnp.logical_not(above), zi > 0))
        def _():
            act(rc(buf.at[u, self.at(i)], buf.at[u, self.at(i)], bs.at[0, u, i], br.at[u, i], {"seq": zi - 1}))
        @pl.when(both(jnp.logical_not(below), zi < self.nz - 1))
        def _():
            act(rc(buf.at[u, self.at(i)], buf.at[u, self.at(i)], bs.at[1, u, i], br.at[u, i], {"seq": zi + 1}))
    def has_farther(self, u):
        zi = lax.axis_index("seq")
        dist, below, above, root, inward = line(u, self.nz)
        return jnp.logical_or(both(below, zi > 0), both(above, zi < self.nz - 1))


class HalfFirst(Flow):
    count = 11
    @staticmethod
    def scratch(n, p, C):
        vm = pltpu.VMEM
        dma = pltpu.SemaphoreType.DMA
        Q = n * p
        return [vm((2, Q, C), bf16), vm((2, Q, C), bf16), vm((Q, C), bf16),
                dma((n,)), dma((n,)), dma((2, n)), dma((2, n)), dma((n,)), dma((2, 2, n)), dma((2, n)), dma((2, 2, n))]
    def __init__(self, src, own, out, bufs, osem, n, p, lag):
        self.setup(n, p, lag)
        self.src, self.own, self.out, self.osem = src, own, out, osem
        self.RX, self.RZ, self.R2, self.x1s, self.x1r, self.rs, self.rr, self.r2, self.bs, self.br, self.x2 = bufs
        self.ticks = n + lag * (2 * self.far + 2)
    def tick(self, k):
        lag, far, RX, RZ, R2 = self.lag, self.far, self.RX, self.RZ, self.R2
        xi = lax.axis_index("dp")
        ox = 1 - xi
        sems = (self.rs, self.rr, self.r2)
        start = lambda c: c.start()
        def x1(i):
            return rc(self.src.at[ox, :, self.at(i)], RX.at[:, self.at(i)], self.x1s.at[i], self.x1r.at[i], {"dp": ox})
        def x2(u, i):
            return rc(RX.at[u, self.at(i)], self.out.at[xi, u, self.at(i)], self.x2.at[0, u, i], self.x2.at[1, u, i], {"dp": ox})
        @pl.when(self.valid(k))
        def _():
            x1(k).start()
        i1 = k - lag
        @pl.when(self.valid(i1))
        def _():
            x1(i1).wait()
            for u in range(2):
                own = self.own(u).at[self.at(i1)]
                own[...] = add(own, RX.at[u, self.at(i1)])
        for u in range(2):
            dist, below, above, root, inward = line(u, self.nz)
            i = k - lag * (1 + far - dist)
            @pl.when(self.valid(i))
            def _():
                own = self.own(u).at[self.at(i)]
                @pl.when(jnp.logical_not(root))
                def _():
                    @pl.when(self.has_farther(u))
                    def _():
                        self.from_main(u, i, own, RZ, sems)
                        own[...] = add(own, RZ.at[u, self.at(i)])
                    self.send_in(u, i, own, RZ, R2, sems, start)
                @pl.when(root)
                def _():
                    self.from_main(u, i, own, RZ, sems)
                    self.from_short(u, i, own, R2, sems)
                    RX[u, self.at(i)] = add(own, RZ.at[u, self.at(i)], R2.at[self.at(i)])
                    self.outward(u, i, RX, self.bs, self.br, start)
                    x2(u, i).start()
            i = k - lag * (1 + far + dist)
            @pl.when(both(self.valid(i), jnp.logical_not(root)))
            def _():
                rc(RX.at[u, self.at(i)], RX.at[u, self.at(i)], self.bs.at[0, u, i], self.br.at[u, i], {"seq": inward}).wait_recv()
                self.outward(u, i, RX, self.bs, self.br, start)
                x2(u, i).start()
            i = i - lag
            @pl.when(self.valid(i))
            def _():
                x2(u, i).wait()
                @pl.when(jnp.logical_not(root))
                def _():
                    self.send_in(u, i, self.own(u).at[self.at(i)], RZ, R2, sems, lambda c: c.wait_send())
                self.outward(u, i, RX, self.bs, self.br, lambda c: c.wait_send())
                pltpu.make_async_copy(RX.at[u, self.at(i)], self.out.at[xi, u, self.at(i)], self.osem).start()
    def drain(self):
        xi = lax.axis_index("dp")
        pltpu.make_async_copy(self.RX, self.out.at[xi], self.osem).wait()


class LineFirst(Flow):
    count = 11
    @staticmethod
    def scratch(n, p, C):
        vm = pltpu.VMEM
        dma = pltpu.SemaphoreType.DMA
        Q = n * p
        return [vm((2, Q, C), bf16), vm((2, Q, C), bf16), vm((Q, C), bf16), vm((Q, C), bf16),
                dma((2, n)), dma((2, n)), dma((n,)), dma((2, 2, n)), dma((2, n)), dma((n,)), dma((n,))]
    def __init__(self, out, bufs, osem, n, p, lag):
        self.setup(n, p, lag)
        self.out, self.osem = out, osem
        self.W, self.Z, self.XB, self.R2, self.rs, self.rr, self.r2, self.bs, self.br, self.xs, self.xr = bufs
        self.ticks = n + lag * (2 * self.far + 2)
    def tick(self, k):
        lag, far, W, Z = self.lag, self.far, self.W, self.Z
        ox = 1 - lax.axis_index("dp")
        sems = (self.rs, self.rr, self.r2)
        start = lambda c: c.start()
        def xb(u, i):
            return rc(W.at[u, self.at(i)], self.XB.at[self.at(i)], self.xs.at[i], self.xr.at[i], {"dp": ox})
        for u in range(2):
            dist, below, above, root, inward = line(u, self.nz)
            i = k - lag * (far - dist)
            @pl.when(self.valid(i))
            def _():
                own = W.at[u, self.at(i)]
                @pl.when(jnp.logical_not(root))
                def _():
                    @pl.when(self.has_farther(u))
                    def _():
                        self.from_main(u, i, own, Z, sems)
                        own[...] = add(own, Z.at[u, self.at(i)])
                    self.send_in(u, i, own, Z, self.R2, sems, start)
                @pl.when(root)
                def _():
                    self.from_main(u, i, own, Z, sems)
                    self.from_short(u, i, own, self.R2, sems)
                    own[...] = add(own, Z.at[u, self.at(i)], self.R2.at[self.at(i)])
                    xb(u, i).start()
            i = k - lag * (far + 1)
            @pl.when(both(self.valid(i), root))
            def _():
                xb(u, i).wait()
                Z[u, self.at(i)] = add(W.at[u, self.at(i)], self.XB.at[self.at(i)])
                self.outward(u, i, Z, self.bs, self.br, start)
            i = k - lag * (far + 1 + dist)
            @pl.when(both(self.valid(i), jnp.logical_not(root)))
            def _():
                rc(Z.at[u, self.at(i)], Z.at[u, self.at(i)], self.bs.at[0, u, i], self.br.at[u, i], {"seq": inward}).wait_recv()
                self.outward(u, i, Z, self.bs, self.br, start)
            i = i - lag
            @pl.when(self.valid(i))
            def _():
                @pl.when(jnp.logical_not(root))
                def _():
                    self.send_in(u, i, W.at[u, self.at(i)], Z, self.R2, sems, lambda c: c.wait_send())
                self.outward(u, i, Z, self.bs, self.br, lambda c: c.wait_send())
                pltpu.make_async_copy(Z.at[u, self.at(i)], self.out.at[u, self.at(i)], self.osem).start()
    def drain(self):
        pltpu.make_async_copy(self.Z, self.out, self.osem).wait()


def backward_kernel(summed, n1, n2, lag, db_in, q_in, kv_in, att_in, lse, wo_in, wt_in, x1_in, pq, pkv, po, cos, sin, tok, dmid_in, gain1, gp2,
                    ga_in, gb_in, ig_out, gains_out, oa, ob, oc, *scr):
    t = lax.axis_index("tensor")
    zi = lax.axis_index("seq")
    nz = lax.axis_size("seq")
    sib, ynb = t ^ 1, t ^ 2
    S, RP, D = tok.shape
    SPAN = 4 * RP
    TQ = 512
    NT = 2 * SPAN // TQ
    HC = D // 4
    scr = list(scr)
    (DB, q, KV, att, wbuf, da, delta, dqT, acc, PB, RB, dqkv, rs1, rs2, W3, GS, GL,
     sKV, rKV, sR1, rR1, sR2, rR2, sG, rG, isem, sems_out) = scr[:27]
    scr = scr[27:]
    xi = lax.axis_index("dp")
    rings = []
    loads = [pltpu.make_async_copy(a, b, isem.at[i]) for i, (a, b) in enumerate(
        ((db_in, DB), (wo_in, wbuf.at[pl.ds(0, 512)]), (att_in, att), (q_in, q), (kv_in, KV), (dmid_in, ig_out)))]
    first = []
    if summed:
        own = scr.pop(0)
        Q1 = own.shape[1]
        b1, scr = scr[:HalfFirst.count], scr[HalfFirst.count:]
        b2, scr = scr[:LineFirst.count], scr[LineFirst.count:]
        b3, scr = scr[:HalfFirst.count], scr[HalfFirst.count:]
        ring_a = HalfFirst(ga_in, lambda u: own.at[u], oa, b1, sems_out.at[0], n1, Q1 // n1, lag)
        ring_b = LineFirst(ob, b2, sems_out.at[1], n1, gb_in.shape[1] // n1, lag)
        ring_c = HalfFirst(W3, lambda u: W3.at[xi, u], oc, b3, sems_out.at[2], n2, HC // n2, lag)
        first = [pltpu.make_async_copy(ga_in.at[xi], own, isem.at[6]), pltpu.make_async_copy(gb_in, ring_b.W, isem.at[7])]
    wt_load = pltpu.make_async_copy(wt_in, wbuf, isem.at[8])
    x1_loads = [pltpu.make_async_copy(x1_in.at[:, :, pl.ds(c * HC, HC)], PB.at[pl.ds(S * c, S)], isem.at[9 + c]) for c in range(4)]
    for c in loads[:2] + first + loads[2:]:
        c.start()
    devs = [{"tensor": sib}, {"tensor": ynb}]
    if summed:
        devs.append({"dp": 1 - xi})
        b = 2
        while b < nz:
            devs.append({"seq": zi ^ b})
            b *= 2
    entry(devs, True)
    def tick(k):
        if summed:
            ring_a.tick(k)
            ring_b.tick(k)
    loads[0].wait()
    loads[1].wait()

    def dast(it, c):
        s = it // 2
        hb = it % 2
        r = nt(DB[s, pl.ds(2 * hb, 2)].reshape(2 * RP, D), wbuf[0:512, :])
        for h in range(4):
            rows = pl.ds(pl.multiple_of((h % 2) * SPAN + hb * 2 * RP, 2 * RP), 2 * RP)
            da[s, h // 2, rows, :] = r[:, h * 128:(h + 1) * 128].astype(bf16)
        @pl.when(it == 0)
        def _():
            for c2 in first:
                c2.wait()
        tick(it)
        return c
    lax.fori_loop(0, 2 * S, dast, 0)
    wt_load.start()
    k = 2 * S
    loads[2].wait()
    def dlt(it, c):
        s = it // 2
        g = it % 2
        d = da[s, g].astype(f32) * att[s, g].astype(f32)
        delta[s, g] = jnp.sum(d.T, axis=0, keepdims=True)
        dqT[s, g] = jnp.zeros((128, 2 * SPAN), f32)
        return c
    lax.fori_loop(0, 2 * S, dlt, 0)
    for c in loads[3:5]:
        c.wait()

    def unit(s, j, diag):
        lane = lax.broadcasted_iota(jnp.int32, (1, 128), 1)
        acc[...] = jnp.zeros((SPAN, 384), f32)
        for g in range(2):
            fm = in_ranges(lane, F_LANES[g])
            def body(qt, c):
                qa = pl.ds(pl.multiple_of(qt * TQ, TQ), TQ)
                kp = KV[s, j, :, g * 128:(g + 1) * 128]
                kv = jnp.concatenate([kp, KV[s, j, :, 256:384]], axis=1)
                qq = q[s, g, qa, :]
                d = da[s, g, qa, :]
                zero = jnp.zeros_like(d)
                d2 = jnp.concatenate([jnp.where(fm, d, zero), jnp.where(fm, zero, d)], axis=1)
                sT = nt(kp, qq) * (SCALE * LOG2E) - lse[s, g, :, qa]
                if diag:
                    sT = causal(sT, qt, TQ, RP, t)
                p = jnp.exp2(sT)
                ds = (p * (nt(kv, d2) - delta[s, g, :, qa])).astype(bf16)
                dk = nn(ds, qq) * SCALE
                dv = nn(p.astype(bf16), d2)
                acc[:, g * 128:(g + 1) * 128] += dk + dv[:, :128]
                acc[:, 256:384] += dv[:, 128:]
                dqT[s, g, :, qa] += tn(kp, ds)
                return c
            lax.fori_loop(0, NT, body, 0, unroll=2)
        PB[j * S + s] = acc[...].astype(bf16)

    def chain(s, j):
        return rc(RB.at[j, s], RB.at[j, s], sKV.at[j, s], rKV.at[j, s], {"seq": zi - 1})
    def event(e):
        j = e // S
        s = e % S
        @pl.when(both(both(e >= 0, e < nz * S), j <= zi))
        def _():
            acc[...] = PB[e].astype(f32)
            @pl.when(zi < nz - 1)
            def _():
                chain(s, j).wait_recv()
                acc[...] += RB[j, s].astype(f32)
            @pl.when(j < zi)
            def _():
                RB[j, s] = acc[...].astype(bf16)
                chain(s, j).start()
            @pl.when(j == zi)
            def _():
                for g in range(2):
                    u = acc[:, g * 128:(g + 1) * 128]
                    dqkv[s, :, 512 + g * 128:512 + (g + 1) * 128] = (u * cos[g] - pltpu.roll(u, 64, 1) * sin[g]).astype(bf16)
                dqkv[s, :, 768:896] = acc[:, 256:384].astype(bf16)
    def step(m, c):
        j = m // S
        s = m % S
        @pl.when(j < zi)
        def _():
            unit(s, j, False)
        @pl.when(j == zi)
        def _():
            unit(s, j, True)
        event(m - 1 - (nz - 1 - zi))
        tick(k + m)
        return c
    steps = nz * S + nz
    lax.fori_loop(0, steps, step, 0)
    k = k + steps
    for c in x1_loads:
        c.start()

    def out_grad(c, x):
        left = DB[:, :, :, pl.ds(pl.multiple_of(c * HC, HC), HC)].reshape(S * SPAN, HC).T
        heads = jnp.concatenate([jnp.concatenate([att[s, g, hh * SPAN:(hh + 1) * SPAN, :] for g in range(2) for hh in range(2)], axis=1)
                                 for s in range(S)], axis=0)
        g0 = nn(left, heads).astype(bf16)
        W3[c // 2, c % 2, :, 0:384] = nn(g0, po[...]).astype(bf16)
        s = c // 2
        for g in range(2):
            @pl.when(c % 2 == g)
            def _():
                for hh in range(2):
                    u = dqT[s, g, :, hh * SPAN:(hh + 1) * SPAN].T * SCALE
                    dqkv[s, :, (2 * g + hh) * 128:(2 * g + hh + 1) * 128] = (u * cos[g] - pltpu.roll(u, 64, 1) * sin[g]).astype(bf16)
        tick(k + c)
        return x
    lax.fori_loop(0, 4, out_grad, 0)
    k = k + 4
    wt_load.wait()

    def ra(s, hb):
        return rc(DB.at[s, 2 + hb], rs1.at[s, hb], sR1.at[s, hb], rR1.at[s, hb], {"tensor": sib})
    def rb(s):
        return rc(DB.at[s, 1], rs2.at[s], sR2.at[s], rR2.at[s], {"tensor": ynb})
    def d_one(it, c):
        s = it // 2
        hb = 1 - it % 2
        rows = pl.ds(pl.multiple_of(hb * 2 * RP, 2 * RP), 2 * RP)
        r = nn(dqkv[s, rows, :], wbuf[...])
        DB[s, hb] = r[:RP].astype(bf16)
        DB[s, 2 + hb] = r[RP:].astype(bf16)
        ra(s, hb).start()
        tick(k + it)
        return c
    lax.fori_loop(0, 2 * S, d_one, 0)
    k = k + 2 * S
    for s in range(S):
        ra(s, 1).wait_recv()
        DB[s, 1] = add(DB.at[s, 1], rs1.at[s, 1])
        rb(s).start()
    for c in x1_loads:
        c.wait()
    def in_grad(c, x):
        left = PB[pl.ds(S * c, S)].reshape(S * SPAN, HC).T
        g0 = nn(left, dqkv[...].reshape(S * SPAN, 896)).astype(bf16)
        W3[c // 2, c % 2, :, 384:768] = nt(g0[:, 0:512], pq[...]).astype(bf16)
        W3[c // 2, c % 2, :, 768:1152] = nt(g0[:, 512:896], pkv[...]).astype(bf16)
        tick(k + c)
        return x
    lax.fori_loop(0, 4, in_grad, 0)
    k = k + 4
    if summed:
        k_c = k
        def joint(m):
            tick(m)
            ring_c.tick(m - k_c)
    else:
        o3 = pltpu.make_async_copy(W3, oc, sems_out.at[2])
        o3.start()
        def joint(m):
            pass
    joint(k)
    joint(k + 1)
    k = k + 2
    loads[5].wait()
    gain = gain1[...].astype(f32)
    gp1 = None
    for s in range(S):
        ra(s, 0).wait_recv()
        rb(s).wait_recv()
        e = DB[s, 0].astype(f32) + rs1[s, 0].astype(f32) + rs2[s].astype(f32)
        gp, dv = norm_back_rows(tok[s].astype(f32), e, gain)
        gp1 = gp if gp1 is None else gp1 + gp
        ig_out[s] += dv
    gains_out[...] = jnp.concatenate([gp1, gp2[...], jnp.zeros((6, D), f32)], axis=0)
    if summed:
        peers = [{"tensor": sib}, {"tensor": ynb}, {"dp": 1 - xi}]
        b = 1
        while b < nz:
            peers.append({"seq": zi ^ b})
            b *= 2
        for m, dev in enumerate(peers):
            GS[m] = gains_out[...]
            c = rc(GS.at[m], GL.at[m], sG.at[m], rG.at[m], dev)
            c.start()
            joint(k)
            k = k + 1
            c.wait()
            gains_out[...] += GL[m]
        last = max(ring_a.ticks, ring_b.ticks, k_c + ring_c.ticks)
        lax.fori_loop(k, last, lambda m, c: (joint(m), c)[1], 0)
    for s in range(S):
        ra(s, 0).wait_send()
        ra(s, 1).wait_send()
        rb(s).wait_send()
        for j in range(nz):
            @pl.when(j < zi)
            def _():
                chain(s, j).wait_send()
    if summed:
        ring_a.drain()
        ring_b.drain()
        ring_c.drain()
    else:
        o3.wait()


def attend_backward(DB, q, KV, att, lse, wo, wt, X1, pq, pkv, po, cos, sin, tok, dmid, gain1, gp2, ga, gb, summed, n1=24, n2=12, lag=1):
    nz = lax.axis_size("seq")
    S, RP, D = tok.shape
    SPAN = 4 * RP
    FL = ga.shape[-1]
    HC = D // 4
    Q1 = ga.shape[0] * ga.shape[1] // 4
    Q2 = gb.shape[0] // 2
    V = pl.BlockSpec(memory_space=pltpu.VMEM)
    A = pl.BlockSpec(memory_space=pl.ANY)
    sd = jax.ShapeDtypeStruct
    dma = pltpu.SemaphoreType.DMA
    vm = pltpu.VMEM
    scratch = [vm(DB.shape, bf16), vm(q.shape, bf16), vm(KV.shape, bf16), vm(att.shape, bf16), vm((896, D), bf16),
               vm(q.shape, bf16), vm((S, 2, 1, 2 * SPAN), f32), vm((S, 2, 128, 2 * SPAN), f32), vm((SPAN, 384), f32),
               vm((nz * S, SPAN, 384), bf16), vm((nz - 1, S, SPAN, 384), bf16), vm((S, SPAN, 896), bf16),
               vm((S, 2, RP, D), bf16), vm((S, RP, D), bf16), vm((2, 2, HC, 1152), bf16), vm((6, 8, D), f32), vm((6, 8, D), f32),
               dma((nz, S)), dma((nz, S)), dma((S, 2)), dma((S, 2)), dma((S,)), dma((S,)), dma((6,)), dma((6,)), dma((13,)), dma((3,))]
    if summed:
        scratch += [vm((2, Q1, FL), bf16)] + HalfFirst.scratch(n1, Q1 // n1, FL) + LineFirst.scratch(n1, Q2 // n1, FL)
        scratch += HalfFirst.scratch(n2, HC // n2, 1152)
    return pl.pallas_call(
        functools.partial(backward_kernel, summed, n1, n2, lag),
        out_shape=[sd((S, RP, D), f32), sd((8, D), f32), sd((2, 2, Q1, FL), bf16), sd((2, Q2, FL), bf16), sd((2, 2, HC, 1152), bf16)],
        in_specs=[A, A, A, A, V, A, A, A, V, V, V, V, V, V, A, V, V, A, A],
        out_specs=[V, V, A, A, A],
        scratch_shapes=scratch,
        compiler_params=pltpu.CompilerParams(collective_id=2, has_side_effects=True, vmem_limit_bytes=VMEM_BYTES),
        name="attend_backward")(DB, q, KV, att, lse, wo, wt, X1.reshape(S, SPAN, D), pq, pkv, po, cos, sin, tok, dmid, gain1, gp2,
                                ga.reshape(2, 2, Q1, FL), gb.reshape(2, Q2, FL))


def local(
    tokens, attn_gain, w_query, w_key, w_value, w_output, ffn_gain, w_gate, w_up, w_down, cotangent
):
    t = lax.axis_index("tensor")
    zi = lax.axis_index("seq")
    kept = w_query.shape[1]
    kv = w_key.shape[1]
    pq, pkv, po = (jnp.asarray(v, bf16) for v in pick_tables())
    tok = jnp.swapaxes(tokens, 0, 1)
    cot = jnp.swapaxes(cotangent, 0, 1)
    S, RP, D = tok.shape
    cos, sin = rope_tables(zi * 4 * RP, 4 * RP, t)
    gain1 = attn_gain.reshape(1, -1)
    gain2 = ffn_gain.reshape(1, -1)
    X1, C, q, KV, att, lse, wqkv, wo, mid, n2 = attend_forward(
        tok, cot, w_query, w_key, w_value, w_output, pq, pkv, po, cos, sin, gain1, gain2)
    DB, ga, gb, down, dmid, gp2 = feed_forward(n2, mid, C, w_gate, w_up, w_down, gain2)
    down_local = lax.psum_scatter(down, "tensor", scatter_dimension=0, tiled=True)[0]
    summed = lax.axis_size("dp") == 2
    ig, gains, oa, ob, oc = attend_backward(
        DB, q, KV, att, lse, wo, wqkv.T, X1, pq, pkv, po, cos, sin, tok, dmid, gain1, gp2, ga, gb, summed)
    FL = w_gate.shape[1]
    if summed:
        gate_up, down_t = oa.reshape(2, D, FL).astype(f32), ob.reshape(D, FL).astype(f32)
        rest = oc.reshape(D, -1).astype(f32)
    else:
        gate_up, down_t, rest = lax.psum((ga.astype(f32), gb.astype(f32), oc.reshape(D, -1).astype(f32)), ("dp", "seq"))
        gains = lax.psum(gains, ("dp", "seq", "tensor"))
    activation = (mid + down_local.astype(f32)).astype(bf16)
    return (
        jnp.swapaxes(activation, 0, 1),
        jnp.swapaxes(ig, 0, 1),
        gains[0],
        rest[:, kept:2 * kept],
        rest[:, 2 * kept:2 * kept + kv],
        rest[:, 2 * kept + kv:],
        rest[:, :kept].T,
        gains[1],
        gate_up[0],
        gate_up[1],
        down_t.T,
    )


def solution(mesh):
    rows = P(("seq", "tensor"), "dp", None)
    columns = P(None, "tensor")
    placed = (rows, P(), columns, columns, columns, P("tensor", None), P(), columns, columns, P("tensor", None), rows)
    return jax.shard_map(
        local,
        mesh=mesh,
        in_specs=placed,
        out_specs=(rows, rows, P(), columns, columns, columns, P("tensor", None), P(), columns, columns, P("tensor", None)),
        check_vma=False,
    )
```

time: 1620 us -> 546 us (0.34)
  waiting for transfers between devices: 1180 us -> 0.02 us
  Pallas kernels: 0 us -> 468 us
  matrix products: 282 us -> 0 us
  blocking collectives: 50.9 us -> 0 us
  other arithmetic: 40.7 us -> 8.76 us
    psum x1 -> x0, waiting for transfers between devices: 725 us -> none  [local(): lax.psum((query_grad, key_grad, value_grad, output_grad, attn_gain_part,...]
    pallas_call x0 -> x3, Pallas kernels: none -> 468 us  [the longest x1 337 us: attend_backward(): pl.pallas_call(functools.partial(backward_kernel, summed, n1, n2, lag), o...]
    reduce_scatter x6 -> x1, waiting for transfers between devices: 283 us -> 0.01 us  [local(): lax.psum_scatter(down, 'tensor', scatter_dimension=0, tiled=True)[0]]
    dot_general x35 -> x0, matrix products: 282 us -> none  [the longest x2 50.3 us: attend_backward(): jnp.einsum('kgct,ckgd->tkd', d_scores, grouped, preferred_element_type=jn...]
    all_gather x6 -> x0, waiting for transfers between devices: 169 us -> none  [the longest x1 38.1 us: local(): lax.all_gather(value_low, 'seq', axis=0, tiled=True)]
    psum x2 -> x0, blocking collectives: 50.9 us -> none  [the longest x1 39.4 us: local(): lax.psum((query_grad, key_grad, value_grad, output_grad, attn_gain_part,...]
  transfers between devices with their start and end apart: 13 -> 1, of which waited for: 13 -> 0; matrix products, arithmetic and copies ran while one was open for 5% -> 7% of each run, Pallas kernels for 0% -> 63%
where the time goes in v1:
time: 546 us; the launch traced here: 538 us
  Pallas kernels  468 us (86%)
  local copies, waits for them, and re-layouts  46.8 us (9%)
  between operations  14.6 us (3%)
  other arithmetic  8.76 us (2%)
    pallas_call x1, Pallas kernels, attend_backward(): pl.pallas_call(functools.partial(backward_kernel, summed, n1, n2, lag), o...  337 us
    pallas_call x1, Pallas kernels, attend_forward(): pl.pallas_call(functools.partial(forward_kernel, nz), out_shape=[sd((S, 4...  65.6 us
    pallas_call x1, Pallas kernels, feed_forward(): pl.pallas_call(feed_kernel, out_shape=[sd((S, 4, RP, D), bf16), sd((2, D,...  64.9 us
    unnamed x25, local copies, waits for them, and re-layouts  18.3 us
  transfers between devices with their start and end apart: 1, of which 0 were waited for; matrix products, arithmetic and copies ran while one was open for 7% of the time, Pallas kernels for 63%

profile of v1, /device:TPU:0, one launch (start us, length us, event | category | flops | bytes accessed | tf_op | source)
XLA Modules:
  0.0 538.0 jit_solution(8779233794539417929)
XLA Ops:
  7.2 0.0 copy-start.7
  7.2 0.0 copy-start.8
  7.2 0.0 copy-start.5
  7.2 0.0 copy-start.6
  7.2 0.0 reduce-scatter.2.cloned.1.call-start
  7.3 1.4 reshape.77.gain1
  8.7 1.3 reshape.78.gain2
  10.0 2.2 copy.30.wk
  12.2 2.2 copy.31.wv
  14.4 0.0 copy-done.5
  14.4 0.0 copy-done.6
  14.4 1.3 copy_bitcast_fusion
  15.7 0.0 copy-done.7
  15.7 0.0 copy-done.8
  15.7 3.1 fusion.2
  18.8 65.6 %attend_forward.1 = (bf16[2,4,128,1536]{3,2,1,0:T(8,128)(2,1)}, bf16[2,4,128,1536]{3,2,1,0:T(8,128)(2,1)}, bf16[2,2,1024,128]{3,2,1,0:T(8,128)(2,1)}, bf16[2,4,5...) custom-call(bf16[2,128,1536]{2,1,0:T(8,128)(2,1)} %get-tuple-element, ...), custom_call_target="tpu_custom_call" | custom-call | tf_op jit(solution)/shard_map/attend_forward/pallas_call | solution.py:341
  84.4 64.9 %feed_forward.1 = (bf16[2,4,128,1536]{3,2,1,0:T(8,128)(2,1)}, bf16[2,1536,1024]{2,1,0:T(8,128)(2,1)}, bf16[1536,1024]{1,0:T(8,128)(2,1)}, bf16[4,2,128,1536]{3,2...) custom-call(bf16[2,128,1536]{2,1,0:T(8,128)(2,1)} %get-tuple-element.33.n2, ...), custom_call_target="tpu_custom_call" | custom-call | tf_op jit(solution)/shard_map/feed_forward/pallas_call | solution.py:499
  149.3 0.0 copy-start.4
  149.3 0.0 reduce-scatter.2.cloned.1.call-update
  149.4 1.7 copy-done.4
  151.1 2.7 copy.32
  153.8 337.2 %attend_backward.1 = (f32[2,128,1536]{2,1,0:T(8,128)}, f32[8,1536]{1,0:T(8,128)}, bf16[2,2,768,1024]{3,2,1,0:T(8,128)(2,1)}, bf16[2,768,1024]{2,1,0:T(8,128)(2,1)}, bf16[2,2,384,1152]{3,2,1,0:T(8,128)(2,1)}) custom-call(bf16[2,4,128,1536]{3,2,1,0:T(8,128)(2,1)} %get-tuple-element.36.db_in, bf16[2,2,1024,128]{3,2,1,0:T(8,128)(2,1)} %get-tuple-element.37.q_in, ...), custom_call_target="tpu_custom_call" | custom-call | tf_op jit(solution)/shard_map/attend_backward/pallas_call | solution.py:981
  491.0 0.0 copy-start.3
  491.1 3.9 copy.38
  495.0 0.0 copy-done.3
  495.0 3.7 bitcast_convert_fusion.1
  498.6 0.0 copy-start.2
  498.6 6.7 %copy.36 = f32[1536,1024]{0,1:T(8,128)} copy(f32[1536,1024]{1,0:T(8,128)} %bitcast_convert_fusion.1) | data formatting | bytes 12582912 | tf_op jit(solution)/shard_map/transpose | solution.py:1032
  505.3 0.0 copy-done.2
  505.3 0.7 bitcast_convert_fusion
  506.1 0.0 copy-start
  506.1 1.9 fusion.15
  508.0 1.6 copy-done
  509.6 1.9 copy.41
  511.6 2.4 fusion.16
  514.0 1.5 copy.40
  515.4 1.5 copy.39
  516.9 1.5 slice_reduce_fusion
  518.4 0.0 copy-start.1
  518.4 9.3 %fusion.17 = (f32[1,2,768,1024]{3,2,1,0:T(8,128)}, f32[1,2,768,1024]{3,2,1,0:T(8,128)}) fusion(bf16[2,2,768,1024]{3,2,1,0:T(8,128)(2,1)} %get-tuple-element.51), kind=kLoop, calls=%fused_computation.30 | loop fusion | bytes 25165824 | tf_op jit(solution)/shard_map/slice | solution.py:1031
  527.7 0.0 reduce-scatter.2.cloned.1.call-done
  527.7 0.0 copy-done.1
  527.7 1.3 fusion.1
  529.0 1.7 copy.37
  (1 shorter events, 0.0 us)
Async XLA Ops:
  7.2 8.5 %copy-start.7 = (f32[2,128]{1,0:T(2,128)S(1)}, f32[2,128]{1,0:T(2,128)}, u32[]{:S(2)}) copy-start(f32[2,128]{1,0:T(2,128)} %constant.71) | copy-start | bytes 3076
  7.2 8.5 %copy-start.8 = (f32[2,128]{1,0:T(2,128)S(1)}, f32[2,128]{1,0:T(2,128)}, u32[]{:S(2)}) copy-start(f32[2,128]{1,0:T(2,128)} %constant.70) | copy-start | bytes 3076
  7.2 7.2 %copy-start.5 = (bf16[128,2,1536]{2,1,0:T(2,128)(2,1)S(1)}, bf16[128,2,1536]{2,1,0:T(2,128)(2,1)}, u32[]{:S(2)}) copy-start(bf16[128,2,1536]{2,1,0:T(2,128)(2,1)} %param.27) | copy-start | bytes 2359300
  7.2 7.2 %copy-start.6 = (bf16[128,2,1536]{2,1,0:T(2,128)(2,1)S(1)}, bf16[128,2,1536]{2,1,0:T(2,128)(2,1)}, u32[]{:S(2)}) copy-start(bf16[128,2,1536]{2,1,0:T(2,128)(2,1)} %param.17) | copy-start | bytes 2359300
  7.2 520.5 %reduce-scatter.2.cloned.1.call-start = ((), (), s32[]{:S(2)}) async-start(), calls=%async_computation.1 | async-start | bytes 3932160 | tf_op jit(solution)/shard_map/reduce_scatter | solution.py:1009
  149.3 1.8 copy-start.4
  491.0 3.9 copy-start.3
  498.6 6.7 %copy-start.2 = (bf16[2,2,384,1152]{3,2,1,0:T(8,128)(2,1)S(1)}, bf16[2,2,384,1152]{3,2,1,0:T(8,128)(2,1)}, u32[]{:S(2)}) copy-start(bf16[2,2,384,1152]{3,2,1,0:T(8,128)(2,1)} %get-tuple-element.50) | copy-start | bytes 10616836
  506.1 3.5 copy-start
  518.4 9.3 %copy-start.1 = (f32[2,128,1536]{2,1,0:T(8,128)S(1)}, f32[2,128,1536]{2,1,0:T(8,128)}, u32[]{:S(2)}) copy-start(f32[2,128,1536]{2,1,0:T(8,128)} %get-tuple-element.32.mid) | copy-start | bytes 4718596
Sparse Core Ops, SparseCore 0:
  149.5 54.6 reduce-scatter.1

commit v2 on v1

--- a/solution.py
+++ b/solution.py
@@ -23,19 +23,19 @@
 
 
 def pick_tables():
-    q = np.zeros((384, 512), np.float32)
+    q = np.zeros((512, 384), np.float32)
     kv = np.zeros((384, 384), np.float32)
-    o = np.zeros((512, 384), np.float32)
+    o = np.zeros((384, 512), np.float32)
     for h in range(4):
         for d in range(96):
-            q[h * 96 + d, h * 128 + K_LANES[h // 2][d]] = 1
+            q[h * 128 + K_LANES[h // 2][d], h * 96 + d] = 1
             lane = F_LANES[h // 2][d] if d < 32 else V_LANES[h // 2][d - 32]
-            o[h * 128 + lane, h * 96 + d] = 1
+            o[h * 96 + d, h * 128 + lane] = 1
     for g in range(2):
         for d in range(96):
-            kv[g * 96 + d, g * 128 + K_LANES[g][d]] = 1
+            kv[g * 128 + K_LANES[g][d], g * 96 + d] = 1
             lane = g * 128 + F_LANES[g][d] if d < 32 else 256 + V_LANES[g][d - 32]
-            kv[192 + g * 96 + d, lane] = 1
+            kv[lane, 192 + g * 96 + d] = 1
     return q, kv, o
 
 
@@ -135,7 +135,7 @@
     SPAN = 4 * RP
     TQ = 256
     NT = 2 * SPAN // TQ
-    g1 = gain1[...].astype(f32)
+    g1 = gain1[...].astype(f32).reshape(1, D)
     for s in range(S):
         xn[s] = rms(tok[s].astype(f32), g1).astype(bf16)
     entry([{"tensor": sib}, {"tensor": ynb}], True)
@@ -150,8 +150,8 @@
     for s in range(S):
         gb(0, s).start()
         ga(0, s).start()
-    wqkv[:, 0:512] = nn(wq[...], pq[...]).astype(bf16)
-    wqkv[:, 512:896] = (nn(wk[...], pkv[0:192, :]) + nn(wv[...], pkv[192:384, :])).astype(bf16)
+    wqkv[0:512, :] = nt(pq[...], wq[...]).astype(bf16)
+    wqkv[512:896, :] = (nn(pkv[:, 0:192], wk[...]) + nn(pkv[:, 192:384], wv[...])).astype(bf16)
     for s in range(S):
         X[s, 0] = xn[s]
 
@@ -172,7 +172,7 @@
                 kvc(s, j, hb).start()
 
     def project(s, hb):
-        r = nn(X[s, 2 * hb:2 * hb + 2].reshape(2 * RP, D), wqkv[...])
+        r = nt(X[s, 2 * hb:2 * hb + 2].reshape(2 * RP, D), wqkv[...])
         base = hb * 2 * RP
         for slot in range(6):
             g = slot // 2 if slot < 4 else slot - 4
@@ -245,14 +245,14 @@
         rs_b(s).wait_recv()
         mid = tok[s].astype(f32) + part[s, 0, 0].astype(f32) + rs1[s, 0].astype(f32) + rs2[s].astype(f32)
         mid_out[s] = mid
-        n2_out[s] = rms(mid, gain2[...].astype(f32)).astype(bf16)
+        n2_out[s] = rms(mid, gain2[...].astype(f32).reshape(1, D)).astype(bf16)
 
     ga(0, 0).wait_recv()
     project(0, 0)
     send_own(0, 0)
     ga(0, 1).wait_recv()
     project(1, 0)
-    wo[...] = nn(po[...], w_out[...]).astype(bf16)
+    wo[...] = tn(po[...], w_out[...]).astype(bf16)
     gb(0, 0).wait_recv()
     gc(0, 0).start()
     arrive(0, 0, 0)
@@ -342,12 +342,12 @@
         functools.partial(forward_kernel, nz),
         out_shape=[sd((S, 4, RP, D), bf16), sd((S, 4, RP, D), bf16), sd((S, 2, 2 * SPAN, 128), bf16),
                    sd((S, nz, SPAN, 384), bf16), sd((S, 2, 2 * SPAN, 128), bf16), sd((S, 2, 1, 2 * SPAN), f32),
-                   sd((D, 896), bf16), sd((512, D), bf16), sd((S, RP, D), f32), sd((S, RP, D), bf16)],
+                   sd((896, D), bf16), sd((512, D), bf16), sd((S, RP, D), f32), sd((S, RP, D), bf16)],
         in_specs=[V] * 13,
         out_specs=[A] * 8 + [V] * 2,
         scratch_shapes=[vm((S, RP, D), bf16), vm((S, 4, RP, D), bf16), vm((S, 4, RP, D), bf16),
                         vm((S, nz, SPAN, 384), bf16), vm((S, 2, 2 * SPAN, 128), bf16),
-                        vm((S, 2, 2 * SPAN, 128), bf16), vm((S, 2, 1, 2 * SPAN), f32), vm((D, 896), bf16), vm((512, D), bf16),
+                        vm((S, 2, 2 * SPAN, 128), bf16), vm((S, 2, 1, 2 * SPAN), f32), vm((896, D), bf16), vm((512, D), bf16),
                         vm((S, 2, 1, 2 * SPAN), f32), vm((S, 2, 1, 2 * SPAN), f32), vm((S, 2, 256, 2 * SPAN), f32),
                         vm((S, 2, 2, RP, D), bf16), vm((S, 2, RP, D), bf16), vm((S, RP, D), bf16), vm((S, RP, D), bf16)]
         + [dma((2, S))] * 6 + [dma((S, nz, 2))] * 2 + [dma((S,))] * 4 + [dma((8,))],
@@ -357,7 +357,7 @@
 
 def feed_kernel(n2, mid, c_in, wg_in, wu_in, wd_in, gain2,
                 db_out, ga_out, gb_out, down_out, dmid_out, gpart_out,
-                X, C, DB, dn, wg, wu, wd, dh, F, G, part, rs1, ysend, rs2, pd,
+                X, C, DB, dn, wg, wu, wd, dh, F, G, GD, part, rs1, ysend, rs2, pd,
                 sA, rA, sB, rB, sC, rC, sR1, rR1, sR2, rR2, isem, osem):
     t = lax.axis_index("tensor")
     sib, ynb = t ^ 1, t ^ 2
@@ -413,7 +413,7 @@
         ra(s, 1).wait_recv()
         ysend[s] = (part[s, 0, 1].astype(f32) + rs1[s, 1].astype(f32)).astype(bf16)
         rb(s).start()
-    gain = gain2[...].astype(f32)
+    gain = gain2[...].astype(f32).reshape(1, D)
     def rs_end(s):
         ra(s, 0).wait_recv()
         rb(s).wait_recv()
@@ -435,6 +435,12 @@
         at = pl.ds(pl.multiple_of(c * CH, CH), CH)
         left = src[:, :, :, at].reshape(S * 4 * RP, CH).T
         G[a, at, :] = nn(left, F[f].reshape(S * 4 * RP, FL)).astype(bf16)
+    half = FL // 2
+    def dgrad(h):
+        left = F[2, :, :, pl.ds(pl.multiple_of(h * half, half), half)].reshape(S * 4 * RP, half).T
+        for c in range(D // CH):
+            at = pl.ds(c * CH, CH)
+            GD[h, :, at] = nn(left, C[:, :, :, at].reshape(S * 4 * RP, CH)).astype(bf16)
     def down(s):
         r = nn(F[2, s], wd[...]).astype(bf16)
         for p in range(4):
@@ -455,8 +461,8 @@
     mlp(1, 1)
     rs_end(0)
     rs_mid(1)
-    lax.fori_loop(0, D // CH, lambda c, x: (wgrad(2, C, 2, c), x)[1], 0)
-    o_down = pltpu.make_async_copy(G.at[2], gb_out, osem.at[0])
+    lax.fori_loop(0, 2, lambda h, x: (dgrad(h), x)[1], 0)
+    o_down = pltpu.make_async_copy(GD, gb_out, osem.at[0])
     o_down.start()
     down(0)
     down(1)
@@ -467,7 +473,7 @@
     rs_end(1)
     lax.fori_loop(0, D // CH, lambda c, x: (wgrad(0, X, 0, c), x)[1], 0)
     lax.fori_loop(0, D // CH, lambda c, x: (wgrad(1, X, 1, c), x)[1], 0)
-    o_up = pltpu.make_async_copy(G.at[pl.ds(0, 2)], ga_out, osem.at[2])
+    o_up = pltpu.make_async_copy(G, ga_out, osem.at[2])
     o_up.start()
     gb(1, 1).wait_recv()
     gc(1, 1).start()
@@ -498,13 +504,13 @@
     vm = pltpu.VMEM
     return pl.pallas_call(
         feed_kernel,
-        out_shape=[sd((S, 4, RP, D), bf16), sd((2, D, FL), bf16), sd((D, FL), bf16), sd((4, S, RP, D), bf16),
+        out_shape=[sd((S, 4, RP, D), bf16), sd((2, D, FL), bf16), sd((2, FL // 2, D), bf16), sd((4, S, RP, D), bf16),
                    sd((S, RP, D), f32), sd((1, D), f32)],
         in_specs=[V, V, A, A, A, A, V],
         out_specs=[A, A, A, A, V, V],
         scratch_shapes=[vm((S, 4, RP, D), bf16), vm((S, 4, RP, D), bf16), vm((S, 4, RP, D), bf16), vm((S, RP, D), bf16),
                         vm((D, FL), bf16), vm((D, FL), bf16), vm((FL, D), bf16), vm((S, 4 * RP, FL), f32),
-                        vm((3, S, 4 * RP, FL), bf16), vm((3, D, FL), bf16), vm((S, 2, 2, RP, D), bf16), vm((S, 2, RP, D), bf16),
+                        vm((3, S, 4 * RP, FL), bf16), vm((2, D, FL), bf16), vm((2, FL // 2, D), bf16), vm((S, 2, 2, RP, D), bf16), vm((S, 2, RP, D), bf16),
                         vm((S, RP, D), bf16), vm((S, RP, D), bf16), vm((4, S, RP, D), bf16)]
         + [dma((2, S))] * 6 + [dma((S, 2))] * 2 + [dma((S,))] * 2 + [dma((4,)), dma((4,))],
         compiler_params=pltpu.CompilerParams(collective_id=1, has_side_effects=True, vmem_limit_bytes=VMEM_BYTES),
@@ -579,9 +585,10 @@
         Q = n * p
         return [vm((2, Q, C), bf16), vm((2, Q, C), bf16), vm((Q, C), bf16),
                 dma((n,)), dma((n,)), dma((2, n)), dma((2, n)), dma((n,)), dma((2, 2, n)), dma((2, n)), dma((2, 2, n))]
-    def __init__(self, src, own, out, bufs, osem, n, p, lag):
+    def __init__(self, src, own, out, bufs, osem, n, p, lag, ahead=False):
         self.setup(n, p, lag)
         self.src, self.own, self.out, self.osem = src, own, out, osem
+        self.ahead = ahead
         self.RX, self.RZ, self.R2, self.x1s, self.x1r, self.rs, self.rr, self.r2, self.bs, self.br, self.x2 = bufs
         self.ticks = n + lag * (2 * self.far + 2)
     def tick(self, k):
@@ -594,9 +601,12 @@
             return rc(self.src.at[ox, :, self.at(i)], RX.at[:, self.at(i)], self.x1s.at[i], self.x1r.at[i], {"dp": ox})
         def x2(u, i):
             return rc(RX.at[u, self.at(i)], self.out.at[xi, u, self.at(i)], self.x2.at[0, u, i], self.x2.at[1, u, i], {"dp": ox})
-        @pl.when(self.valid(k))
-        def _():
-            x1(k).start()
+        @pl.when(k == 0 if self.ahead else self.valid(k))
+        def _():
+            if self.ahead:
+                lax.fori_loop(0, self.n, lambda i, c: (x1(i).start(), c)[1], 0)
+            else:
+                x1(k).start()
         i1 = k - lag
         @pl.when(self.valid(i1))
         def _():
@@ -645,18 +655,18 @@
 
 
 class LineFirst(Flow):
-    count = 11
+    count = 10
     @staticmethod
     def scratch(n, p, C):
         vm = pltpu.VMEM
         dma = pltpu.SemaphoreType.DMA
         Q = n * p
-        return [vm((2, Q, C), bf16), vm((2, Q, C), bf16), vm((Q, C), bf16), vm((Q, C), bf16),
+        return [vm((2, Q, C), bf16), vm((Q, C), bf16), vm((Q, C), bf16),
                 dma((2, n)), dma((2, n)), dma((n,)), dma((2, 2, n)), dma((2, n)), dma((n,)), dma((n,))]
-    def __init__(self, out, bufs, osem, n, p, lag):
+    def __init__(self, W, out, bufs, osem, n, p, lag):
         self.setup(n, p, lag)
-        self.out, self.osem = out, osem
-        self.W, self.Z, self.XB, self.R2, self.rs, self.rr, self.r2, self.bs, self.br, self.xs, self.xr = bufs
+        self.W, self.out, self.osem = W, out, osem
+        self.Z, self.XB, self.R2, self.rs, self.rr, self.r2, self.bs, self.br, self.xs, self.xr = bufs
         self.ticks = n + lag * (2 * self.far + 2)
     def tick(self, k):
         lag, far, W, Z = self.lag, self.far, self.W, self.Z
@@ -707,8 +717,13 @@
         pltpu.make_async_copy(self.Z, self.out, self.osem).wait()
 
 
-def backward_kernel(summed, n1, n2, lag, db_in, q_in, kv_in, att_in, lse, wo_in, wt_in, x1_in, pq, pkv, po, cos, sin, tok, dmid_in, gain1, gp2,
-                    ga_in, gb_in, ig_out, gains_out, oa, ob, oc, *scr):
+NO = 192
+CROWS = 6 * NO
+HOP = 2
+
+
+def backward_kernel(summed, plan, db_in, q_in, kv_in, att_in, lse, wo_in, wt_in, x1_in, pq, pkv, po, cos, sin, tok, dmid_in, gain1, gp2,
+                    g_in, gd_in, ig_out, gains_out, o_gate, o_up, o_down, o_rest, *scr):
     t = lax.axis_index("tensor")
     zi = lax.axis_index("seq")
     nz = lax.axis_size("seq")
@@ -718,25 +733,42 @@
     TQ = 512
     NT = 2 * SPAN // TQ
     HC = D // 4
+    QC = CROWS // 4
     scr = list(scr)
-    (DB, q, KV, att, wbuf, da, delta, dqT, acc, PB, RB, dqkv, rs1, rs2, W3, GS, GL,
-     sKV, rKV, sR1, rR1, sR2, rR2, sG, rG, isem, sems_out) = scr[:27]
-    scr = scr[27:]
+    (DB, q, KV, att, wbuf, da, delta, dqT, acc, PB, RB, dqkv, rs1, rs2, W3, heads, GS, GL,
+     sKV, rKV, sR1, rR1, sR2, rR2, sG, rG, isem, sems_out) = scr[:28]
+    scr = scr[28:]
     xi = lax.axis_index("dp")
     rings = []
     loads = [pltpu.make_async_copy(a, b, isem.at[i]) for i, (a, b) in enumerate(
         ((db_in, DB), (wo_in, wbuf.at[pl.ds(0, 512)]), (att_in, att), (q_in, q), (kv_in, KV), (dmid_in, ig_out)))]
     first = []
     if summed:
-        own = scr.pop(0)
-        Q1 = own.shape[1]
-        b1, scr = scr[:HalfFirst.count], scr[HalfFirst.count:]
-        b2, scr = scr[:LineFirst.count], scr[LineFirst.count:]
-        b3, scr = scr[:HalfFirst.count], scr[HalfFirst.count:]
-        ring_a = HalfFirst(ga_in, lambda u: own.at[u], oa, b1, sems_out.at[0], n1, Q1 // n1, lag)
-        ring_b = LineFirst(ob, b2, sems_out.at[1], n1, gb_in.shape[1] // n1, lag)
-        ring_c = HalfFirst(W3, lambda u: W3.at[xi, u], oc, b3, sems_out.at[2], n2, HC // n2, lag)
-        first = [pltpu.make_async_copy(ga_in.at[xi], own, isem.at[6]), pltpu.make_async_copy(gb_in, ring_b.W, isem.at[7])]
+        def take(cls):
+            got = scr[:cls.count]
+            del scr[:cls.count]
+            return got
+        own_g, own_d, WU = scr.pop(0), scr.pop(0), scr.pop(0)
+        def make(name, cls, *a):
+            n, lag, off, pace, *ahead = plan[name]
+            return cls(*a[:-1], take(cls), sems_out.at[len(rings)], n, a[-1] // n, lag, *ahead), off, pace
+        rings.append(make("gate", HalfFirst, g_in.at[0], lambda u: own_g.at[u], o_gate, own_g.shape[1]))
+        rings.append(make("down", HalfFirst, gd_in, lambda u: own_d.at[u], o_down, own_d.shape[1]))
+        rings.append(make("up", LineFirst, WU, o_up, WU.shape[1]))
+        rings.append(make("rest", HalfFirst, W3, lambda u: W3.at[xi, u], o_rest, QC))
+        first = [pltpu.make_async_copy(g_in.at[0, xi], own_g, isem.at[6]), pltpu.make_async_copy(gd_in.at[xi], own_d, isem.at[7])]
+        QG = own_g.shape[1]
+        for u in range(2):
+            for h in range(2):
+                first.append(pltpu.make_async_copy(g_in.at[1, u, h], WU.at[u, pl.ds(h * QG, QG)], isem.at[13 + 2 * u + h]))
+    def tick(g):
+        for ring, off, pace in rings[:3]:
+            if pace == 1:
+                ring.tick(g - off)
+            else:
+                @pl.when((g - off) % pace == 0)
+                def _():
+                    ring.tick((g - off) // pace)
     wt_load = pltpu.make_async_copy(wt_in, wbuf, isem.at[8])
     x1_loads = [pltpu.make_async_copy(x1_in.at[:, :, pl.ds(c * HC, HC)], PB.at[pl.ds(S * c, S)], isem.at[9 + c]) for c in range(4)]
     for c in loads[:2] + first + loads[2:]:
@@ -749,10 +781,6 @@
             devs.append({"seq": zi ^ b})
             b *= 2
     entry(devs, True)
-    def tick(k):
-        if summed:
-            ring_a.tick(k)
-            ring_b.tick(k)
     loads[0].wait()
     loads[1].wait()
 
@@ -842,21 +870,30 @@
         @pl.when(j == zi)
         def _():
             unit(s, j, True)
-        event(m - 1 - (nz - 1 - zi))
+        event(m - 1 - HOP * (nz - 1 - zi))
         tick(k + m)
         return c
-    steps = nz * S + nz
+    steps = nz * S + 1 + HOP * (nz - 1)
     lax.fori_loop(0, steps, step, 0)
     k = k + steps
     for c in x1_loads:
         c.start()
 
+    def put(row, at, value):
+        lo = 0
+        while lo < value.shape[0]:
+            blk, r = (row + lo) // QC, (row + lo) % QC
+            cnt = min(value.shape[0] - lo, QC - r)
+            W3[blk // 2, blk % 2, r:r + cnt, at] = value[lo:lo + cnt, :]
+            lo += cnt
+    for s in range(S):
+        for r in range(4):
+            heads[s * SPAN:(s + 1) * SPAN, r * 128:(r + 1) * 128] = att[s, r // 2, (r % 2) * SPAN:(r % 2 + 1) * SPAN, :]
     def out_grad(c, x):
-        left = DB[:, :, :, pl.ds(pl.multiple_of(c * HC, HC), HC)].reshape(S * SPAN, HC).T
-        heads = jnp.concatenate([jnp.concatenate([att[s, g, hh * SPAN:(hh + 1) * SPAN, :] for g in range(2) for hh in range(2)], axis=1)
-                                 for s in range(S)], axis=0)
-        g0 = nn(left, heads).astype(bf16)
-        W3[c // 2, c % 2, :, 0:384] = nn(g0, po[...]).astype(bf16)
+        at = pl.ds(pl.multiple_of(c * HC, HC), HC)
+        g0 = nn(heads[...].T, DB[:, :, :, at].reshape(S * SPAN, HC)).astype(bf16)
+        g0 = nn(po[...], g0).astype(bf16)
+        put(4 * NO, at, g0)
         s = c // 2
         for g in range(2):
             @pl.when(c % 2 == g)
@@ -893,29 +930,37 @@
     for c in x1_loads:
         c.wait()
     def in_grad(c, x):
-        left = PB[pl.ds(S * c, S)].reshape(S * SPAN, HC).T
-        g0 = nn(left, dqkv[...].reshape(S * SPAN, 896)).astype(bf16)
-        W3[c // 2, c % 2, :, 384:768] = nt(g0[:, 0:512], pq[...]).astype(bf16)
-        W3[c // 2, c % 2, :, 768:1152] = nt(g0[:, 512:896], pkv[...]).astype(bf16)
+        at = pl.ds(pl.multiple_of(c * HC, HC), HC)
+        g0 = nn(dqkv[...].reshape(S * SPAN, 896).T, PB[pl.ds(S * c, S)].reshape(S * SPAN, HC)).astype(bf16)
+        gq = tn(pq[...], g0[0:512]).astype(bf16)
+        gkv = tn(pkv[...], g0[512:896]).astype(bf16)
+        put(0, at, gq)
+        put(2 * NO, at, gkv)
         tick(k + c)
         return x
     lax.fori_loop(0, 4, in_grad, 0)
     k = k + 4
     if summed:
-        k_c = k
-        def joint(m):
-            tick(m)
-            ring_c.tick(m - k_c)
+        start_rest = k
+        def joint(g):
+            for i, (ring, off, pace) in enumerate(rings):
+                kk = g - (start_rest if i == 3 else off)
+                if pace == 1:
+                    ring.tick(kk)
+                else:
+                    @pl.when(kk % pace == 0)
+                    def _():
+                        ring.tick(kk // pace)
     else:
-        o3 = pltpu.make_async_copy(W3, oc, sems_out.at[2])
+        o3 = pltpu.make_async_copy(W3, o_rest, sems_out.at[3])
         o3.start()
-        def joint(m):
+        def joint(g):
             pass
     joint(k)
     joint(k + 1)
     k = k + 2
     loads[5].wait()
-    gain = gain1[...].astype(f32)
+    gain = gain1[...].astype(f32).reshape(1, D)
     gp1 = None
     for s in range(S):
         ra(s, 0).wait_recv()
@@ -939,7 +984,7 @@
             k = k + 1
             c.wait()
             gains_out[...] += GL[m]
-        last = max(ring_a.ticks, ring_b.ticks, k_c + ring_c.ticks)
+        last = max((start_rest if i == 3 else off) + (ring.ticks - 1) * pace + 1 for i, (ring, off, pace) in enumerate(rings))
         lax.fori_loop(k, last, lambda m, c: (joint(m), c)[1], 0)
     for s in range(S):
         ra(s, 0).wait_send()
@@ -950,21 +995,21 @@
             def _():
                 chain(s, j).wait_send()
     if summed:
-        ring_a.drain()
-        ring_b.drain()
-        ring_c.drain()
+        for ring, off, pace in rings:
+            ring.drain()
     else:
         o3.wait()
 
 
-def attend_backward(DB, q, KV, att, lse, wo, wt, X1, pq, pkv, po, cos, sin, tok, dmid, gain1, gp2, ga, gb, summed, n1=24, n2=12, lag=1):
+PLAN = {"gate": (12, 2, 9, 1, True), "down": (8, 1, 0, 2, True), "up": (24, 2, 21, 1), "rest": (18, 2, 0, 1)}
+
+
+def attend_backward(DB, q, KV, att, lse, wo, wt, X1, pq, pkv, po, cos, sin, tok, dmid, gain1, gp2, g, gd, summed, plan=PLAN):
     nz = lax.axis_size("seq")
     S, RP, D = tok.shape
     SPAN = 4 * RP
-    FL = ga.shape[-1]
-    HC = D // 4
-    Q1 = ga.shape[0] * ga.shape[1] // 4
-    Q2 = gb.shape[0] // 2
+    FL = g.shape[-1]
+    QG, QD, QU, QC = D // 4, FL // 4, D // 2, CROWS // 4
     V = pl.BlockSpec(memory_space=pltpu.VMEM)
     A = pl.BlockSpec(memory_space=pl.ANY)
     sd = jax.ShapeDtypeStruct
@@ -973,20 +1018,24 @@
     scratch = [vm(DB.shape, bf16), vm(q.shape, bf16), vm(KV.shape, bf16), vm(att.shape, bf16), vm((896, D), bf16),
                vm(q.shape, bf16), vm((S, 2, 1, 2 * SPAN), f32), vm((S, 2, 128, 2 * SPAN), f32), vm((SPAN, 384), f32),
                vm((nz * S, SPAN, 384), bf16), vm((nz - 1, S, SPAN, 384), bf16), vm((S, SPAN, 896), bf16),
-               vm((S, 2, RP, D), bf16), vm((S, RP, D), bf16), vm((2, 2, HC, 1152), bf16), vm((6, 8, D), f32), vm((6, 8, D), f32),
-               dma((nz, S)), dma((nz, S)), dma((S, 2)), dma((S, 2)), dma((S,)), dma((S,)), dma((6,)), dma((6,)), dma((13,)), dma((3,))]
+               vm((S, 2, RP, D), bf16), vm((S, RP, D), bf16), vm((2, 2, QC, D), bf16), vm((S * SPAN, 512), bf16),
+               vm((6, 8, D), f32), vm((6, 8, D), f32),
+               dma((nz, S)), dma((nz, S)), dma((S, 2)), dma((S, 2)), dma((S,)), dma((S,)), dma((6,)), dma((6,)), dma((17,)), dma((4,))]
     if summed:
-        scratch += [vm((2, Q1, FL), bf16)] + HalfFirst.scratch(n1, Q1 // n1, FL) + LineFirst.scratch(n1, Q2 // n1, FL)
-        scratch += HalfFirst.scratch(n2, HC // n2, 1152)
+        scratch += [vm((2, QG, FL), bf16), vm((2, QD, D), bf16), vm((2, QU, FL), bf16)]
+        for name, cls, Q, C in (("gate", HalfFirst, QG, FL), ("down", HalfFirst, QD, D), ("up", LineFirst, QU, FL), ("rest", HalfFirst, QC, D)):
+            n = plan[name][0]
+            scratch += cls.scratch(n, Q // n, C)
     return pl.pallas_call(
-        functools.partial(backward_kernel, summed, n1, n2, lag),
-        out_shape=[sd((S, RP, D), f32), sd((8, D), f32), sd((2, 2, Q1, FL), bf16), sd((2, Q2, FL), bf16), sd((2, 2, HC, 1152), bf16)],
+        functools.partial(backward_kernel, summed, plan),
+        out_shape=[sd((S, RP, D), f32), sd((8, D), f32), sd((2, 2, QG, FL), bf16), sd((2, QU, FL), bf16), sd((2, 2, QD, D), bf16),
+                   sd((2, 2, QC, D), bf16)],
         in_specs=[A, A, A, A, V, A, A, A, V, V, V, V, V, V, A, V, V, A, A],
-        out_specs=[V, V, A, A, A],
+        out_specs=[V, V, A, A, A, A],
         scratch_shapes=scratch,
         compiler_params=pltpu.CompilerParams(collective_id=2, has_side_effects=True, vmem_limit_bytes=VMEM_BYTES),
         name="attend_backward")(DB, q, KV, att, lse, wo, wt, X1.reshape(S, SPAN, D), pq, pkv, po, cos, sin, tok, dmid, gain1, gp2,
-                                ga.reshape(2, 2, Q1, FL), gb.reshape(2, Q2, FL))
+                                g.reshape(2, 2, 2, QG, FL), gd.reshape(2, 2, QD, D))
 
 
 def local(
@@ -994,42 +1043,37 @@
 ):
     t = lax.axis_index("tensor")
     zi = lax.axis_index("seq")
-    kept = w_query.shape[1]
-    kv = w_key.shape[1]
     pq, pkv, po = (jnp.asarray(v, bf16) for v in pick_tables())
     tok = jnp.swapaxes(tokens, 0, 1)
     cot = jnp.swapaxes(cotangent, 0, 1)
     S, RP, D = tok.shape
     cos, sin = rope_tables(zi * 4 * RP, 4 * RP, t)
-    gain1 = attn_gain.reshape(1, -1)
-    gain2 = ffn_gain.reshape(1, -1)
     X1, C, q, KV, att, lse, wqkv, wo, mid, n2 = attend_forward(
-        tok, cot, w_query, w_key, w_value, w_output, pq, pkv, po, cos, sin, gain1, gain2)
-    DB, ga, gb, down, dmid, gp2 = feed_forward(n2, mid, C, w_gate, w_up, w_down, gain2)
+        tok, cot, w_query, w_key.T, w_value.T, w_output, pq, pkv, po, cos, sin, attn_gain, ffn_gain)
+    summed = lax.axis_size("dp") == 2
+    DB, g, gd, down, dmid, gp2 = feed_forward(n2, mid, C, w_gate, w_up, w_down, ffn_gain)
     down_local = lax.psum_scatter(down, "tensor", scatter_dimension=0, tiled=True)[0]
-    summed = lax.axis_size("dp") == 2
-    ig, gains, oa, ob, oc = attend_backward(
-        DB, q, KV, att, lse, wo, wqkv.T, X1, pq, pkv, po, cos, sin, tok, dmid, gain1, gp2, ga, gb, summed)
-    FL = w_gate.shape[1]
-    if summed:
-        gate_up, down_t = oa.reshape(2, D, FL).astype(f32), ob.reshape(D, FL).astype(f32)
-        rest = oc.reshape(D, -1).astype(f32)
-    else:
-        gate_up, down_t, rest = lax.psum((ga.astype(f32), gb.astype(f32), oc.reshape(D, -1).astype(f32)), ("dp", "seq"))
+    ig, gains, gate, up, wd, rest = attend_backward(
+        DB, q, KV, att, lse, wo, wqkv, X1, pq, pkv, po, cos, sin, tok, dmid, attn_gain, gp2, g, gd, summed)
+    if not summed:
+        g, wd, rest = lax.psum((g.astype(f32), gd.astype(f32), rest.astype(f32)), ("dp", "seq"))
+        gate, up = g[0], g[1]
         gains = lax.psum(gains, ("dp", "seq", "tensor"))
+    rest = rest.reshape(-1, D).astype(f32)
+    nq, nk = w_query.shape[1], w_key.shape[1]
     activation = (mid + down_local.astype(f32)).astype(bf16)
     return (
         jnp.swapaxes(activation, 0, 1),
         jnp.swapaxes(ig, 0, 1),
         gains[0],
-        rest[:, kept:2 * kept],
-        rest[:, 2 * kept:2 * kept + kv],
-        rest[:, 2 * kept + kv:],
-        rest[:, :kept].T,
+        rest[:nq].T,
+        rest[nq:nq + nk].T,
+        rest[nq + nk:nq + 2 * nk].T,
+        rest[nq + 2 * nk:],
         gains[1],
-        gate_up[0],
-        gate_up[1],
-        down_t.T,
+        gate.reshape(D, -1).astype(f32),
+        up.reshape(D, -1).astype(f32),
+        wd.reshape(-1, D).astype(f32),
     )
 
 

time: 546 us -> 486 us (0.89)
  Pallas kernels: 468 us -> 427 us
  local copies, waits for them, and re-layouts: 46.8 us -> 18.5 us
  other arithmetic: 8.76 us -> 18.5 us
    pallas_call x1, Pallas kernels: 337 us -> 296 us  [attend_backward(): pl.pallas_call(functools.partial(backward_kernel, summed, plan), out_shap...]
    convert_element_type x1 -> x4, other arithmetic: 0.73 us -> 14.1 us  [the longest x1 3.78 us: local(): wd.reshape(-1, D).astype(f32)]
    slice x3 -> x1, local copies, waits for them, and re-layouts: 13.6 us -> 1.98 us  [local(): rest[nq + 2 * nk:]]
    unnamed x25 -> x17, local copies, waits for them, and re-layouts: 18.3 us -> 9.07 us
  transfers between devices with their start and end apart: 1 -> 1, of which waited for: 0 -> 0; matrix products, arithmetic and copies ran while one was open for 7% -> 6% of each run, Pallas kernels for 63% -> 62%
where the time goes in v2:
time: 486 us; the launch traced here: 479 us
  Pallas kernels  427 us (88%)
  local copies, waits for them, and re-layouts  18.5 us (4%)
  other arithmetic  18.5 us (4%)
  between operations  14.6 us (3%)
    pallas_call x1, Pallas kernels, attend_backward(): pl.pallas_call(functools.partial(backward_kernel, summed, plan), out_shap...  296 us
    pallas_call x1, Pallas kernels, attend_forward(): pl.pallas_call(functools.partial(forward_kernel, nz), out_shape=[sd((S, 4...  65.4 us
    pallas_call x1, Pallas kernels, feed_forward(): pl.pallas_call(feed_kernel, out_shape=[sd((S, 4, RP, D), bf16), sd((2, D,...  65.2 us
  transfers between devices with their start and end apart: 1, of which 0 were waited for; matrix products, arithmetic and copies ran while one was open for 6% of the time, Pallas kernels for 62%

profile of v2, /device:TPU:0, one launch (start us, length us, event | category | flops | bytes accessed | tf_op | source)
XLA Modules:
  0.0 478.5 jit_solution(15395451256416914340)
XLA Ops:
  7.2 0.0 copy-start.5
  7.2 0.0 copy-start.6
  7.2 0.0 reduce-scatter.2.cloned.1.call-start
  7.3 2.7 copy_bitcast_fusion
  10.0 0.0 copy-done.5
  10.0 0.0 copy-done.6
  10.0 3.1 fusion.2
  13.0 65.4 %attend_forward.1 = (bf16[2,4,128,1536]{3,2,1,0:T(8,128)(2,1)}, bf16[2,4,128,1536]{3,2,1,0:T(8,128)(2,1)}, bf16[2,2,1024,128]{3,2,1,0:T(8,128)(2,1)}, bf16[2,4,5...) custom-call(bf16[2,128,1536]{2,1,0:T(8,128)(2,1)} %get-tuple-element, ...), custom_call_target="tpu_custom_call" | custom-call | tf_op jit(solution)/shard_map/attend_forward/pallas_call | solution.py:341
  78.4 65.2 %feed_forward.1 = (bf16[2,4,128,1536]{3,2,1,0:T(8,128)(2,1)}, bf16[2,1536,1024]{2,1,0:T(8,128)(2,1)}, bf16[2,512,1536]{2,1,0:T(8,128)(2,1)}, bf16[4,2,128,1536]{...) custom-call(bf16[2,128,1536]{2,1,0:T(8,128)(2,1)} %get-tuple-element.34.n2, ...), custom_call_target="tpu_custom_call" | custom-call | tf_op jit(solution)/shard_map/feed_forward/pallas_call | solution.py:505
  143.6 0.0 reduce-scatter.2.cloned.1.call-update
  143.7 296.3 %attend_backward.1 = (f32[2,128,1536]{2,1,0:T(8,128)}, f32[8,1536]{1,0:T(8,128)}, bf16[2,2,384,1024]{3,2,1,0:T(8,128)(2,1)}, bf16[2,768,1024]{2,1,0:T(8,128)(2,1...) custom-call(bf16[2,4,128,1536]{3,2,1,0:T(8,128)(2,1)} %get-tuple-element.37.db_in, ...), custom_call_target="tpu_custom_call" | custom-call | tf_op jit(solution)/shard_map/attend_backward/pallas_call | solution.py:1029
  440.0 3.8 copy.31
  443.8 3.0 bitcast_convert_fusion
  446.7 0.0 copy-start
  446.7 2.0 fusion.15
  448.7 1.6 copy-done
  450.4 1.9 copy.32
  452.3 0.0 copy-start.4
  452.3 1.6 slice_reduce_fusion
  453.9 3.2 slice_bitcast_fusion.1
  457.1 0.0 copy-done.4
  457.1 0.0 copy-start.3
  457.1 3.7 bitcast_convert_fusion.3
  460.8 0.0 copy-done.3
  460.8 0.0 copy-start.2
  460.8 3.7 bitcast_convert_fusion.2
  464.4 0.0 copy-done.2
  464.4 0.0 copy-start.1
  464.4 3.8 bitcast_convert_fusion.1
  468.2 0.0 reduce-scatter.2.cloned.1.call-done
  468.2 0.0 copy-done.1
  468.2 1.3 fusion.1
  469.5 1.7 copy.30
  (1 shorter events, 0.0 us)
Async XLA Ops:
  7.2 2.8 copy-start.5
  7.2 2.8 copy-start.6
  7.2 461.0 %reduce-scatter.2.cloned.1.call-start = ((), (), s32[]{:S(2)}) async-start(), calls=%async_computation.1 | async-start | bytes 3932160 | tf_op jit(solution)/shard_map/reduce_scatter | solution.py:1055
  446.7 3.6 copy-start
  452.3 4.8 %copy-start.4 = (bf16[2,2,384,1024]{3,2,1,0:T(8,128)(2,1)S(1)}, bf16[2,2,384,1024]{3,2,1,0:T(8,128)(2,1)}, u32[]{:S(2)}) copy-start(bf16[2,2,384,1024]{3,2,1,0:T(8,128)(2,1)} %get-tuple-element.52) | copy-start | bytes 9437188
  457.1 3.7 copy-start.3
  460.8 3.7 copy-start.2
  464.4 3.8 copy-start.1
Sparse Core Ops, SparseCore 0:
  143.8 54.4 reduce-scatter.1

commit v3 on v2

--- a/solution.py
+++ b/solution.py
@@ -356,8 +356,8 @@
 
 
 def feed_kernel(n2, mid, c_in, wg_in, wu_in, wd_in, gain2,
-                db_out, ga_out, gb_out, down_out, dmid_out, gpart_out,
-                X, C, DB, dn, wg, wu, wd, dh, F, G, GD, part, rs1, ysend, rs2, pd,
+                dn_out, ga_out, gb_out, down_out, dmid_out, gpart_out,
+                X, C, wg, wu, wd, dh, F, G, GD, part, rs1, ysend, rs2, pd,
                 sA, rA, sB, rB, sC, rC, sR1, rR1, sR2, rR2, isem, osem):
     t = lax.axis_index("tensor")
     sib, ynb = t ^ 1, t ^ 2
@@ -369,20 +369,19 @@
         c.start()
     entry([{"tensor": sib}, {"tensor": ynb}], False)
 
-    def ga(w, s):
-        return rc((n2, dn)[w].at[s], (X, DB)[w].at[s, 1], sA.at[w, s], rA.at[w, s], {"tensor": sib})
-    def gb(w, s):
-        return rc((n2, dn)[w].at[s], (X, DB)[w].at[s, 2], sB.at[w, s], rB.at[w, s], {"tensor": ynb})
-    def gc(w, s):
-        buf = (X, DB)[w]
-        return rc(buf.at[s, 2], buf.at[s, 3], sC.at[w, s], rC.at[w, s], {"tensor": sib})
+    def ga(s):
+        return rc(n2.at[s], X.at[s, 1], sA.at[s], rA.at[s], {"tensor": sib})
+    def gb(s):
+        return rc(n2.at[s], X.at[s, 2], sB.at[s], rB.at[s], {"tensor": ynb})
+    def gc(s):
+        return rc(X.at[s, 2], X.at[s, 3], sC.at[s], rC.at[s], {"tensor": sib})
     def ra(s, hb):
         return rc(part.at[s, 1, hb], rs1.at[s, hb], sR1.at[s, hb], rR1.at[s, hb], {"tensor": sib})
     def rb(s):
         return rc(ysend.at[s], rs2.at[s], sR2.at[s], rR2.at[s], {"tensor": ynb})
     for s in range(S):
-        gb(0, s).start()
-        ga(0, s).start()
+        gb(s).start()
+        ga(s).start()
     for s in range(S):
         X[s, 0] = n2[s]
     loads[0].wait()
@@ -425,10 +424,7 @@
             gpart_out[...] += gp
         dm = C[s, 0].astype(f32) + dv
         dmid_out[s] = dm
-        dn[s] = dm.astype(bf16)
-        gb(1, s).start()
-        ga(1, s).start()
-        DB[s, 0] = dn[s]
+        dn_out[s] = dm.astype(bf16)
 
     CH = 512
     def wgrad(a, src, f, c):
@@ -446,18 +442,18 @@
         for p in range(4):
             pd[t ^ p, s] = r[p * RP:(p + 1) * RP]
 
-    ga(0, 0).wait_recv()
+    ga(0).wait_recv()
     mlp(0, 0)
-    gb(0, 0).wait_recv()
-    gc(0, 0).start()
-    gc(0, 0).wait_recv()
+    gb(0).wait_recv()
+    gc(0).start()
+    gc(0).wait_recv()
     mlp(0, 1)
-    ga(0, 1).wait_recv()
-    gb(0, 1).wait_recv()
-    gc(0, 1).start()
+    ga(1).wait_recv()
+    gb(1).wait_recv()
+    gc(1).start()
     rs_mid(0)
     mlp(1, 0)
-    gc(0, 1).wait_recv()
+    gc(1).wait_recv()
     mlp(1, 1)
     rs_end(0)
     rs_mid(1)
@@ -468,29 +464,19 @@
     down(1)
     o_pd = pltpu.make_async_copy(pd, down_out, osem.at[1])
     o_pd.start()
-    gb(1, 0).wait_recv()
-    gc(1, 0).start()
     rs_end(1)
     lax.fori_loop(0, D // CH, lambda c, x: (wgrad(0, X, 0, c), x)[1], 0)
     lax.fori_loop(0, D // CH, lambda c, x: (wgrad(1, X, 1, c), x)[1], 0)
     o_up = pltpu.make_async_copy(G, ga_out, osem.at[2])
     o_up.start()
-    gb(1, 1).wait_recv()
-    gc(1, 1).start()
-    for s in range(S):
-        ga(1, s).wait_recv()
-        gc(1, s).wait_recv()
-    o_db = pltpu.make_async_copy(DB, db_out, osem.at[3])
-    o_db.start()
-    for s in range(S):
-        for w in range(2):
-            ga(w, s).wait_send()
-            gb(w, s).wait_send()
-            gc(w, s).wait_send()
+    for s in range(S):
+        ga(s).wait_send()
+        gb(s).wait_send()
+        gc(s).wait_send()
         ra(s, 0).wait_send()
         ra(s, 1).wait_send()
         rb(s).wait_send()
-    for o in (o_down, o_pd, o_up, o_db):
+    for o in (o_down, o_pd, o_up):
         o.wait()
 
 
@@ -504,22 +490,22 @@
     vm = pltpu.VMEM
     return pl.pallas_call(
         feed_kernel,
-        out_shape=[sd((S, 4, RP, D), bf16), sd((2, D, FL), bf16), sd((2, FL // 2, D), bf16), sd((4, S, RP, D), bf16),
+        out_shape=[sd((S, RP, D), bf16), sd((2, D, FL), bf16), sd((2, FL // 2, D), bf16), sd((4, S, RP, D), bf16),
                    sd((S, RP, D), f32), sd((1, D), f32)],
         in_specs=[V, V, A, A, A, A, V],
-        out_specs=[A, A, A, A, V, V],
-        scratch_shapes=[vm((S, 4, RP, D), bf16), vm((S, 4, RP, D), bf16), vm((S, 4, RP, D), bf16), vm((S, RP, D), bf16),
+        out_specs=[V, A, A, A, V, V],
+        scratch_shapes=[vm((S, 4, RP, D), bf16), vm((S, 4, RP, D), bf16),
                         vm((D, FL), bf16), vm((D, FL), bf16), vm((FL, D), bf16), vm((S, 4 * RP, FL), f32),
                         vm((3, S, 4 * RP, FL), bf16), vm((2, D, FL), bf16), vm((2, FL // 2, D), bf16), vm((S, 2, 2, RP, D), bf16), vm((S, 2, RP, D), bf16),
                         vm((S, RP, D), bf16), vm((S, RP, D), bf16), vm((4, S, RP, D), bf16)]
-        + [dma((2, S))] * 6 + [dma((S, 2))] * 2 + [dma((S,))] * 2 + [dma((4,)), dma((4,))],
+        + [dma((S,))] * 6 + [dma((S, 2))] * 2 + [dma((S,))] * 2 + [dma((4,)), dma((3,))],
         compiler_params=pltpu.CompilerParams(collective_id=1, has_side_effects=True, vmem_limit_bytes=VMEM_BYTES),
         name="feed_forward")(n2, mid, C, wg, wu, wd, gain2)
 
 
-def line(u, nz):
+def line(u, nz, edge=False):
     zi = lax.axis_index("seq")
-    root = nz // 2 - 1 + u
+    root = (nz - 1) * u if edge else nz // 2 - 1 + u
     below, above = zi < root, zi > root
     dist = jnp.where(below, root - zi, zi - root)
     return dist, below, above, zi == root, jnp.where(below, zi + 1, zi - 1)
@@ -537,17 +523,22 @@
 
 
 class Flow:
-    def setup(self, n, p, lag):
-        self.n, self.p, self.lag = n, p, lag
+    def setup(self, n, p, lag, edge=False):
+        self.n, self.p, self.lag, self.edge = n, p, lag, edge
         self.nz = lax.axis_size("seq")
-        self.far = self.nz // 2
+        self.far = self.nz - 1 if edge else self.nz // 2
+    def line(self, u):
+        return line(u, self.nz, self.edge)
     def at(self, i):
         return pl.ds(pl.multiple_of(i * self.p, self.p), self.p)
     def valid(self, i):
         return both(i >= 0, i < self.n)
     def send_in(self, u, i, own, main, short, sems, act):
-        dist, below, above, root, inward = line(u, self.nz)
+        dist, below, above, root, inward = self.line(u)
         ss, rr, r2 = sems
+        if self.edge:
+            act(rc(own, main.at[u, self.at(i)], ss.at[u, i], rr.at[u, i], {"seq": inward}))
+            return
         to_short = both(dist == 1, below if u == 0 else above)
         @pl.when(to_short)
         def _():
@@ -557,13 +548,13 @@
             act(rc(own, main.at[u, self.at(i)], ss.at[u, i], rr.at[u, i], {"seq": inward}))
     def from_main(self, u, i, own, main, sems):
         ss, rr, r2 = sems
-        rc(own, main.at[u, self.at(i)], ss.at[u, i], rr.at[u, i], {"seq": line(u, self.nz)[4]}).wait_recv()
+        rc(own, main.at[u, self.at(i)], ss.at[u, i], rr.at[u, i], {"seq": self.line(u)[4]}).wait_recv()
     def from_short(self, u, i, own, short, sems):
         ss, rr, r2 = sems
-        rc(own, short.at[self.at(i)], ss.at[u, i], r2.at[i], {"seq": line(u, self.nz)[4]}).wait_recv()
+        rc(own, short.at[self.at(i)], ss.at[u, i], r2.at[i], {"seq": self.line(u)[4]}).wait_recv()
     def outward(self, u, i, buf, bs, br, act):
         zi = lax.axis_index("seq")
-        dist, below, above, root, inward = line(u, self.nz)
+        dist, below, above, root, inward = self.line(u)
         @pl.when(both(jnp.logical_not(above), zi > 0))
         def _():
             act(rc(buf.at[u, self.at(i)], buf.at[u, self.at(i)], bs.at[0, u, i], br.at[u, i], {"seq": zi - 1}))
@@ -572,7 +563,7 @@
             act(rc(buf.at[u, self.at(i)], buf.at[u, self.at(i)], bs.at[1, u, i], br.at[u, i], {"seq": zi + 1}))
     def has_farther(self, u):
         zi = lax.axis_index("seq")
-        dist, below, above, root, inward = line(u, self.nz)
+        dist, below, above, root, inward = self.line(u)
         return jnp.logical_or(both(below, zi > 0), both(above, zi < self.nz - 1))
 
 
@@ -615,7 +606,7 @@
                 own = self.own(u).at[self.at(i1)]
                 own[...] = add(own, RX.at[u, self.at(i1)])
         for u in range(2):
-            dist, below, above, root, inward = line(u, self.nz)
+            dist, below, above, root, inward = self.line(u)
             i = k - lag * (1 + far - dist)
             @pl.when(self.valid(i))
             def _():
@@ -663,8 +654,8 @@
         Q = n * p
         return [vm((2, Q, C), bf16), vm((Q, C), bf16), vm((Q, C), bf16),
                 dma((2, n)), dma((2, n)), dma((n,)), dma((2, 2, n)), dma((2, n)), dma((n,)), dma((n,))]
-    def __init__(self, W, out, bufs, osem, n, p, lag):
-        self.setup(n, p, lag)
+    def __init__(self, W, out, bufs, osem, n, p, lag, edge=False):
+        self.setup(n, p, lag, edge)
         self.W, self.out, self.osem = W, out, osem
         self.Z, self.XB, self.R2, self.rs, self.rr, self.r2, self.bs, self.br, self.xs, self.xr = bufs
         self.ticks = n + lag * (2 * self.far + 2)
@@ -676,7 +667,7 @@
         def xb(u, i):
             return rc(W.at[u, self.at(i)], self.XB.at[self.at(i)], self.xs.at[i], self.xr.at[i], {"dp": ox})
         for u in range(2):
-            dist, below, above, root, inward = line(u, self.nz)
+            dist, below, above, root, inward = self.line(u)
             i = k - lag * (far - dist)
             @pl.when(self.valid(i))
             def _():
@@ -691,8 +682,11 @@
                 @pl.when(root)
                 def _():
                     self.from_main(u, i, own, Z, sems)
-                    self.from_short(u, i, own, self.R2, sems)
-                    own[...] = add(own, Z.at[u, self.at(i)], self.R2.at[self.at(i)])
+                    if self.edge:
+                        own[...] = add(own, Z.at[u, self.at(i)])
+                    else:
+                        self.from_short(u, i, own, self.R2, sems)
+                        own[...] = add(own, Z.at[u, self.at(i)], self.R2.at[self.at(i)])
                     xb(u, i).start()
             i = k - lag * (far + 1)
             @pl.when(both(self.valid(i), root))
@@ -719,10 +713,13 @@
 
 NO = 192
 CROWS = 6 * NO
-HOP = 2
-
-
-def backward_kernel(summed, plan, db_in, q_in, kv_in, att_in, lse, wo_in, wt_in, x1_in, pq, pkv, po, cos, sin, tok, dmid_in, gain1, gp2,
+PHASES = {"dast": 1, "steps": 1, "out": 1, "done": 1, "in": 1}
+EARLY = False
+PRE = 3
+HOP = 1
+
+
+def backward_kernel(summed, plan, dn_in, q_in, kv_in, att_in, lse, wo_in, wt_in, x1_in, pq, pkv, po, cos, sin, tok, dmid_in, gain1, gp2,
                     g_in, gd_in, ig_out, gains_out, o_gate, o_up, o_down, o_rest, *scr):
     t = lax.axis_index("tensor")
     zi = lax.axis_index("seq")
@@ -736,39 +733,48 @@
     QC = CROWS // 4
     scr = list(scr)
     (DB, q, KV, att, wbuf, da, delta, dqT, acc, PB, RB, dqkv, rs1, rs2, W3, heads, GS, GL,
-     sKV, rKV, sR1, rR1, sR2, rR2, sG, rG, isem, sems_out) = scr[:28]
-    scr = scr[28:]
+     sKV, rKV, sR1, rR1, sR2, rR2, sG, rG, sDB, rDB, isem, sems_out) = scr[:30]
+    scr = scr[30:]
     xi = lax.axis_index("dp")
     rings = []
     loads = [pltpu.make_async_copy(a, b, isem.at[i]) for i, (a, b) in enumerate(
-        ((db_in, DB), (wo_in, wbuf.at[pl.ds(0, 512)]), (att_in, att), (q_in, q), (kv_in, KV), (dmid_in, ig_out)))]
+        ((dn_in, DB.at[:, 0]), (wo_in, wbuf.at[pl.ds(0, 512)]), (att_in, att), (q_in, q), (kv_in, KV), (dmid_in, ig_out)))]
     first = []
     if summed:
         def take(cls):
             got = scr[:cls.count]
             del scr[:cls.count]
             return got
-        own_g, own_d, WU = scr.pop(0), scr.pop(0), scr.pop(0)
+        own_g, own_d, WU, WE = (scr.pop(0) for _ in range(4))
         def make(name, cls, *a):
-            n, lag, off, pace, *ahead = plan[name]
-            return cls(*a[:-1], take(cls), sems_out.at[len(rings)], n, a[-1] // n, lag, *ahead), off, pace
+            n, lag, off, pace, *more = plan[name]
+            return cls(*a[:-1], take(cls), sems_out.at[len(rings)], n, a[-1] // n, lag, *more), off, pace
         rings.append(make("gate", HalfFirst, g_in.at[0], lambda u: own_g.at[u], o_gate, own_g.shape[1]))
         rings.append(make("down", HalfFirst, gd_in, lambda u: own_d.at[u], o_down, own_d.shape[1]))
-        rings.append(make("up", LineFirst, WU, o_up, WU.shape[1]))
+        rings.append(make("up", LineFirst, WU, o_up.at[0], WU.shape[1]))
+        rings.append(make("up_edge", LineFirst, WE, o_up.at[1], WE.shape[1]))
         rings.append(make("rest", HalfFirst, W3, lambda u: W3.at[xi, u], o_rest, QC))
-        first = [pltpu.make_async_copy(g_in.at[0, xi], own_g, isem.at[6]), pltpu.make_async_copy(gd_in.at[xi], own_d, isem.at[7])]
-        QG = own_g.shape[1]
-        for u in range(2):
-            for h in range(2):
-                first.append(pltpu.make_async_copy(g_in.at[1, u, h], WU.at[u, pl.ds(h * QG, QG)], isem.at[13 + 2 * u + h]))
+        first = [pltpu.make_async_copy(a, b, isem.at[13 + i]) for i, (a, b) in enumerate(
+            ((gd_in.at[xi], own_d), (g_in.at[0, xi], own_g), (g_in.at[1, 0], WU), (g_in.at[1, 1], WE)))]
     def tick(g):
-        for ring, off, pace in rings[:3]:
+        for ring, off, pace in rings[:-1]:
             if pace == 1:
                 ring.tick(g - off)
             else:
                 @pl.when((g - off) % pace == 0)
                 def _():
                     ring.tick((g - off) // pace)
+    def ptick(phase, it, k):
+        mode = PHASES[phase]
+        if mode == 1:
+            tick(k + it)
+        elif mode:
+            @pl.when(it % mode == 0)
+            def _():
+                tick(k + it // mode)
+    def after(phase, count, k):
+        mode = PHASES[phase]
+        return k + (-(-count // mode) if mode else 0)
     wt_load = pltpu.make_async_copy(wt_in, wbuf, isem.at[8])
     x1_loads = [pltpu.make_async_copy(x1_in.at[:, :, pl.ds(c * HC, HC)], PB.at[pl.ds(S * c, S)], isem.at[9 + c]) for c in range(4)]
     for c in loads[:2] + first + loads[2:]:
@@ -781,8 +787,28 @@
             devs.append({"seq": zi ^ b})
             b *= 2
     entry(devs, True)
+    def ga(s):
+        return rc(DB.at[s, 0], DB.at[s, 1], sDB.at[0, s], rDB.at[0, s], {"tensor": sib})
+    def gb(s):
+        return rc(DB.at[s, 0], DB.at[s, 2], sDB.at[1, s], rDB.at[1, s], {"tensor": ynb})
+    def gc(s):
+        return rc(DB.at[s, 2], DB.at[s, 3], sDB.at[2, s], rDB.at[2, s], {"tensor": sib})
     loads[0].wait()
+    for s in range(S):
+        gb(s).start()
+        ga(s).start()
+    for c in first:
+        c.wait()
+    lax.fori_loop(0, PRE, lambda k, c: (tick(k), c)[1], 0)
+    gb(0).wait_recv()
+    gc(0).start()
+    lax.fori_loop(PRE, 2 * PRE, lambda k, c: (tick(k), c)[1], 0)
+    gb(1).wait_recv()
+    gc(1).start()
     loads[1].wait()
+    for s in range(S):
+        ga(s).wait_recv()
+        gc(s).wait_recv()
 
     def dast(it, c):
         s = it // 2
@@ -791,15 +817,11 @@
         for h in range(4):
             rows = pl.ds(pl.multiple_of((h % 2) * SPAN + hb * 2 * RP, 2 * RP), 2 * RP)
             da[s, h // 2, rows, :] = r[:, h * 128:(h + 1) * 128].astype(bf16)
-        @pl.when(it == 0)
-        def _():
-            for c2 in first:
-                c2.wait()
-        tick(it)
+        ptick("dast", it, 2 * PRE)
         return c
     lax.fori_loop(0, 2 * S, dast, 0)
     wt_load.start()
-    k = 2 * S
+    k = after("dast", 2 * S, 2 * PRE)
     loads[2].wait()
     def dlt(it, c):
         s = it // 2
@@ -811,6 +833,26 @@
     lax.fori_loop(0, 2 * S, dlt, 0)
     for c in loads[3:5]:
         c.wait()
+
+    def put(row, at, value):
+        lo = 0
+        while lo < value.shape[0]:
+            blk, r = (row + lo) // QC, (row + lo) % QC
+            cnt = min(value.shape[0] - lo, QC - r)
+            W3[blk // 2, blk % 2, r:r + cnt, at] = value[lo:lo + cnt, :]
+            lo += cnt
+    for s in range(S):
+        for r in range(4):
+            heads[s * SPAN:(s + 1) * SPAN, r * 128:(r + 1) * 128] = att[s, r // 2, (r % 2) * SPAN:(r % 2 + 1) * SPAN, :]
+    def out_grad(k, c, x):
+        at = pl.ds(pl.multiple_of(c * HC, HC), HC)
+        g0 = nn(heads[...].T, DB[:, :, :, at].reshape(S * SPAN, HC)).astype(bf16)
+        put(4 * NO, at, nn(po[...], g0).astype(bf16))
+        ptick("out", c, k)
+        return x
+    if EARLY:
+        lax.fori_loop(0, 4, functools.partial(out_grad, k), 0)
+        k = after("out", 4, k)
 
     def unit(s, j, diag):
         lane = lax.broadcasted_iota(jnp.int32, (1, 128), 1)
@@ -871,29 +913,18 @@
         def _():
             unit(s, j, True)
         event(m - 1 - HOP * (nz - 1 - zi))
-        tick(k + m)
+        ptick("steps", m, k)
         return c
     steps = nz * S + 1 + HOP * (nz - 1)
     lax.fori_loop(0, steps, step, 0)
-    k = k + steps
+    k = after("steps", steps, k)
     for c in x1_loads:
         c.start()
 
-    def put(row, at, value):
-        lo = 0
-        while lo < value.shape[0]:
-            blk, r = (row + lo) // QC, (row + lo) % QC
-            cnt = min(value.shape[0] - lo, QC - r)
-            W3[blk // 2, blk % 2, r:r + cnt, at] = value[lo:lo + cnt, :]
-            lo += cnt
-    for s in range(S):
-        for r in range(4):
-            heads[s * SPAN:(s + 1) * SPAN, r * 128:(r + 1) * 128] = att[s, r // 2, (r % 2) * SPAN:(r % 2 + 1) * SPAN, :]
-    def out_grad(c, x):
-        at = pl.ds(pl.multiple_of(c * HC, HC), HC)
-        g0 = nn(heads[...].T, DB[:, :, :, at].reshape(S * SPAN, HC)).astype(bf16)
-        g0 = nn(po[...], g0).astype(bf16)
-        put(4 * NO, at, g0)
+    if not EARLY:
+        lax.fori_loop(0, 4, functools.partial(out_grad, k), 0)
+        k = after("out", 4, k)
+    def rotate(c, x):
         s = c // 2
         for g in range(2):
             @pl.when(c % 2 == g)
@@ -901,11 +932,13 @@
                 for hh in range(2):
                     u = dqT[s, g, :, hh * SPAN:(hh + 1) * SPAN].T * SCALE
                     dqkv[s, :, (2 * g + hh) * 128:(2 * g + hh + 1) * 128] = (u * cos[g] - pltpu.roll(u, 64, 1) * sin[g]).astype(bf16)
-        tick(k + c)
         return x
-    lax.fori_loop(0, 4, out_grad, 0)
-    k = k + 4
+    lax.fori_loop(0, 2 * S, rotate, 0)
     wt_load.wait()
+    for s in range(S):
+        ga(s).wait_send()
+        gb(s).wait_send()
+        gc(s).wait_send()
 
     def ra(s, hb):
         return rc(DB.at[s, 2 + hb], rs1.at[s, hb], sR1.at[s, hb], rR1.at[s, hb], {"tensor": sib})
@@ -919,10 +952,10 @@
         DB[s, hb] = r[:RP].astype(bf16)
         DB[s, 2 + hb] = r[RP:].astype(bf16)
         ra(s, hb).start()
-        tick(k + it)
+        ptick("done", it, k)
         return c
     lax.fori_loop(0, 2 * S, d_one, 0)
-    k = k + 2 * S
+    k = after("done", 2 * S, k)
     for s in range(S):
         ra(s, 1).wait_recv()
         DB[s, 1] = add(DB.at[s, 1], rs1.at[s, 1])
@@ -936,15 +969,15 @@
         gkv = tn(pkv[...], g0[512:896]).astype(bf16)
         put(0, at, gq)
         put(2 * NO, at, gkv)
-        tick(k + c)
+        ptick("in", c, k)
         return x
     lax.fori_loop(0, 4, in_grad, 0)
-    k = k + 4
+    k = after("in", 4, k)
     if summed:
         start_rest = k
         def joint(g):
             for i, (ring, off, pace) in enumerate(rings):
-                kk = g - (start_rest if i == 3 else off)
+                kk = g - (start_rest if i == len(rings) - 1 else off)
                 if pace == 1:
                     ring.tick(kk)
                 else:
@@ -952,7 +985,7 @@
                     def _():
                         ring.tick(kk // pace)
     else:
-        o3 = pltpu.make_async_copy(W3, o_rest, sems_out.at[3])
+        o3 = pltpu.make_async_copy(W3, o_rest, sems_out.at[4])
         o3.start()
         def joint(g):
             pass
@@ -984,7 +1017,7 @@
             k = k + 1
             c.wait()
             gains_out[...] += GL[m]
-        last = max((start_rest if i == 3 else off) + (ring.ticks - 1) * pace + 1 for i, (ring, off, pace) in enumerate(rings))
+        last = max((start_rest if i == len(rings) - 1 else off) + (ring.ticks - 1) * pace + 1 for i, (ring, off, pace) in enumerate(rings))
         lax.fori_loop(k, last, lambda m, c: (joint(m), c)[1], 0)
     for s in range(S):
         ra(s, 0).wait_send()
@@ -1001,40 +1034,40 @@
         o3.wait()
 
 
-PLAN = {"gate": (12, 2, 9, 1, True), "down": (8, 1, 0, 2, True), "up": (24, 2, 21, 1), "rest": (18, 2, 0, 1)}
-
-
-def attend_backward(DB, q, KV, att, lse, wo, wt, X1, pq, pkv, po, cos, sin, tok, dmid, gain1, gp2, g, gd, summed, plan=PLAN):
+PLAN = {"gate": (6, 1, 0, 2), "down": (16, 2, 12, 1, True), "up": (12, 1, 25, 3), "up_edge": (8, 1, 17, 3, True), "rest": (18, 3, 0, 1)}
+
+
+def attend_backward(dn, q, KV, att, lse, wo, wt, X1, pq, pkv, po, cos, sin, tok, dmid, gain1, gp2, g, gd, summed, plan=PLAN):
     nz = lax.axis_size("seq")
     S, RP, D = tok.shape
     SPAN = 4 * RP
     FL = g.shape[-1]
-    QG, QD, QU, QC = D // 4, FL // 4, D // 2, CROWS // 4
+    QG, QD, QC = D // 4, FL // 4, CROWS // 4
     V = pl.BlockSpec(memory_space=pltpu.VMEM)
     A = pl.BlockSpec(memory_space=pl.ANY)
     sd = jax.ShapeDtypeStruct
     dma = pltpu.SemaphoreType.DMA
     vm = pltpu.VMEM
-    scratch = [vm(DB.shape, bf16), vm(q.shape, bf16), vm(KV.shape, bf16), vm(att.shape, bf16), vm((896, D), bf16),
+    scratch = [vm((S, 4, RP, D), bf16), vm(q.shape, bf16), vm(KV.shape, bf16), vm(att.shape, bf16), vm((896, D), bf16),
                vm(q.shape, bf16), vm((S, 2, 1, 2 * SPAN), f32), vm((S, 2, 128, 2 * SPAN), f32), vm((SPAN, 384), f32),
                vm((nz * S, SPAN, 384), bf16), vm((nz - 1, S, SPAN, 384), bf16), vm((S, SPAN, 896), bf16),
                vm((S, 2, RP, D), bf16), vm((S, RP, D), bf16), vm((2, 2, QC, D), bf16), vm((S * SPAN, 512), bf16),
                vm((6, 8, D), f32), vm((6, 8, D), f32),
-               dma((nz, S)), dma((nz, S)), dma((S, 2)), dma((S, 2)), dma((S,)), dma((S,)), dma((6,)), dma((6,)), dma((17,)), dma((4,))]
+               dma((nz, S)), dma((nz, S)), dma((S, 2)), dma((S, 2)), dma((S,)), dma((S,)), dma((6,)), dma((6,)), dma((3, S)), dma((3, S)), dma((17,)), dma((5,))]
     if summed:
-        scratch += [vm((2, QG, FL), bf16), vm((2, QD, D), bf16), vm((2, QU, FL), bf16)]
-        for name, cls, Q, C in (("gate", HalfFirst, QG, FL), ("down", HalfFirst, QD, D), ("up", LineFirst, QU, FL), ("rest", HalfFirst, QC, D)):
+        scratch += [vm((2, QG, FL), bf16), vm((2, QD, D), bf16), vm((2, QG, FL), bf16), vm((2, QG, FL), bf16)]
+        for name, cls, Q, C in (("gate", HalfFirst, QG, FL), ("down", HalfFirst, QD, D), ("up", LineFirst, QG, FL), ("up_edge", LineFirst, QG, FL), ("rest", HalfFirst, QC, D)):
             n = plan[name][0]
             scratch += cls.scratch(n, Q // n, C)
     return pl.pallas_call(
         functools.partial(backward_kernel, summed, plan),
-        out_shape=[sd((S, RP, D), f32), sd((8, D), f32), sd((2, 2, QG, FL), bf16), sd((2, QU, FL), bf16), sd((2, 2, QD, D), bf16),
+        out_shape=[sd((S, RP, D), f32), sd((8, D), f32), sd((2, 2, QG, FL), bf16), sd((2, 2, QG, FL), bf16), sd((2, 2, QD, D), bf16),
                    sd((2, 2, QC, D), bf16)],
         in_specs=[A, A, A, A, V, A, A, A, V, V, V, V, V, V, A, V, V, A, A],
         out_specs=[V, V, A, A, A, A],
         scratch_shapes=scratch,
         compiler_params=pltpu.CompilerParams(collective_id=2, has_side_effects=True, vmem_limit_bytes=VMEM_BYTES),
-        name="attend_backward")(DB, q, KV, att, lse, wo, wt, X1.reshape(S, SPAN, D), pq, pkv, po, cos, sin, tok, dmid, gain1, gp2,
+        name="attend_backward")(dn, q, KV, att, lse, wo, wt, X1.reshape(S, SPAN, D), pq, pkv, po, cos, sin, tok, dmid, gain1, gp2,
                                 g.reshape(2, 2, 2, QG, FL), gd.reshape(2, 2, QD, D))
 
 
@@ -1051,25 +1084,25 @@
     X1, C, q, KV, att, lse, wqkv, wo, mid, n2 = attend_forward(
         tok, cot, w_query, w_key.T, w_value.T, w_output, pq, pkv, po, cos, sin, attn_gain, ffn_gain)
     summed = lax.axis_size("dp") == 2
-    DB, g, gd, down, dmid, gp2 = feed_forward(n2, mid, C, w_gate, w_up, w_down, ffn_gain)
+    dn, g, gd, down, dmid, gp2 = feed_forward(n2, mid, C, w_gate, w_up, w_down, ffn_gain)
     down_local = lax.psum_scatter(down, "tensor", scatter_dimension=0, tiled=True)[0]
     ig, gains, gate, up, wd, rest = attend_backward(
-        DB, q, KV, att, lse, wo, wqkv, X1, pq, pkv, po, cos, sin, tok, dmid, attn_gain, gp2, g, gd, summed)
+        dn, q, KV, att, lse, wo, wqkv, X1, pq, pkv, po, cos, sin, tok, dmid, attn_gain, gp2, g, gd, summed)
     if not summed:
         g, wd, rest = lax.psum((g.astype(f32), gd.astype(f32), rest.astype(f32)), ("dp", "seq"))
         gate, up = g[0], g[1]
         gains = lax.psum(gains, ("dp", "seq", "tensor"))
-    rest = rest.reshape(-1, D).astype(f32)
+    rest = rest.reshape(-1, D)
     nq, nk = w_query.shape[1], w_key.shape[1]
     activation = (mid + down_local.astype(f32)).astype(bf16)
     return (
         jnp.swapaxes(activation, 0, 1),
         jnp.swapaxes(ig, 0, 1),
         gains[0],
-        rest[:nq].T,
-        rest[nq:nq + nk].T,
-        rest[nq + nk:nq + 2 * nk].T,
-        rest[nq + 2 * nk:],
+        rest[:nq].astype(f32).T,
+        rest[nq:nq + nk].astype(f32).T,
+        rest[nq + nk:nq + 2 * nk].astype(f32).T,
+        rest[nq + 2 * nk:].astype(f32),
         gains[1],
         gate.reshape(D, -1).astype(f32),
         up.reshape(D, -1).astype(f32),

time: 486 us -> 470 us (0.967)
  Pallas kernels: 427 us -> 414 us
  local copies, waits for them, and re-layouts: 18.5 us -> 11.7 us
    pallas_call x1, Pallas kernels: 65.2 us -> 55.8 us  [feed_forward(): pl.pallas_call(feed_kernel, out_shape=[sd((S, RP, D), bf16), sd((2, D, FL...]
  transfers between devices with their start and end apart: 1 -> 1, of which waited for: 0 -> 0; matrix products, arithmetic and copies ran while one was open for 6% -> 5% of each run, Pallas kernels for 62% -> 63%
where the time goes in v3:
time: 470 us; the launch traced here: 462 us
  Pallas kernels  414 us (88%)
  other arithmetic  22.1 us (5%)
  between operations  14.2 us (3%)
  local copies, waits for them, and re-layouts  11.7 us (2%)
    pallas_call x1, Pallas kernels, attend_backward(): pl.pallas_call(functools.partial(backward_kernel, summed, plan), out_shap...  293 us
    pallas_call x1, Pallas kernels, attend_forward(): pl.pallas_call(functools.partial(forward_kernel, nz), out_shape=[sd((S, 4...  65.4 us
    pallas_call x1, Pallas kernels, feed_forward(): pl.pallas_call(feed_kernel, out_shape=[sd((S, RP, D), bf16), sd((2, D, FL...  55.8 us
  transfers between devices with their start and end apart: 1, of which 0 were waited for; matrix products, arithmetic and copies ran while one was open for 5% of the time, Pallas kernels for 63%

profile of v3, /device:TPU:0, one launch (start us, length us, event | category | flops | bytes accessed | tf_op | source)
XLA Modules:
  0.0 462.0 jit_solution(5062092633419453585)
XLA Ops:
  7.2 0.0 copy-start.4
  7.2 0.0 copy-start.5
  7.2 0.0 reduce-scatter.2.cloned.1.call-start
  7.3 2.7 copy_bitcast_fusion
  10.0 0.0 copy-done.4
  10.0 0.0 copy-done.5
  10.0 3.1 fusion.2
  13.0 65.4 %attend_forward.1 = (bf16[2,4,128,1536]{3,2,1,0:T(8,128)(2,1)}, bf16[2,4,128,1536]{3,2,1,0:T(8,128)(2,1)}, bf16[2,2,1024,128]{3,2,1,0:T(8,128)(2,1)}, bf16[2,4,5...) custom-call(bf16[2,128,1536]{2,1,0:T(8,128)(2,1)} %get-tuple-element, ...), custom_call_target="tpu_custom_call" | custom-call | tf_op jit(solution)/shard_map/attend_forward/pallas_call | solution.py:341
  78.4 55.8 %feed_forward.1 = (bf16[2,128,1536]{2,1,0:T(8,128)(2,1)}, bf16[2,1536,1024]{2,1,0:T(8,128)(2,1)}, bf16[2,512,1536]{2,1,0:T(8,128)(2,1)}, bf16[4,2,128,1536]{3,2,...) custom-call(bf16[2,128,1536]{2,1,0:T(8,128)(2,1)} %get-tuple-element.34.n2, ...), custom_call_target="tpu_custom_call" | custom-call | tf_op jit(solution)/shard_map/feed_forward/pallas_call | solution.py:491
  134.3 0.0 reduce-scatter.2.cloned.1.call-update
  134.3 292.6 %attend_backward.1 = (f32[2,128,1536]{2,1,0:T(8,128)}, f32[8,1536]{1,0:T(8,128)}, bf16[2,2,384,1024]{3,2,1,0:T(8,128)(2,1)}, bf16[2,2,384,1024]{3,2,1,0:T(8,128)...) custom-call(bf16[2,128,1536]{2,1,0:T(8,128)(2,1)} %get-tuple-element.37.dn_in, ...), custom_call_target="tpu_custom_call" | custom-call | tf_op jit(solution)/shard_map/attend_backward/pallas_call | solution.py:1062
  426.9 3.8 copy.31
  430.7 3.7 slice_convert_fusion
  434.4 1.9 copy.32
  436.3 0.0 copy-start.3
  436.3 1.6 slice_reduce_fusion
  437.9 2.9 convert_bitcast_fusion.1
  440.9 0.0 copy-done.3
  440.9 0.0 copy-start.2
  440.9 3.7 bitcast_convert_fusion.2
  444.5 0.0 copy-done.2
  444.5 0.0 copy-start.1
  444.5 3.7 bitcast_convert_fusion.1
  448.2 0.0 copy-done.1
  448.2 0.0 copy-start
  448.2 3.8 bitcast_convert_fusion
  452.0 0.0 reduce-scatter.2.cloned.1.call-done
  452.0 0.0 copy-done
  452.0 1.3 fusion.1
  453.3 1.7 copy.30
  (1 shorter events, 0.0 us)
Async XLA Ops:
  7.2 2.8 copy-start.4
  7.2 2.8 copy-start.5
  7.2 444.8 %reduce-scatter.2.cloned.1.call-start = ((), (), s32[]{:S(2)}) async-start(), calls=%async_computation.1 | async-start | bytes 3932160 | tf_op jit(solution)/shard_map/reduce_scatter | solution.py:1088
  436.3 4.5 copy-start.3
  440.9 3.7 copy-start.2
  444.5 3.7 copy-start.1
  448.2 3.8 copy-start
Sparse Core Ops, SparseCore 0:
  134.4 53.3 reduce-scatter.1

commit v4 on v3

--- a/solution.py
+++ b/solution.py
@@ -355,10 +355,10 @@
         name="attend_forward")(tok, cot, wq, wk, wv, w_out, pq, pkv, po, cos, sin, gain1, gain2)
 
 
-def feed_kernel(n2, mid, c_in, wg_in, wu_in, wd_in, gain2,
+def feed_kernel(summed, n2, mid, c_in, wg_in, wu_in, wd_in, gain2,
                 dn_out, ga_out, gb_out, down_out, dmid_out, gpart_out,
-                X, C, wg, wu, wd, dh, F, G, GD, part, rs1, ysend, rs2, pd,
-                sA, rA, sB, rB, sC, rC, sR1, rR1, sR2, rR2, isem, osem):
+                X, C, wg, wu, wd, dh, F, G, GD, XR, part, rs1, ysend, rs2, pd,
+                sA, rA, sB, rB, sC, rC, sR1, rR1, sR2, rR2, sX, rX, isem, osem):
     t = lax.axis_index("tensor")
     sib, ynb = t ^ 1, t ^ 2
     S, RP, D = n2.shape
@@ -367,7 +367,9 @@
         ((wd_in, wd), (c_in, C), (wg_in, wg), (wu_in, wu)))]
     for c in loads:
         c.start()
-    entry([{"tensor": sib}, {"tensor": ynb}], False)
+    xi = lax.axis_index("dp")
+    ox = 1 - xi
+    entry([{"tensor": sib}, {"tensor": ynb}] + ([{"dp": ox}] if summed else []), False)
 
     def ga(s):
         return rc(n2.at[s], X.at[s, 1], sA.at[s], rA.at[s], {"tensor": sib})
@@ -457,18 +459,35 @@
     mlp(1, 1)
     rs_end(0)
     rs_mid(1)
-    lax.fori_loop(0, 2, lambda h, x: (dgrad(h), x)[1], 0)
-    o_down = pltpu.make_async_copy(GD, gb_out, osem.at[0])
-    o_down.start()
+    if summed:
+        low, high = pl.ds(0, half // 2), pl.ds(half // 2, half // 2)
+        xc = rc(GD.at[ox, low], XR, sX, rX, {"dp": ox})
+        def part_of_two(i, x):
+            dgrad(jnp.where(i == 0, ox, xi))
+            @pl.when(i == 0)
+            def _():
+                xc.start()
+            return x
+        lax.fori_loop(0, 2, part_of_two, 0)
+        o_down = [pltpu.make_async_copy(GD.at[h, at], gb_out.at[h, at], osem.at[n]) for n, (h, at) in enumerate(((ox, high), (xi, high), (xi, low)))]
+    else:
+        lax.fori_loop(0, 2, lambda h, x: (dgrad(h), x)[1], 0)
+        o_down = [pltpu.make_async_copy(GD, gb_out, osem.at[0])]
+    for o in o_down[:2]:
+        o.start()
     down(0)
     down(1)
-    o_pd = pltpu.make_async_copy(pd, down_out, osem.at[1])
+    o_pd = pltpu.make_async_copy(pd, down_out, osem.at[3])
     o_pd.start()
     rs_end(1)
     lax.fori_loop(0, D // CH, lambda c, x: (wgrad(0, X, 0, c), x)[1], 0)
     lax.fori_loop(0, D // CH, lambda c, x: (wgrad(1, X, 1, c), x)[1], 0)
-    o_up = pltpu.make_async_copy(G, ga_out, osem.at[2])
+    o_up = pltpu.make_async_copy(G, ga_out, osem.at[4])
     o_up.start()
+    if summed:
+        xc.wait()
+        GD[xi, low] = (GD[xi, low].astype(f32) + XR[...].astype(f32)).astype(bf16)
+        o_down[2].start()
     for s in range(S):
         ga(s).wait_send()
         gb(s).wait_send()
@@ -476,11 +495,11 @@
         ra(s, 0).wait_send()
         ra(s, 1).wait_send()
         rb(s).wait_send()
-    for o in (o_down, o_pd, o_up):
+    for o in o_down + [o_pd, o_up]:
         o.wait()
 
 
-def feed_forward(n2, mid, C, wg, wu, wd, gain2):
+def feed_forward(n2, mid, C, wg, wu, wd, gain2, summed):
     S, RP, D = n2.shape
     FL = wg.shape[1]
     V = pl.BlockSpec(memory_space=pltpu.VMEM)
@@ -489,16 +508,16 @@
     dma = pltpu.SemaphoreType.DMA
     vm = pltpu.VMEM
     return pl.pallas_call(
-        feed_kernel,
+        functools.partial(feed_kernel, summed),
         out_shape=[sd((S, RP, D), bf16), sd((2, D, FL), bf16), sd((2, FL // 2, D), bf16), sd((4, S, RP, D), bf16),
                    sd((S, RP, D), f32), sd((1, D), f32)],
         in_specs=[V, V, A, A, A, A, V],
         out_specs=[V, A, A, A, V, V],
         scratch_shapes=[vm((S, 4, RP, D), bf16), vm((S, 4, RP, D), bf16),
                         vm((D, FL), bf16), vm((D, FL), bf16), vm((FL, D), bf16), vm((S, 4 * RP, FL), f32),
-                        vm((3, S, 4 * RP, FL), bf16), vm((2, D, FL), bf16), vm((2, FL // 2, D), bf16), vm((S, 2, 2, RP, D), bf16), vm((S, 2, RP, D), bf16),
+                        vm((3, S, 4 * RP, FL), bf16), vm((2, D, FL), bf16), vm((2, FL // 2, D), bf16), vm((FL // 4, D), bf16), vm((S, 2, 2, RP, D), bf16), vm((S, 2, RP, D), bf16),
                         vm((S, RP, D), bf16), vm((S, RP, D), bf16), vm((4, S, RP, D), bf16)]
-        + [dma((S,))] * 6 + [dma((S, 2))] * 2 + [dma((S,))] * 2 + [dma((4,)), dma((3,))],
+        + [dma((S,))] * 6 + [dma((S, 2))] * 2 + [dma((S,))] * 2 + [pltpu.SemaphoreType.DMA] * 2 + [dma((4,)), dma((5,))],
         compiler_params=pltpu.CompilerParams(collective_id=1, has_side_effects=True, vmem_limit_bytes=VMEM_BYTES),
         name="feed_forward")(n2, mid, C, wg, wu, wd, gain2)
 
@@ -576,10 +595,11 @@
         Q = n * p
         return [vm((2, Q, C), bf16), vm((2, Q, C), bf16), vm((Q, C), bf16),
                 dma((n,)), dma((n,)), dma((2, n)), dma((2, n)), dma((n,)), dma((2, 2, n)), dma((2, n)), dma((2, 2, n))]
-    def __init__(self, src, own, out, bufs, osem, n, p, lag, ahead=False):
+    def __init__(self, src, own, out, bufs, osem, n, p, lag, ahead=False, halved=(0, 1)):
         self.setup(n, p, lag)
         self.src, self.own, self.out, self.osem = src, own, out, osem
         self.ahead = ahead
+        self.halved = halved
         self.RX, self.RZ, self.R2, self.x1s, self.x1r, self.rs, self.rr, self.r2, self.bs, self.br, self.x2 = bufs
         self.ticks = n + lag * (2 * self.far + 2)
     def tick(self, k):
@@ -589,7 +609,8 @@
         sems = (self.rs, self.rr, self.r2)
         start = lambda c: c.start()
         def x1(i):
-            return rc(self.src.at[ox, :, self.at(i)], RX.at[:, self.at(i)], self.x1s.at[i], self.x1r.at[i], {"dp": ox})
+            cls = pl.ds(self.halved[0], len(self.halved))
+            return rc(self.src.at[ox, cls, self.at(i)], RX.at[cls, self.at(i)], self.x1s.at[i], self.x1r.at[i], {"dp": ox})
         def x2(u, i):
             return rc(RX.at[u, self.at(i)], self.out.at[xi, u, self.at(i)], self.x2.at[0, u, i], self.x2.at[1, u, i], {"dp": ox})
         @pl.when(k == 0 if self.ahead else self.valid(k))
@@ -602,7 +623,7 @@
         @pl.when(self.valid(i1))
         def _():
             x1(i1).wait()
-            for u in range(2):
+            for u in self.halved:
                 own = self.own(u).at[self.at(i1)]
                 own[...] = add(own, RX.at[u, self.at(i1)])
         for u in range(2):
@@ -713,9 +734,9 @@
 
 NO = 192
 CROWS = 6 * NO
-PHASES = {"dast": 1, "steps": 1, "out": 1, "done": 1, "in": 1}
-EARLY = False
-PRE = 3
+PHASES = {"dast": 1, "steps": 2, "out": 2, "done": 1, "in": 1}
+EARLY = True
+PRE = 4
 HOP = 1
 
 
@@ -1034,7 +1055,7 @@
         o3.wait()
 
 
-PLAN = {"gate": (6, 1, 0, 2), "down": (16, 2, 12, 1, True), "up": (12, 1, 25, 3), "up_edge": (8, 1, 17, 3, True), "rest": (18, 3, 0, 1)}
+PLAN = {"gate": (12, 2, 7, 1), "down": (8, 2, 0, 1, False, (1,)), "up": (8, 1, 21, 3), "up_edge": (24, 3, 2, 1, True), "rest": (18, 3, 0, 1)}
 
 
 def attend_backward(dn, q, KV, att, lse, wo, wt, X1, pq, pkv, po, cos, sin, tok, dmid, gain1, gp2, g, gd, summed, plan=PLAN):
@@ -1084,7 +1105,7 @@
     X1, C, q, KV, att, lse, wqkv, wo, mid, n2 = attend_forward(
         tok, cot, w_query, w_key.T, w_value.T, w_output, pq, pkv, po, cos, sin, attn_gain, ffn_gain)
     summed = lax.axis_size("dp") == 2
-    dn, g, gd, down, dmid, gp2 = feed_forward(n2, mid, C, w_gate, w_up, w_down, ffn_gain)
+    dn, g, gd, down, dmid, gp2 = feed_forward(n2, mid, C, w_gate, w_up, w_down, ffn_gain, summed)
     down_local = lax.psum_scatter(down, "tensor", scatter_dimension=0, tiled=True)[0]
     ig, gains, gate, up, wd, rest = attend_backward(
         dn, q, KV, att, lse, wo, wqkv, X1, pq, pkv, po, cos, sin, tok, dmid, attn_gain, gp2, g, gd, summed)

time: 470 us -> 468 us (level)
  no operation moved by 1% of the time
where the time goes in v4:
time: 468 us; the launch traced here: 460 us
  Pallas kernels  412 us (88%)
  other arithmetic  22.1 us (5%)
  between operations  14.3 us (3%)
  local copies, waits for them, and re-layouts  11.7 us (2%)
    pallas_call x1, Pallas kernels, attend_backward(): pl.pallas_call(functools.partial(backward_kernel, summed, plan), out_shap...  290 us
    pallas_call x1, Pallas kernels, attend_forward(): pl.pallas_call(functools.partial(forward_kernel, nz), out_shape=[sd((S, 4...  65.4 us
    pallas_call x1, Pallas kernels, feed_forward(): pl.pallas_call(functools.partial(feed_kernel, summed), out_shape=[sd((S,...  56.1 us
  transfers between devices with their start and end apart: 1, of which 0 were waited for; matrix products, arithmetic and copies ran while one was open for 5% of the time, Pallas kernels for 63%

profile of v4, /device:TPU:0, one launch (start us, length us, event | category | flops | bytes accessed | tf_op | source)
XLA Modules:
  0.0 459.7 jit_solution(15775780292795162905)
XLA Ops:
  7.2 0.0 copy-start.4
  7.2 0.0 copy-start.5
  7.2 0.0 reduce-scatter.2.cloned.1.call-start
  7.3 2.7 copy_bitcast_fusion
  10.0 0.0 copy-done.4
  10.0 0.0 copy-done.5
  10.0 3.1 fusion.2
  13.0 65.4 %attend_forward.1 = (bf16[2,4,128,1536]{3,2,1,0:T(8,128)(2,1)}, bf16[2,4,128,1536]{3,2,1,0:T(8,128)(2,1)}, bf16[2,2,1024,128]{3,2,1,0:T(8,128)(2,1)}, bf16[2,4,5...) custom-call(bf16[2,128,1536]{2,1,0:T(8,128)(2,1)} %get-tuple-element, ...), custom_call_target="tpu_custom_call" | custom-call | tf_op jit(solution)/shard_map/attend_forward/pallas_call | solution.py:341
  78.4 56.1 %feed_forward.1 = (bf16[2,128,1536]{2,1,0:T(8,128)(2,1)}, bf16[2,1536,1024]{2,1,0:T(8,128)(2,1)}, bf16[2,512,1536]{2,1,0:T(8,128)(2,1)}, bf16[4,2,128,1536]{3,2,...) custom-call(bf16[2,128,1536]{2,1,0:T(8,128)(2,1)} %get-tuple-element.34.n2, ...), custom_call_target="tpu_custom_call" | custom-call | tf_op jit(solution)/shard_map/feed_forward/pallas_call | solution.py:510
  134.6 0.0 reduce-scatter.2.cloned.1.call-update
  134.6 290.0 %attend_backward.1 = (f32[2,128,1536]{2,1,0:T(8,128)}, f32[8,1536]{1,0:T(8,128)}, bf16[2,2,384,1024]{3,2,1,0:T(8,128)(2,1)}, bf16[2,2,384,1024]{3,2,1,0:T(8,128)...) custom-call(bf16[2,128,1536]{2,1,0:T(8,128)(2,1)} %get-tuple-element.37.dn_in, ...), custom_call_target="tpu_custom_call" | custom-call | tf_op jit(solution)/shard_map/attend_backward/pallas_call | solution.py:1083
  424.6 3.8 copy.31
  428.4 3.7 slice_convert_fusion
  432.0 1.9 copy.32
  434.0 0.0 copy-start.3
  434.0 1.6 slice_reduce_fusion
  435.6 2.9 convert_bitcast_fusion.1
  438.5 0.0 copy-done.3
  438.5 0.0 copy-start.2
  438.5 3.7 bitcast_convert_fusion.2
  442.2 0.0 copy-done.2
  442.2 0.0 copy-start.1
  442.2 3.7 bitcast_convert_fusion.1
  445.9 0.0 copy-done.1
  445.9 0.0 copy-start
  445.9 3.8 bitcast_convert_fusion
  449.6 0.0 reduce-scatter.2.cloned.1.call-done
  449.7 0.0 copy-done
  449.7 1.3 fusion.1
  451.0 1.7 copy.30
  (1 shorter events, 0.0 us)
Async XLA Ops:
  7.2 2.8 copy-start.4
  7.2 2.8 copy-start.5
  7.2 442.5 %reduce-scatter.2.cloned.1.call-start = ((), (), s32[]{:S(2)}) async-start(), calls=%async_computation.1 | async-start | bytes 3932160 | tf_op jit(solution)/shard_map/reduce_scatter | solution.py:1109
  434.0 4.5 copy-start.3
  438.5 3.7 copy-start.2
  442.2 3.7 copy-start.1
  445.9 3.8 copy-start
Sparse Core Ops, SparseCore 0:
  134.7 53.4 reduce-scatter.1

commit v5 on v4

--- a/solution.py
+++ b/solution.py
@@ -733,15 +733,15 @@
 
 
 NO = 192
-CROWS = 6 * NO
+WROWS = 384
+CROWS = 4 * NO
 PHASES = {"dast": 1, "steps": 2, "out": 2, "done": 1, "in": 1}
-EARLY = True
 PRE = 4
-HOP = 1
+HOP = 2
 
 
 def backward_kernel(summed, plan, dn_in, q_in, kv_in, att_in, lse, wo_in, wt_in, x1_in, pq, pkv, po, cos, sin, tok, dmid_in, gain1, gp2,
-                    g_in, gd_in, ig_out, gains_out, o_gate, o_up, o_down, o_rest, *scr):
+                    g_in, gd_in, ig_out, gains_out, o_gate, o_up, o_down, o_wo, o_rest, *scr):
     t = lax.axis_index("tensor")
     zi = lax.axis_index("seq")
     nz = lax.axis_size("seq")
@@ -753,11 +753,14 @@
     HC = D // 4
     QC = CROWS // 4
     scr = list(scr)
-    (DB, q, KV, att, wbuf, da, delta, dqT, acc, PB, RB, dqkv, rs1, rs2, W3, heads, GS, GL,
-     sKV, rKV, sR1, rR1, sR2, rR2, sG, rG, sDB, rDB, isem, sems_out) = scr[:30]
-    scr = scr[30:]
+    (DB, q, KV, att, wbuf, da, delta, dqT, acc, PB, RB, dqkv, rs1, rs2, W3, WO, heads, GS, GL,
+     sKV, rKV, sR1, rR1, sR2, rR2, sG, rG, sDB, rDB, isem, sems_out) = scr[:31]
+    scr = scr[31:]
     xi = lax.axis_index("dp")
     rings = []
+    def sites(phase, count):
+        mode = PHASES[phase]
+        return -(-count // mode) if mode else 0
     loads = [pltpu.make_async_copy(a, b, isem.at[i]) for i, (a, b) in enumerate(
         ((dn_in, DB.at[:, 0]), (wo_in, wbuf.at[pl.ds(0, 512)]), (att_in, att), (q_in, q), (kv_in, KV), (dmid_in, ig_out)))]
     first = []
@@ -774,6 +777,9 @@
         rings.append(make("down", HalfFirst, gd_in, lambda u: own_d.at[u], o_down, own_d.shape[1]))
         rings.append(make("up", LineFirst, WU, o_up.at[0], WU.shape[1]))
         rings.append(make("up_edge", LineFirst, WE, o_up.at[1], WE.shape[1]))
+        rings.append(make("wo", HalfFirst, WO, lambda u: WO.at[xi, u], o_wo, WROWS // 4))
+        ring, off, pace = rings.pop()
+        rings.append((ring, off + 2 * PRE + sites("dast", 2 * S) + sites("out", 4), pace))
         rings.append(make("rest", HalfFirst, W3, lambda u: W3.at[xi, u], o_rest, QC))
         first = [pltpu.make_async_copy(a, b, isem.at[13 + i]) for i, (a, b) in enumerate(
             ((gd_in.at[xi], own_d), (g_in.at[0, xi], own_g), (g_in.at[1, 0], WU), (g_in.at[1, 1], WE)))]
@@ -794,8 +800,7 @@
             def _():
                 tick(k + it // mode)
     def after(phase, count, k):
-        mode = PHASES[phase]
-        return k + (-(-count // mode) if mode else 0)
+        return k + sites(phase, count)
     wt_load = pltpu.make_async_copy(wt_in, wbuf, isem.at[8])
     x1_loads = [pltpu.make_async_copy(x1_in.at[:, :, pl.ds(c * HC, HC)], PB.at[pl.ds(S * c, S)], isem.at[9 + c]) for c in range(4)]
     for c in loads[:2] + first + loads[2:]:
@@ -868,12 +873,13 @@
     def out_grad(k, c, x):
         at = pl.ds(pl.multiple_of(c * HC, HC), HC)
         g0 = nn(heads[...].T, DB[:, :, :, at].reshape(S * SPAN, HC)).astype(bf16)
-        put(4 * NO, at, nn(po[...], g0).astype(bf16))
+        g0 = nn(po[...], g0).astype(bf16)
+        for b in range(4):
+            WO[b // 2, b % 2, :, at] = g0[b * (WROWS // 4):(b + 1) * (WROWS // 4), :]
         ptick("out", c, k)
         return x
-    if EARLY:
-        lax.fori_loop(0, 4, functools.partial(out_grad, k), 0)
-        k = after("out", 4, k)
+    lax.fori_loop(0, 4, functools.partial(out_grad, k), 0)
+    k = after("out", 4, k)
 
     def unit(s, j, diag):
         lane = lax.broadcasted_iota(jnp.int32, (1, 128), 1)
@@ -942,9 +948,6 @@
     for c in x1_loads:
         c.start()
 
-    if not EARLY:
-        lax.fori_loop(0, 4, functools.partial(out_grad, k), 0)
-        k = after("out", 4, k)
     def rotate(c, x):
         s = c // 2
         for g in range(2):
@@ -1006,8 +1009,9 @@
                     def _():
                         ring.tick(kk // pace)
     else:
-        o3 = pltpu.make_async_copy(W3, o_rest, sems_out.at[4])
-        o3.start()
+        o3 = [pltpu.make_async_copy(W3, o_rest, sems_out.at[5]), pltpu.make_async_copy(WO, o_wo, sems_out.at[4])]
+        for o in o3:
+            o.start()
         def joint(g):
             pass
     joint(k)
@@ -1052,10 +1056,11 @@
         for ring, off, pace in rings:
             ring.drain()
     else:
-        o3.wait()
-
-
-PLAN = {"gate": (12, 2, 7, 1), "down": (8, 2, 0, 1, False, (1,)), "up": (8, 1, 21, 3), "up_edge": (24, 3, 2, 1, True), "rest": (18, 3, 0, 1)}
+        for o in o3:
+            o.wait()
+
+
+PLAN = {"gate": (12, 2, 6, 1), "down": (8, 2, 0, 1, False, (1,)), "up": (12, 1, 23, 2), "up_edge": (24, 2, 7, 1, True), "wo": (6, 2, 2, 1), "rest": (12, 2, 0, 1)}
 
 
 def attend_backward(dn, q, KV, att, lse, wo, wt, X1, pq, pkv, po, cos, sin, tok, dmid, gain1, gp2, g, gd, summed, plan=PLAN):
@@ -1072,20 +1077,20 @@
     scratch = [vm((S, 4, RP, D), bf16), vm(q.shape, bf16), vm(KV.shape, bf16), vm(att.shape, bf16), vm((896, D), bf16),
                vm(q.shape, bf16), vm((S, 2, 1, 2 * SPAN), f32), vm((S, 2, 128, 2 * SPAN), f32), vm((SPAN, 384), f32),
                vm((nz * S, SPAN, 384), bf16), vm((nz - 1, S, SPAN, 384), bf16), vm((S, SPAN, 896), bf16),
-               vm((S, 2, RP, D), bf16), vm((S, RP, D), bf16), vm((2, 2, QC, D), bf16), vm((S * SPAN, 512), bf16),
+               vm((S, 2, RP, D), bf16), vm((S, RP, D), bf16), vm((2, 2, QC, D), bf16), vm((2, 2, WROWS // 4, D), bf16), vm((S * SPAN, 512), bf16),
                vm((6, 8, D), f32), vm((6, 8, D), f32),
-               dma((nz, S)), dma((nz, S)), dma((S, 2)), dma((S, 2)), dma((S,)), dma((S,)), dma((6,)), dma((6,)), dma((3, S)), dma((3, S)), dma((17,)), dma((5,))]
+               dma((nz, S)), dma((nz, S)), dma((S, 2)), dma((S, 2)), dma((S,)), dma((S,)), dma((6,)), dma((6,)), dma((3, S)), dma((3, S)), dma((17,)), dma((6,))]
     if summed:
         scratch += [vm((2, QG, FL), bf16), vm((2, QD, D), bf16), vm((2, QG, FL), bf16), vm((2, QG, FL), bf16)]
-        for name, cls, Q, C in (("gate", HalfFirst, QG, FL), ("down", HalfFirst, QD, D), ("up", LineFirst, QG, FL), ("up_edge", LineFirst, QG, FL), ("rest", HalfFirst, QC, D)):
+        for name, cls, Q, C in (("gate", HalfFirst, QG, FL), ("down", HalfFirst, QD, D), ("up", LineFirst, QG, FL), ("up_edge", LineFirst, QG, FL), ("wo", HalfFirst, WROWS // 4, D), ("rest", HalfFirst, QC, D)):
             n = plan[name][0]
             scratch += cls.scratch(n, Q // n, C)
     return pl.pallas_call(
         functools.partial(backward_kernel, summed, plan),
         out_shape=[sd((S, RP, D), f32), sd((8, D), f32), sd((2, 2, QG, FL), bf16), sd((2, 2, QG, FL), bf16), sd((2, 2, QD, D), bf16),
-                   sd((2, 2, QC, D), bf16)],
+                   sd((2, 2, WROWS // 4, D), bf16), sd((2, 2, QC, D), bf16)],
         in_specs=[A, A, A, A, V, A, A, A, V, V, V, V, V, V, A, V, V, A, A],
-        out_specs=[V, V, A, A, A, A],
+        out_specs=[V, V, A, A, A, A, A],
         scratch_shapes=scratch,
         compiler_params=pltpu.CompilerParams(collective_id=2, has_side_effects=True, vmem_limit_bytes=VMEM_BYTES),
         name="attend_backward")(dn, q, KV, att, lse, wo, wt, X1.reshape(S, SPAN, D), pq, pkv, po, cos, sin, tok, dmid, gain1, gp2,
@@ -1107,10 +1112,10 @@
     summed = lax.axis_size("dp") == 2
     dn, g, gd, down, dmid, gp2 = feed_forward(n2, mid, C, w_gate, w_up, w_down, ffn_gain, summed)
     down_local = lax.psum_scatter(down, "tensor", scatter_dimension=0, tiled=True)[0]
-    ig, gains, gate, up, wd, rest = attend_backward(
+    ig, gains, gate, up, wd, out, rest = attend_backward(
         dn, q, KV, att, lse, wo, wqkv, X1, pq, pkv, po, cos, sin, tok, dmid, attn_gain, gp2, g, gd, summed)
     if not summed:
-        g, wd, rest = lax.psum((g.astype(f32), gd.astype(f32), rest.astype(f32)), ("dp", "seq"))
+        g, wd, out, rest = lax.psum((g.astype(f32), gd.astype(f32), out.astype(f32), rest.astype(f32)), ("dp", "seq"))
         gate, up = g[0], g[1]
         gains = lax.psum(gains, ("dp", "seq", "tensor"))
     rest = rest.reshape(-1, D)
@@ -1123,7 +1128,7 @@
         rest[:nq].astype(f32).T,
         rest[nq:nq + nk].astype(f32).T,
         rest[nq + nk:nq + 2 * nk].astype(f32).T,
-        rest[nq + 2 * nk:].astype(f32),
+        out.reshape(-1, D).astype(f32),
         gains[1],
         gate.reshape(D, -1).astype(f32),
         up.reshape(D, -1).astype(f32),

time: 468 us -> 464 us (level)
  no operation moved by 1% of the time
where the time goes in v5:
time: 464 us; the launch traced here: 456 us
  Pallas kernels  408 us (88%)
  other arithmetic  20.5 us (4%)
  between operations  14.3 us (3%)
  local copies, waits for them, and re-layouts  12.9 us (3%)
    pallas_call x1, Pallas kernels, attend_backward(): pl.pallas_call(functools.partial(backward_kernel, summed, plan), out_shap...  287 us
    pallas_call x1, Pallas kernels, attend_forward(): pl.pallas_call(functools.partial(forward_kernel, nz), out_shape=[sd((S, 4...  65.4 us
    pallas_call x1, Pallas kernels, feed_forward(): pl.pallas_call(functools.partial(feed_kernel, summed), out_shape=[sd((S,...  56.1 us
  transfers between devices with their start and end apart: 1, of which 0 were waited for; matrix products, arithmetic and copies ran while one was open for 5% of the time, Pallas kernels for 63%

profile of v5, /device:TPU:0, one launch (start us, length us, event | category | flops | bytes accessed | tf_op | source)
XLA Modules:
  0.0 456.2 jit_solution(14227636746761626902)
XLA Ops:
  7.2 0.0 copy-start.6
  7.2 0.0 copy-start.7
  7.2 0.0 reduce-scatter.2.cloned.1.call-start
  7.3 2.7 copy_bitcast_fusion
  10.0 0.0 copy-done.6
  10.0 0.0 copy-done.7
  10.0 3.1 fusion.2
  13.0 65.4 %attend_forward.1 = (bf16[2,4,128,1536]{3,2,1,0:T(8,128)(2,1)}, bf16[2,4,128,1536]{3,2,1,0:T(8,128)(2,1)}, bf16[2,2,1024,128]{3,2,1,0:T(8,128)(2,1)}, bf16[2,4,5...) custom-call(bf16[2,128,1536]{2,1,0:T(8,128)(2,1)} %get-tuple-element, ...), custom_call_target="tpu_custom_call" | custom-call | tf_op jit(solution)/shard_map/attend_forward/pallas_call | solution.py:341
  78.4 56.1 %feed_forward.1 = (bf16[2,128,1536]{2,1,0:T(8,128)(2,1)}, bf16[2,1536,1024]{2,1,0:T(8,128)(2,1)}, bf16[2,512,1536]{2,1,0:T(8,128)(2,1)}, bf16[4,2,128,1536]{3,2,...) custom-call(bf16[2,128,1536]{2,1,0:T(8,128)(2,1)} %get-tuple-element.35.n2, ...), custom_call_target="tpu_custom_call" | custom-call | tf_op jit(solution)/shard_map/feed_forward/pallas_call | solution.py:510
  134.6 0.0 reduce-scatter.2.cloned.1.call-update
  134.6 286.8 %attend_backward.1 = (f32[2,128,1536]{2,1,0:T(8,128)}, f32[8,1536]{1,0:T(8,128)}, bf16[2,2,384,1024]{3,2,1,0:T(8,128)(2,1)}, bf16[2,2,384,1024]{3,2,1,0:T(8,128)...) custom-call(bf16[2,128,1536]{2,1,0:T(8,128)(2,1)} %get-tuple-element.3, ...), custom_call_target="tpu_custom_call" | custom-call | tf_op jit(solution)/shard_map/attend_backward/pallas_call | solution.py:1088
  421.4 0.0 copy-start.4
  421.4 3.9 copy.32
  425.4 0.0 copy-done.4
  425.4 0.1 slice.17
  425.4 0.4 bitcast_convert_fusion.4
  425.8 2.0 copy.30
  427.8 0.0 copy-start.5
  427.8 1.6 slice_reduce_fusion
  429.3 2.9 convert_bitcast_fusion
  432.3 0.0 copy-start.3
  432.3 0.0 copy-done.5
  432.3 1.8 bitcast_convert_fusion.3
  434.0 1.0 copy-done.3
  435.0 0.0 copy-start.2
  435.0 3.7 bitcast_convert_fusion.2
  438.7 0.0 copy-done.2
  438.7 0.0 copy-start.1
  438.7 3.7 bitcast_convert_fusion.1
  442.3 0.0 copy-done.1
  442.3 0.0 copy-start
  442.3 3.8 bitcast_convert_fusion
  446.1 0.0 reduce-scatter.2.cloned.1.call-done
  446.1 0.0 copy-done
  446.1 1.3 fusion.1
  447.4 1.7 copy.31
  (1 shorter events, 0.0 us)
Async XLA Ops:
  7.2 2.8 copy-start.6
  7.2 2.8 copy-start.7
  7.2 438.9 %reduce-scatter.2.cloned.1.call-start = ((), (), s32[]{:S(2)}) async-start(), calls=%async_computation.1 | async-start | bytes 3932160 | tf_op jit(solution)/shard_map/reduce_scatter | solution.py:1114
  421.4 3.9 copy-start.4
  427.8 4.5 copy-start.5
  432.3 2.7 copy-start.3
  435.0 3.7 copy-start.2
  438.7 3.7 copy-start.1
  442.3 3.8 copy-start
Sparse Core Ops, SparseCore 0:
  134.7 53.3 reduce-scatter.1
